TPU v7x, 32 devices: a whole 2x2x4 slice. The times are simulated.
32 devices in a mesh: brick: 8 (over z, x), chan: 4 (over y, core).
Axes of the slice: x: 2, y: 2, z: 4, core: 2. Of those that a mesh axis runs over, the one named last changes fastest.
Arguments:
- features: bfloat16 [32, 128, 512], P('brick', 'chan'), may hold values from -6 to 6
- fine_links: int32 [32, 26], P('brick'), may hold values from -1 to 31, as said below
- coarse_links: int32 [16, 26], P('brick'), may hold values from -1 to 15, as said below
- parents: int32 [32], P('brick'), may hold values from 0 to 127, as said below
- down_weight: bfloat16 [8, 128, 128], P(None, None, 'chan'), may hold values from -0.1875 to 0.1875
- coarse_weight: bfloat16 [27, 128, 128], P(None, 'chan'), may hold values from -0.109375 to 0.109375
- up_weight: bfloat16 [8, 128, 128], P(None, 'chan'), may hold values from -0.5 to 0.5
- fine_weight: bfloat16 [27, 128, 128], P(None, 'chan'), may hold values from -0.109375 to 0.109375
- coarse_bias: float32 [128], P('chan'), may hold values from -3 to 3
- fine_bias: float32 [128], P('chan'), may hold values from -3 to 3
Outputs:
- refined: bfloat16 [32, 128, 512], P('brick', 'chan')
Inputs may be any that keep to these rules, and one draw needn't show every extreme that they name: `fine_links`: A fine brick's index is its owner times 4 plus its place there; the owner of fine brick b is b // 4. Among the rows of one owner's bricks, at most 3 of the entries in columns 0 to 5 name bricks of any one owner, and at most 10 of the entries in columns 6 to 25 do. `coarse_links`: A coarse brick's index is its owner times 2 plus its place there. Among the rows of one owner's coarse bricks, at most 2 of the entries in columns 0 to 5 name coarse bricks of any one owner, and at most 5 of the entries in columns 6 to 25 do. parents[b] // 8 is a coarse brick; at most 1 of one owner's fine bricks have parents on any one owner.
All inputs are finite; a program needn't handle non-finite values.
Results may differ from a plain program's by a relative error of at most 0.0059.
Values may be sent and summed in bfloat16 or wider, within the bound.
No kernel may reach another device: no remote copies, remote signals or barrier semaphores. Data moves between devices by JAX's collectives and lax.ppermute only.
A program may use at most 64 MiB of HBM per device.

v0:
```python
import numpy as np
import jax
import jax.numpy as jnp
from jax import lax
from jax.experimental import pallas as pl
from jax.experimental.pallas import tpu as pltpu
from jax.sharding import PartitionSpec as P

EDGE = 8
HALF = EDGE // 2
CUBE = HALF**3
FRAME = EDGE + 2
NBLK = 32
F32 = jnp.float32
BF16 = jnp.bfloat16
VMEM_LIMIT = 56 * 1024 * 1024


def headings():
    face_steps = [(1, 0, 0), (-1, 0, 0), (0, 1, 0), (0, -1, 0), (0, 0, 1), (0, 0, -1)]
    others = []
    for step_x in (-1, 0, 1):
        for step_y in (-1, 0, 1):
            for step_z in (-1, 0, 1):
                if abs(step_x) + abs(step_y) + abs(step_z) >= 2:
                    others.append((step_x, step_y, step_z))
    return face_steps + others


HEADINGS = headings()
HEADING_INDEX = {d: k for k, d in enumerate(HEADINGS)}
HEADING_INDEX[(0, 0, 0)] = len(HEADINGS)


def piece_lanes():
    starts, at = [], 0
    order = sorted(
        range(len(HEADINGS)), key=lambda k: (sum(1 for e in HEADINGS[k] if e), k)
    )
    starts = [0] * len(HEADINGS)
    voxels = [None] * len(HEADINGS)
    for k in order:
        spans = [
            [0] if e == 1 else [EDGE - 1] if e == -1 else list(range(EDGE))
            for e in HEADINGS[k]
        ]
        voxels[k] = [
            (x * EDGE + y) * EDGE + z
            for x in spans[0]
            for y in spans[1]
            for z in spans[2]
        ]
        starts[k] = at
        at += len(voxels[k])
    return starts, voxels


STARTS, VOXELS = piece_lanes()


def octant_selector():
    sel = np.zeros((EDGE**3, EDGE**3), np.float32)
    for x in range(EDGE):
        for y in range(EDGE):
            for z in range(EDGE):
                o = (x % 2) * 4 + (y % 2) * 2 + z % 2
                u = ((x // 2) * HALF + y // 2) * HALF + z // 2
                sel[(x * EDGE + y) * EDGE + z, o * CUBE + u] = 1
    return sel


def outer_selector():
    sel = np.zeros((EDGE**3, EDGE**3), np.float32)
    for k in range(len(HEADINGS)):
        for i, v in enumerate(VOXELS[k]):
            sel[v, STARTS[k] + i] = 1
    return sel


def pair_selector():
    sel = np.zeros((256, 256), np.float32)
    for x in range(2):
        for y in range(8):
            for b in range(2):
                for z in range(8):
                    sel[((x * 8 + y) * 2 + b) * 8 + z, ((b * 2 + x) * 8 + y) * 8 + z] = 1
    return sel


def dot(a, b):
    return lax.dot_general(a, b, (((1,), (0,)), ((), ())), preferred_element_type=F32)


def dot_t(a, b):
    return lax.dot_general(a, b, (((1,), (1,)), ((), ())), preferred_element_type=F32)


def params():
    return pltpu.CompilerParams(vmem_limit_bytes=VMEM_LIMIT)


def cost(flops, moved):
    return pl.CostEstimate(flops=flops, bytes_accessed=moved, transcendentals=0)


VM = pltpu.VMEM
SM = pltpu.SMEM


def project_kernel(chans, me_ref, f_ref, oct_ref, outer_ref, w_ref, *rest):
    outs, hs_ref, part = rest[:chans], rest[chans], rest[chans + 1]
    q = w_ref.shape[2]
    fine = f_ref.shape[0] // q
    x = f_ref[...]
    picked = dot(x, oct_ref[...]).astype(BF16)
    acc = None
    for o in range(8):
        z = jnp.concatenate(
            [picked[b * q : (b + 1) * q, o * CUBE : (o + 1) * CUBE] for b in range(fine)],
            axis=1,
        )
        term = dot(w_ref[o], z)
        acc = term if acc is None else acc + term
    part[...] = acc
    me = me_ref[0]
    for s in range(chans):
        outs[s][...] = part[pl.ds(pl.multiple_of((me ^ s) * q, q), q), :].astype(BF16)
    hs_ref[...] = dot(x, outer_ref[...]).astype(BF16)


def project(me, features, down_weight, chans):
    fine, q, vox = features.shape
    c_out = down_weight.shape[1]
    lanes = fine * CUBE
    res = pl.pallas_call(
        lambda *refs: project_kernel(chans, *refs),
        out_shape=[jax.ShapeDtypeStruct((q, lanes), BF16)] * chans
        + [jax.ShapeDtypeStruct((fine * q, vox), BF16)],
        in_specs=[pl.BlockSpec(memory_space=SM)] + [pl.BlockSpec(memory_space=VM)] * 4,
        out_specs=[pl.BlockSpec(memory_space=VM)] * (chans + 1),
        scratch_shapes=[pltpu.VMEM((c_out, lanes), F32)],
        compiler_params=params(),
        cost_estimate=cost(2 * c_out * 8 * q * lanes, 2 * 1024 * 1024),
        name="project",
    )(
        me,
        features.reshape(fine * q, vox),
        jnp.asarray(octant_selector(), BF16),
        jnp.asarray(outer_selector(), BF16),
        down_weight,
    )
    return res[:chans], res[chans]


def assemble_kernel(chans, *refs):
    slots, hs_ref, meta_ref, out_ref = refs[:chans], refs[chans], refs[chans + 1], refs[chans + 2]
    total = slots[0][...].astype(F32)
    for s in slots[1:]:
        total = total + s[...].astype(F32)
    q, lanes = slots[0].shape
    rows = hs_ref.shape[0]
    out_ref[0, 0:q, :] = total.astype(BF16)
    at = q
    for h in range(hs_ref.shape[1] // lanes):
        out_ref[0, at : at + rows, :] = hs_ref[:, h * lanes : (h + 1) * lanes]
        at += rows
    out_ref[0, at : at + meta_ref.shape[0], :] = meta_ref[...]


def assemble(slots, outer, meta, owners):
    q, lanes = slots[0].shape
    rows = q + outer.shape[0] * outer.shape[1] // lanes + meta.shape[0]
    whole = lambda a: pl.BlockSpec(a.shape, lambda i: (0,) * a.ndim)
    ins = list(slots) + [outer, meta]
    return pl.pallas_call(
        lambda *refs: assemble_kernel(len(slots), *refs),
        out_shape=jax.ShapeDtypeStruct((owners, rows, lanes), BF16),
        grid=(owners,),
        in_specs=[whole(a) for a in ins],
        out_specs=pl.BlockSpec((1, rows, lanes), lambda i: (i, 0, 0)),
        compiler_params=params(),
        name="assemble",
    )(*ins)


def halo_kernel(q, links_ref, recv_ref, out_ref):
    fine = out_ref.shape[0]
    lanes = recv_ref.shape[2]
    lane = lax.broadcasted_iota(jnp.int32, (q, 128), 1)
    for b in range(fine):
        for chunk in range(out_ref.shape[2] // 128):
            here = jnp.zeros((q, 128), F32)
            base = q + (chunk * 128 // lanes) * fine * q
            col = chunk * 128 % lanes
            for k in range(len(HEADINGS)):
                if STARTS[k] // 128 != chunk:
                    continue
                first = STARTS[k] % 128
                last = first + len(VOXELS[k])
                m = links_ref[b, k]
                safe = jnp.maximum(m, 0)
                row = pl.multiple_of(base + lax.rem(safe, fine) * q, 16)
                got = recv_ref[lax.div(safe, fine), pl.ds(row, q), col : col + 128].astype(F32)
                got = jnp.where(m >= 0, got, 0.0)
                here = jnp.where((lane >= first) & (lane < last), got, here)
            out_ref[b, :, chunk * 128 : (chunk + 1) * 128] = here.astype(BF16)


def halo(links, recv, fine, q, vox):
    return pl.pallas_call(
        lambda *refs: halo_kernel(q, *refs),
        out_shape=jax.ShapeDtypeStruct((fine, q, vox), BF16),
        in_specs=[pl.BlockSpec(memory_space=SM), pl.BlockSpec(memory_space=VM)],
        out_specs=pl.BlockSpec(memory_space=VM),
        compiler_params=params(),
        name="halo",
    )(links, recv)


def axis_places(u):
    found = [(0, 1 + u)]
    if u == 0:
        found.append((1, HALF + 1))
    if u == HALF - 1:
        found.append((-1, 0))
    return found


def coarse_kernel(proj_ref, target_ref, parents_ref, w_ref, bias_ref, out_ref, rows_ref, sel_ref, nb_ref):
    chans, owners, q, lanes = proj_ref.shape
    fine = lanes // CUBE
    total = owners * fine

    def spread(w, _):
        block = jnp.concatenate([proj_ref[c, w] for c in range(chans)], axis=0)
        turned = block.astype(F32).T
        for b in range(fine):
            rows_ref[pl.ds(w * fine + b, CUBE, stride=total), :] = turned[b * CUBE : (b + 1) * CUBE]
        return 0

    @pl.when(pl.program_id(0) == 0)
    def _():
        if owners <= 8:
            for w in range(owners):
                spread(w, 0)
        else:
            lax.fori_loop(0, owners, spread, 0)

    for d in range(27):
        sel_ref[d * NBLK : (d + 1) * NBLK, :] = (
            (target_ref[:, d : d + 1] == parents_ref[0:1, :]).astype(F32).astype(BF16)
        )
    for ux in range(HALF):
        for uy in range(HALF):
            for uz in range(HALF):
                places = [
                    (9 * (a[0] + 1) + 3 * (b[0] + 1) + c[0] + 1, a[1], b[1], c[1])
                    for a in axis_places(ux)
                    for b in axis_places(uy)
                    for c in axis_places(uz)
                ]
                u = (ux * HALF + uy) * HALF + uz
                source = rows_ref[u * total : (u + 1) * total, :].astype(BF16)
                picker = jnp.concatenate(
                    [sel_ref[d * NBLK : (d + 1) * NBLK, :] for d, _, _, _ in places], axis=0
                )
                got = dot(picker, source).astype(BF16)
                for i, (_, x, y, z) in enumerate(places):
                    nb_ref[x, y, z] = got[i * NBLK : (i + 1) * NBLK]
    span = HALF + 2
    size = span * HALF * HALF * NBLK
    acc = conv_rows(
        w_ref,
        lambda a2, a3: nb_ref[:, a2 : a2 + HALF, a3 : a3 + HALF].reshape(size, nb_ref.shape[4]),
    )
    step = HALF * HALF * NBLK
    n = HALF * step
    res = acc[0:q, 0:n] + acc[q : 2 * q, step : step + n] + acc[2 * q : 3 * q, 2 * step : 2 * step + n]
    out_ref[0] = jnp.maximum(res + bias_ref[...], 0.0).astype(BF16)


def conv_rows(w_ref, rows_of):
    taps = [(a2, a3) for a2 in range(3) for a3 in range(3)]
    acc = None
    for i in range(0, 9, 2):
        some = taps[i : i + 2]
        lhs = jnp.concatenate(
            [
                jnp.concatenate([w_ref[9 * a1 + 3 * a2 + a3] for a1 in range(3)], axis=0)
                for a2, a3 in some
            ],
            axis=1,
        )
        rhs = jnp.concatenate([rows_of(a2, a3) for a2, a3 in some], axis=1)
        term = dot_t(lhs, rhs)
        acc = term if acc is None else acc + term
    return acc


def coarse(proj, target, parents, weight, bias):
    chans, owners, q, lanes = proj.shape
    total = owners * lanes // CUBE
    blocks = total // NBLK
    c_in = weight.shape[2]
    whole = lambda a: pl.BlockSpec(a.shape, lambda i: (0,) * a.ndim)
    return pl.pallas_call(
        coarse_kernel,
        out_shape=jax.ShapeDtypeStruct((blocks, q, CUBE * NBLK), BF16),
        grid=(blocks,),
        in_specs=[
            whole(proj),
            pl.BlockSpec((NBLK, target.shape[1]), lambda i: (i, 0)),
            whole(parents),
            whole(weight),
            whole(bias),
        ],
        out_specs=pl.BlockSpec((1, q, CUBE * NBLK), lambda i: (i, 0, 0)),
        scratch_shapes=[
            pltpu.VMEM((CUBE * total, c_in), F32),
            pltpu.VMEM((27 * NBLK, total), BF16),
            pltpu.VMEM((HALF + 2, HALF + 2, HALF + 2, NBLK, c_in), BF16),
        ],
        compiler_params=params(),
        cost_estimate=cost(2 * 27 * c_in * q * CUBE * total, 2 * 1024 * 1024),
        name="coarse",
    )(proj, target, parents, weight, bias)


def frame_axis(f):
    if f == 0:
        return -1, EDGE - 1
    if f == FRAME - 1:
        return 1, 0
    return 0, f - 1


def frame_kernel(owner_ref, links_ref, fi_ref, fh_ref, ff_ref, sel_ref, inner, outer, plane):
    chans, fine, q, vox = fi_ref.shape
    span = 8 * fine
    owner = owner_ref[0]
    for b in range(fine):
        inner[b] = jnp.concatenate([fi_ref[c, b] for c in range(chans)], axis=0).astype(F32).T
        outer[b] = jnp.concatenate([fh_ref[c, b] for c in range(chans)], axis=0).astype(F32).T
    for b in range(fine):
        for s in range(2):
            dz = 2 * s - 1
            row = 2 * b + s
            for fx in range(FRAME):
                dx, vx = frame_axis(fx)
                start = STARTS[HEADING_INDEX[(dx, 0, dz)]] + (0 if dx else vx * EDGE)
                plane[pl.ds((fx * FRAME + 1) * 8 + row, EDGE, stride=8), :] = outer[b, start : start + EDGE, :]
            for fy in (0, FRAME - 1):
                dy = frame_axis(fy)[0]
                start = STARTS[HEADING_INDEX[(0, dy, dz)]]
                plane[pl.ds((FRAME + fy) * 8 + row, EDGE, stride=8 * FRAME), :] = outer[b, start : start + EDGE, :]
                for fx in (0, FRAME - 1):
                    start = STARTS[HEADING_INDEX[(frame_axis(fx)[0], dy, dz)]]
                    plane[pl.ds((fx * FRAME + fy) * 8 + row, 1), :] = outer[b, start : start + 1, :]
    for fx in range(FRAME):
        for fy in range(FRAME):
            dx, vx = frame_axis(fx)
            dy, vy = frame_axis(fy)
            at = ((1 - fx % 2) * 2 + 1 - fy % 2) * 25 + (fx // 2) * 5 + fy // 2
            tiles = []
            for b in range(fine):
                if dx == 0 and dy == 0:
                    start = (vx * EDGE + vy) * EDGE
                    tiles.append(inner[b, start : start + EDGE, :])
                else:
                    start = STARTS[HEADING_INDEX[(dx, dy, 0)]]
                    if dx == 0:
                        start += vx * EDGE
                    elif dy == 0:
                        start += vy * EDGE
                    tiles.append(outer[b, start : start + EDGE, :])
            tiles.append(plane[(fx * FRAME + fy) * 8 : (fx * FRAME + fy) * 8 + 8, :])
            tiles.append(jnp.zeros((8, plane.shape[1]), F32))
            ff_ref[at] = jnp.concatenate(tiles, axis=0).astype(BF16)
    blocks = sel_ref.shape[0]
    lane = lax.broadcasted_iota(jnp.int32, (8, 128), 1)
    row = lax.broadcasted_iota(jnp.int32, (8, 128), 0)

    def pick(j, _):
        for dx in (-1, 0, 1):
            for dy in (-1, 0, 1):
                def brick(b, dz):
                    k = HEADING_INDEX[(dx, dy, dz)]
                    n = owner * fine + b if k == len(HEADINGS) else links_ref[b, k]
                    n = n - j * NBLK
                    return jnp.where((n >= 0) & (n < NBLK), n, -1024)

                tiles = []
                for b in range(fine):
                    tiles.append((lane - (row // 2) * NBLK == brick(b, 0)).astype(F32))
                low = jnp.full((8, 128), -1024, jnp.int32)
                for b in range(fine):
                    for s in range(2):
                        n = brick(b, 2 * s - 1) + (HALF - 1) * (1 - s) * NBLK
                        low = jnp.where(row == 2 * b + s, n, low)
                tiles.append((lane == low).astype(F32))
                tiles.append(jnp.zeros((8, 128), F32))
                sel_ref[j, 3 * (dx + 1) + dy + 1] = jnp.concatenate(tiles, axis=0).astype(BF16)
        return 0

    if blocks == 1:
        pick(0, 0)
    else:
        lax.fori_loop(0, blocks, pick, 0)


def frames(owner, links, inner, outer, blocks):
    chans, fine, q, vox = inner.shape
    rows = 8 * fine + 16
    return pl.pallas_call(
        frame_kernel,
        out_shape=[
            jax.ShapeDtypeStruct((FRAME * FRAME, rows, chans * q), BF16),
            jax.ShapeDtypeStruct((blocks, 9, rows, 128), BF16),
        ],
        in_specs=[pl.BlockSpec(memory_space=SM)] * 2 + [pl.BlockSpec(memory_space=VM)] * 2,
        out_specs=[pl.BlockSpec(memory_space=VM)] * 2,
        scratch_shapes=[
            pltpu.VMEM((fine, vox, chans * q), F32),
            pltpu.VMEM((fine, vox, chans * q), F32),
            pltpu.VMEM((FRAME * FRAME * 8, chans * q), F32),
        ],
        compiler_params=params(),
        name="frames",
    )(owner, links, inner, outer)


def fine_kernel(co_ref, ff_ref, sel_ref, up_ref, w_ref, bias_ref, pair_ref, out_ref, cr, g3):
    chans, blocks, q, _ = co_ref.shape
    c_all = chans * q
    fine = out_ref.shape[0]
    rows = ff_ref.shape[1]
    for ux in range(HALF):
        for uy in range(HALF):
            places = [
                (3 * (a[0] + 1) + b[0] + 1, a[1], b[1])
                for a in axis_places(ux)
                for b in axis_places(uy)
            ]
            col = (ux * HALF + uy) * 128

            def part(j):
                source = jnp.concatenate(
                    [co_ref[c, j, :, col : col + 128] for c in range(chans)], axis=0
                )
                picker = jnp.concatenate([sel_ref[j, d] for d, _, _ in places], axis=0)
                return dot_t(picker, source)

            if blocks == 1:
                got = part(0)
            else:
                got = lax.fori_loop(
                    0,
                    blocks,
                    lambda j, a: a + part(j),
                    jnp.zeros((len(places) * rows, c_all), F32),
                )
            got = got.astype(BF16)
            for i, (_, x, y) in enumerate(places):
                cr[x, y] = got[i * rows : (i + 1) * rows]
    r = lax.broadcasted_iota(jnp.int32, (rows, c_all), 0)
    odd = (r % 2 == 1) ^ (r >= 8 * fine)
    sub = lax.broadcasted_iota(jnp.int32, (5, 8, c_all), 1)
    for px in range(2):
        for py in range(2):
            lift = jnp.concatenate([up_ref[4 * px + 2 * py], up_ref[4 * px + 2 * py + 1]], axis=0)
            for i in range(5):
                x = i + 1 - px
                src = cr[x, 1 - py : 6 - py].reshape(5 * rows, c_all)
                both = dot_t(src, lift).reshape(5, rows, 2 * c_all)
                up = jnp.where(odd[None], both[:, :, c_all:], both[:, :, :c_all])
                at = (px * 2 + py) * 25 + i * 5
                merged = (ff_ref[at : at + 5].astype(F32) + up).astype(BF16).astype(F32)
                fx = 2 * i + 1 - px
                plane = merged[:, 8 * fine : 8 * fine + 8, :]
                for pair in range(fine // 2):
                    made = [[], [], []]
                    for h in range(2):
                        b = 2 * pair + h
                        mid = merged[:, 8 * b : 8 * b + 8, :]
                        made[0].append(
                            jnp.where(
                                sub == 0,
                                pltpu.roll(plane, (8 - 2 * b) % 8, 1),
                                pltpu.roll(mid, 1, 1),
                            )
                        )
                        made[1].append(mid)
                        made[2].append(
                            jnp.where(
                                sub == 7,
                                pltpu.roll(plane, 7 - (2 * b + 1), 1),
                                pltpu.roll(mid, 7, 1),
                            )
                        )
                    for a3 in range(3):
                        tile = jnp.concatenate(made[a3], axis=1).astype(BF16)
                        for j in range(5):
                            g3[a3, pair, fx, 2 * j + 1 - py] = tile[j]
    step = EDGE * 2 * EDGE
    n = EDGE * step
    for pair in range(fine // 2):
        acc = conv_rows(
            w_ref,
            lambda a2, a3: g3[a3, pair, :, a2 : a2 + EDGE].reshape(FRAME * step, c_all),
        )
        res = acc[0:q, 0:n] + acc[q : 2 * q, step : step + n] + acc[2 * q : 3 * q, 2 * step : 2 * step + n]
        res = jnp.maximum(res + bias_ref[...], 0.0).astype(BF16)
        for h in range(n // 256):
            turned = dot(res[:, 256 * h : 256 * h + 256], pair_ref[...]).astype(BF16)
            for b in range(2):
                out_ref[2 * pair + b, :, 128 * h : 128 * h + 128] = turned[:, 128 * b : 128 * b + 128]


def refine(co, ff, sel, up_weight, weight, bias):
    chans, blocks, q, _ = co.shape
    rows = ff.shape[1]
    fine = (rows - 16) // 8
    c_all = chans * q
    return pl.pallas_call(
        fine_kernel,
        out_shape=jax.ShapeDtypeStruct((fine, q, EDGE**3), BF16),
        in_specs=[pl.BlockSpec(memory_space=VM)] * 7,
        out_specs=pl.BlockSpec(memory_space=VM),
        scratch_shapes=[
            pltpu.VMEM((HALF + 2, HALF + 2, rows, c_all), BF16),
            pltpu.VMEM((3, fine // 2, FRAME, FRAME, 2 * EDGE, c_all), BF16),
        ],
        compiler_params=params(),
        cost_estimate=cost(2 * 27 * c_all * q * fine * EDGE**3, 4 * 1024 * 1024),
        name="refine",
    )(co, ff, sel, up_weight, weight, bias, jnp.asarray(pair_selector(), BF16))


def octant_table():
    columns = np.zeros((8, 27), np.int32)
    octants = np.zeros((8, 27), np.int32)
    for o in range(8):
        bits = (o >> 2 & 1, o >> 1 & 1, o & 1)
        for d in range(27):
            go = (d // 9 - 1, d // 3 % 3 - 1, d % 3 - 1)
            cross, land = [], []
            for bit, g in zip(bits, go):
                t = bit + g
                cross.append(-1 if t < 0 else 1 if t > 1 else 0)
                land.append(t % 2)
            columns[o, d] = HEADING_INDEX[tuple(cross)]
            octants[o, d] = land[0] * 4 + land[1] * 2 + land[2]
    return columns, octants


def described(coarse_links, parents, owner, lanes):
    count = coarse_links.shape[0]
    columns, octants = octant_table()
    mine = owner * count + jnp.arange(count, dtype=jnp.int32)
    links = jnp.concatenate([coarse_links, mine[:, None]], axis=1)
    there = links[:, columns.reshape(-1)].reshape(count, 8, 27)
    codes = jnp.where(there >= 0, there * 8 + octants[None], -1).reshape(count * 8, 27) + 1
    ups = jnp.pad(parents[:, None] + 1, ((0, count * 8 - parents.shape[0]), (0, 0)))
    both = jnp.concatenate([codes, ups], axis=1)
    digits = jnp.concatenate([both // 128, both % 128], axis=1)
    return jnp.pad(digits, ((0, 0), (0, lanes - digits.shape[1]))).astype(BF16)


def understood(meta, fine):
    value = meta[:, :, :56].astype(jnp.int32)
    value = value[:, :, :28] * 128 + value[:, :, 28:] - 1
    table = value[:, :, :27].reshape(-1, 27)
    parents = value[:, :fine, 27].reshape(-1)
    return jnp.take(table, parents, axis=0), parents[None, :]


def per_device(
    features,
    fine_links,
    coarse_links,
    parents,
    down_weight,
    coarse_weight,
    up_weight,
    fine_weight,
    coarse_bias,
    fine_bias,
):
    owners = lax.axis_size("brick")
    chans = lax.axis_size("chan")
    owner = lax.axis_index("brick").astype(jnp.int32)
    me = lax.axis_index("chan").astype(jnp.int32)
    fine, q, vox = features.shape
    lanes = fine * CUBE
    meta = described(coarse_links, parents, owner, lanes)
    slots, outer = project(me[None], features, down_weight, chans)
    arrived = [slots[0]] + [
        lax.ppermute(slots[s], "chan", [(i, i ^ s) for i in range(chans)])
        for s in range(1, chans)
    ]
    sending = assemble(arrived, outer, meta, owners)
    recv = lax.all_to_all(sending, "brick", split_axis=0, concat_axis=0, tiled=True)
    proj = lax.all_gather(recv[:, :q], "chan", axis=0)
    target, all_parents = understood(recv[:, recv.shape[1] - meta.shape[0] :], fine)
    co = coarse(proj, target, all_parents, coarse_weight, coarse_bias[:, None])
    co = lax.all_gather(co, "chan", axis=0)
    around = halo(fine_links, recv, fine, q, vox)
    fi = lax.all_gather(features, "chan", axis=0)
    fh = lax.all_gather(around, "chan", axis=0)
    up_all = lax.all_gather(up_weight, "chan", axis=1, tiled=True)
    ff, sel = frames(owner[None], fine_links, fi, fh, co.shape[1])
    return refine(co, ff, sel, up_all, fine_weight, fine_bias[:, None])


def solution(mesh):
    in_specs = (
        P("brick", "chan", None),
        P("brick", None),
        P("brick", None),
        P("brick"),
        P(None, None, "chan"),
        P(None, "chan", None),
        P(None, "chan", None),
        P(None, "chan", None),
        P("chan"),
        P("chan"),
    )
    return jax.shard_map(
        per_device,
        mesh=mesh,
        in_specs=in_specs,
        out_specs=P("brick", "chan", None),
        check_vma=False,
    )
```

profile of v0, /device:TPU:0, one launch (start us, length us, event | category | flops | bytes accessed | tf_op | source)
XLA Modules:
  0.0 94.9 jit_solution(2726753315607210741)
XLA Ops:
  0.0 1.7 %copy.31.refs_4_ = bf16[8,128,32]{2,1,0:T(8,128)(2,1)} copy(bf16[8,128,32]{1,2,0:T(8,128)(2,1)} %param.20) | data formatting | bytes 131072 | tf_op args[4]
  1.7 2.7 %project.1 = (bf16[32,256]{1,0:T(8,128)(2,1)}, bf16[32,256]{1,0:T(8,128)(2,1)}, bf16[32,256]{1,0:T(8,128)(2,1)}, bf16[32,256]{1,0:T(8,128)(2,1)}, bf16[128,512]{1,0:T(8,128)(2,1)}) custom-call(s32[1]{0:T(128)} %bitcast.refs_0_, bf16[128,512]{1,0:T(8,128)(2,1)} %bitcast.30, bf16[512,512]{1,0:T(8,128)(2,1)} %constant.81.clone.refs_2_, ...), custom_call_target="tpu_custom_call" | custom-call | flops 16777216 | bytes 2097152 | tf_op jit(solution)/shard_map/project/pallas_call | solution.py:135
  4.4 0.5 collective-permute-start
  4.8 2.5 %collective-permute-start.1 = (bf16[32,256]{1,0:T(8,128)(2,1)}, bf16[32,256]{1,0:T(8,128)(2,1)S(1)}, u32[]{:S(2)}, u32[]{:S(2)}) collective-permute-start(bf16[32,256]{1,0:T(8,128)(2,1)} %get-tuple-element.14), channel_id=1, source_target_pairs={{0,2},{1,3},{2,0},{3,1},{4,6},{5,7},{6,4},{7,5},{8,10},{9,11},{10,... | collective-permute-start | bytes 49160 | tf_op jit(solution)/shard_map/ppermute | solution.py:598
  7.4 0.1 collective-permute-start.2
  7.5 0.0 copy-done.7
  7.5 0.1 pad_add_fusion.1
  7.6 0.1 copy.32
  7.7 0.0 copy-done.8
  7.7 0.7 gather_fusion
  8.5 0.1 copy.34
  8.5 0.1 mul.22
  8.6 0.1 copy.33
  8.7 0.1 ge.21
  8.8 0.0 copy-done.11
  8.8 0.1 copy.35
  8.9 0.0 copy-done.6
  8.9 0.1 fusion.3
  9.0 0.7 fusion.5.refs_5_
  9.7 0.0 collective-permute-done.refs_1_
  9.7 0.0 collective-permute-done.1.refs_2_
  9.7 0.0 copy-start.4
  9.7 1.0 %collective-permute-done.2.refs_3_ = bf16[32,256]{1,0:T(8,128)(2,1)S(1)} collective-permute-done((bf16[32,256]{1,0:T(8,128)(2,1)}, bf16[32,256]{1,0:T(8,128)(2,1)S(1)}, u32[]{:S(2)}, u32[]{:S(2)}) %collective-permute-start.2) | collective-permute-done | bytes 16416 | tf_op jit(solution)/shard_map/ppermute | solution.py:598
  10.8 0.0 copy-done.3
  10.8 0.0 copy-done.4
  10.8 0.6 copy-done.5
  11.4 3.8 %assemble.1 = bf16[8,304,256]{2,1,0:T(8,128)(2,1)} custom-call(bf16[32,256]{1,0:T(8,128)(2,1)} %get-tuple-element.12.refs_0_, bf16[32,256]{1,0:T(8,128)(2,1)} %copy-done.3, bf16[32,256]{1,0:T(8,128)(2,1)} %copy-done.4, bf16[32,256]{1,0:T(8,128)(2,1)} %copy-done.5, bf16[128,512]{1,0:T(8,128)(2,1)} %get-tuple-element.16.refs_4_, bf16[16,256]{1,0:T(8,128)(2,1)} %fusion.5.refs_5_), custom_call_target="tpu_custom_call" | custom-call | tf_op jit(solution)/shard_map/assemble/pallas_call | solution.py:175
  15.1 0.0 copy-start.1
  15.1 6.0 %all-to-all-start = ((bf16[8,304,256]{2,1,0:T(8,128)(2,1)}), bf16[8,304,256]{2,1,0:T(8,128)(2,1)S(1)}, u32[]{:S(2)}, u32[]{:S(2)}) async-start(bf16[8,304,256]{2,1,0:T(8,128)(2,1)} %assemble.1), calls=%async_computation | async-start | bytes 2490368 | tf_op jit(solution)/shard_map/all_to_all | solution.py:602
  21.1 0.7 copy.36.bias_ref
  21.8 0.7 copy.37.bias_ref
  22.5 6.2 %all_gather.35.up_ref = bf16[8,128,128]{2,1,0:T(8,128)(2,1)} all-gather(bf16[8,32,128]{2,1,0:T(8,128)(2,1)S(1)} %copy-done.2), channel_id=1, replica_groups=mesh['brick'=8,'chan'=4] {'chan'}, dimensions={1}, use_global_device_ids=true | all-gather | bytes 327680 | tf_op jit(solution)/shard_map/all_gather | solution.py:610
  28.7 7.7 %all-gather.2 = bf16[16,32,512]{2,1,0:T(8,128)(2,1)} all-gather(bf16[4,32,512]{2,1,0:T(8,128)(2,1)S(1)} %copy-done.1), channel_id=4, replica_groups=mesh['brick'=8,'chan'=4] {'chan'}, dimensions={0}, use_global_device_ids=true | all-gather | bytes 655360 | tf_op jit(solution)/shard_map/all_gather | solution.py:608
  36.5 15.0 %all-to-all-done.refs_1_ = bf16[8,304,256]{2,1,0:T(8,128)(2,1)S(1)} async-done(((bf16[8,304,256]{2,1,0:T(8,128)(2,1)}), bf16[8,304,256]{2,1,0:T(8,128)(2,1)S(1)}, u32[]{:S(2)}, u32[]{:S(2)}) %all-to-all-start) | async-done | bytes 1245216 | tf_op jit(solution)/shard_map/all_to_all | solution.py:602
  51.5 0.1 fusion
  51.6 0.3 slice_reduce_fusion
  51.8 0.1 reshape_squeeze.6
  51.9 0.1 reshape_squeeze.5
  52.0 0.7 broadcast_in_dim_reshape_squeeze.3.parents_ref
  52.7 7.0 %all-gather = bf16[32,32,256]{2,1,0:T(8,128)(2,1)} all-gather(bf16[8,32,256]{2,1,0:T(8,128)(2,1)S(1)} %slice.30), channel_id=2, replica_groups=mesh['brick'=8,'chan'=4] {'chan'}, dimensions={0}, use_global_device_ids=true | all-gather | bytes 655360 | tf_op jit(solution)/shard_map/all_gather | solution.py:603
  59.7 0.6 gather_fusion.1
  60.2 0.7 broadcast_select_fusion.target_ref
  60.9 5.2 %coarse.1 = bf16[1,32,2048]{2,1,0:T(8,128)(2,1)} custom-call(bf16[4,8,32,256]{3,2,1,0:T(8,128)(2,1)} %bitcast.29, s32[32,27]{1,0:T(8,128)} %broadcast_select_fusion.target_ref, s32[1,32]{1,0:T(1,128)} %broadcast_in_dim_reshape_squeeze.3.parents_ref, bf16[27,32,128]{2,1,0:T(8,128)(2,1)} %w_ref.2, f32[32,1]{1,0:T(8,128)} %copy.36.bias_ref), custom_call_target="tpu_custom_call" | custom-call | flops 452984832 | bytes 2097152 | tf_op jit(solution)/shard_map/coarse/pallas_call | solution.py:306
  66.1 8.9 %all-gather.1 = bf16[4,32,2048]{2,1,0:T(8,128)(2,1)} all-gather(bf16[1,32,2048]{2,1,0:T(8,128)(2,1)} %coarse.1), channel_id=3, replica_groups=mesh['brick'=8,'chan'=4] {'chan'}, dimensions={0}, use_global_device_ids=true | all-gather | bytes 655360 | tf_op jit(solution)/shard_map/all_gather | solution.py:606
  75.0 2.5 %halo.1 = bf16[4,32,512]{2,1,0:T(8,128)(2,1)} custom-call(s32[4,26]{1,0:T(4,128)} %links_ref.1, bf16[8,304,256]{2,1,0:T(8,128)(2,1)} %copy-done), custom_call_target="tpu_custom_call" | custom-call | tf_op jit(solution)/shard_map/halo/pallas_call | solution.py:210
  77.4 8.5 %all-gather.3 = bf16[16,32,512]{2,1,0:T(8,128)(2,1)} all-gather(bf16[4,32,512]{2,1,0:T(8,128)(2,1)} %halo.1), channel_id=5, replica_groups=mesh['brick'=8,'chan'=4] {'chan'}, dimensions={0}, use_global_device_ids=true | all-gather | bytes 655360 | tf_op jit(solution)/shard_map/all_gather | solution.py:609
  85.9 2.7 %frames.1 = (bf16[100,48,128]{2,1,0:T(8,128)(2,1)}, bf16[1,9,48,128]{3,2,1,0:T(8,128)(2,1)}) custom-call(s32[1]{0:T(128)} %bitcast.11.owner_ref, s32[4,26]{1,0:T(4,128)} %links_ref.1, bf16[4,4,32,512]{3,2,1,0:T(8,128)(2,1)} %bitcast.26, bf16[4,4,32,512]{3,2,1,0:T(8,128)(2,1)} %bitcast.27), custom_call_target="tpu_custom_call" | custom-call | tf_op jit(solution)/shard_map/frames/pallas_call | solution.py:414
  88.6 6.3 %refine.1 = bf16[4,32,512]{2,1,0:T(8,128)(2,1)} custom-call(bf16[4,1,32,2048]{3,2,1,0:T(8,128)(2,1)} %bitcast.25, bf16[100,48,128]{2,1,0:T(8,128)(2,1)} %get-tuple-element.17.ff_ref, bf16[1,9,48,128]{3,2,1,0:T(8,128)(2,1)} %get-tuple-element.18.sel_ref, bf16[8,128,128]{2,1,0:T(8,128)(2,1)} %all_gather.35.up_ref, bf16[27,32,128]{2,1,0:T(8,128)(2,1)} %w_ref.3, ...), custom_call_target="tpu_custom_call" | custom-call | flops 452984832 | bytes 4194304 | tf_op jit(solution)/shard_map/refine/pallas_call | solution.py:524
  (26 shorter events, 0.1 us)
Async XLA Ops:
  0.0 7.7 %copy-start.8 = (s32[216]{0:T(256)S(1)}, s32[216]{0:T(256)}, u32[]{:S(2)}) copy-start(s32[216]{0:T(256)} %constant.94) | copy-start | bytes 2596
  0.0 8.9 %copy-start.6 = (s32[8,27]{1,0:T(8,128)S(1)}, s32[8,27]{1,0:T(8,128)}, u32[]{:S(2)}) copy-start(s32[8,27]{1,0:T(8,128)} %constant.93) | copy-start | bytes 2596
  0.0 7.5 %copy-start.7 = (s32[2,26]{1,0:T(2,128)S(1)}, s32[2,26]{1,0:T(2,128)}, u32[]{:S(2)}) copy-start(s32[2,26]{1,0:T(2,128)} %param.18) | copy-start | bytes 628
  0.0 8.8 %copy-start.11 = (s32[4]{0:T(128)S(1)}, s32[4]{0:T(128)}, u32[]{:S(2)}) copy-start(s32[4]{0:T(128)} %param.19) | copy-start | bytes 52
  4.4 5.3 %collective-permute-start = (bf16[32,256]{1,0:T(8,128)(2,1)}, bf16[32,256]{1,0:T(8,128)(2,1)S(1)}, u32[]{:S(2)}, u32[]{:S(2)}) collective-permute-start(bf16[32,256]{1,0:T(8,128)(2,1)} %get-tuple-element.13), channel_id=1, source_target_pairs={{0,1},{1,0},{2,3},{3,2},{4,5},{5,4},{6,7},{7,6},{8,9},{9,8},{10,11... | collective-permute-start | bytes 49160 | tf_op jit(solution)/shard_map/ppermute | solution.py:598
  4.8 4.9 %collective-permute-start.1 = (bf16[32,256]{1,0:T(8,128)(2,1)}, bf16[32,256]{1,0:T(8,128)(2,1)S(1)}, u32[]{:S(2)}, u32[]{:S(2)}) collective-permute-start(bf16[32,256]{1,0:T(8,128)(2,1)} %get-tuple-element.14), channel_id=1, source_target_pairs={{0,2},{1,3},{2,0},{3,1},{4,6},{5,7},{6,4},{7,5},{8,10},{9,11},{10,... | collective-permute-start | bytes 49160 | tf_op jit(solution)/shard_map/ppermute | solution.py:598
  7.4 3.4 %collective-permute-start.2 = (bf16[32,256]{1,0:T(8,128)(2,1)}, bf16[32,256]{1,0:T(8,128)(2,1)S(1)}, u32[]{:S(2)}, u32[]{:S(2)}) collective-permute-start(bf16[32,256]{1,0:T(8,128)(2,1)} %get-tuple-element.15), channel_id=1, source_target_pairs={{0,3},{1,2},{2,1},{3,0},{4,7},{5,6},{6,5},{7,4},{8,11},{9,10},{10,... | collective-permute-start | bytes 49160 | tf_op jit(solution)/shard_map/ppermute | solution.py:598
  9.7 1.1 %copy-start.3 = (bf16[32,256]{1,0:T(8,128)(2,1)}, bf16[32,256]{1,0:T(8,128)(2,1)S(1)}, u32[]{:S(2)}) copy-start(bf16[32,256]{1,0:T(8,128)(2,1)S(1)} %collective-permute-done.refs_1_) | copy-start | bytes 49156
  9.7 1.1 %copy-start.4 = (bf16[32,256]{1,0:T(8,128)(2,1)}, bf16[32,256]{1,0:T(8,128)(2,1)S(1)}, u32[]{:S(2)}) copy-start(bf16[32,256]{1,0:T(8,128)(2,1)S(1)} %collective-permute-done.1.refs_2_) | copy-start | bytes 49156
  10.8 0.6 copy-start.5
  15.1 6.0 %copy-start.9 = (f32[32]{0:T(128)S(1)}, f32[32]{0:T(128)}, u32[]{:S(2)}) copy-start(f32[32]{0:T(128)} %param.24) | copy-start | bytes 388
  15.1 6.7 %copy-start.10 = (f32[32]{0:T(128)S(1)}, f32[32]{0:T(128)}, u32[]{:S(2)}) copy-start(f32[32]{0:T(128)} %param.25) | copy-start | bytes 388
  15.1 7.4 %copy-start.2 = (bf16[8,32,128]{2,1,0:T(8,128)(2,1)S(1)}, bf16[8,32,128]{2,1,0:T(8,128)(2,1)}, u32[]{:S(2)}) copy-start(bf16[8,32,128]{2,1,0:T(8,128)(2,1)} %param.22) | copy-start | bytes 196612
  15.1 13.6 %copy-start.1 = (bf16[4,32,512]{2,1,0:T(8,128)(2,1)S(1)}, bf16[4,32,512]{2,1,0:T(8,128)(2,1)}, u32[]{:S(2)}) copy-start(bf16[4,32,512]{2,1,0:T(8,128)(2,1)} %param.16) | copy-start | bytes 393220
  15.1 36.3 %all-to-all-start = ((bf16[8,304,256]{2,1,0:T(8,128)(2,1)}), bf16[8,304,256]{2,1,0:T(8,128)(2,1)S(1)}, u32[]{:S(2)}, u32[]{:S(2)}) async-start(bf16[8,304,256]{2,1,0:T(8,128)(2,1)} %assemble.1), calls=%async_computation | async-start | bytes 2490368 | tf_op jit(solution)/shard_map/all_to_all | solution.py:602
  51.4 14.6 %copy-start = (bf16[8,304,256]{2,1,0:T(8,128)(2,1)}, bf16[8,304,256]{2,1,0:T(8,128)(2,1)S(1)}, u32[]{:S(2)}) copy-start(bf16[8,304,256]{2,1,0:T(8,128)(2,1)S(1)} %all-to-all-done.refs_1_) | copy-start | bytes 3735556
where the time goes:
time: 95.4 us; the launch traced here: 94.9 us
  blocking collectives  38.3 us (40%)
  Pallas kernels  23 us (24%)
  waiting for transfers between devices  16 us (17%)
  starting transfers between devices  9.07 us (10%)
  local copies, waits for them, and re-layouts  6.68 us (7%)
  other arithmetic  1.66 us (2%)
    all_to_all x1, waiting for transfers between devices, per_device(): lax.all_to_all(sending, 'brick', split_axis=0, concat_axis=0, tiled=True)  15 us
    all_gather x1, blocking collectives, per_device(): co = lax.all_gather(co, 'chan', axis=0)  8.87 us
    all_gather x1, blocking collectives, per_device(): fh = lax.all_gather(around, 'chan', axis=0)  8.51 us
    all_gather x1, blocking collectives, per_device(): fi = lax.all_gather(features, 'chan', axis=0)  7.72 us
    all_gather x1, blocking collectives, per_device(): proj = lax.all_gather(recv[:, :q], 'chan', axis=0)  6.96 us
    pallas_call x1, Pallas kernels, refine(): pl.pallas_call(fine_kernel, out_shape=jax.ShapeDtypeStruct((fine, q, EDGE...  6.32 us
    all_gather x1, blocking collectives, per_device(): up_all = lax.all_gather(up_weight, 'chan', axis=1, tiled=True)  6.25 us
    all_to_all x1, starting transfers between devices, per_device(): lax.all_to_all(sending, 'brick', split_axis=0, concat_axis=0, tiled=True)  5.95 us
  transfers between devices with their start and end apart: 4, of which 2 were waited for; matrix products, arithmetic and copies ran while one was open for 4% of the time, Pallas kernels for 0%

commit v1 on v0

--- a/solution.py
+++ b/solution.py
@@ -33,12 +33,10 @@
 
 
 def piece_lanes():
-    starts, at = [], 0
     order = sorted(
         range(len(HEADINGS)), key=lambda k: (sum(1 for e in HEADINGS[k] if e), k)
     )
-    starts = [0] * len(HEADINGS)
-    voxels = [None] * len(HEADINGS)
+    starts, voxels, at = [0] * len(HEADINGS), [None] * len(HEADINGS), 0
     for k in order:
         spans = [
             [0] if e == 1 else [EDGE - 1] if e == -1 else list(range(EDGE))
@@ -56,6 +54,19 @@
 
 
 STARTS, VOXELS = piece_lanes()
+for k in (2, 3):
+    VOXELS[k] = [VOXELS[k][x * EDGE + z] for z in range(EDGE) for x in range(EDGE)]
+SENT = [v for k in range(6) for v in VOXELS[k]]
+SOURCES = []
+for k, heading in enumerate(HEADINGS):
+    for f in range(6):
+        run = VOXELS[f]
+        want = VOXELS[k]
+        first = run.index(want[0]) if want[0] in run else -1
+        if first >= 0 and run[first : first + len(want)] == want:
+            SOURCES.append(EDGE**2 * f + first)
+            break
+assert len(SOURCES) == len(HEADINGS)
 
 
 def octant_selector():
@@ -70,10 +81,9 @@
 
 
 def outer_selector():
-    sel = np.zeros((EDGE**3, EDGE**3), np.float32)
-    for k in range(len(HEADINGS)):
-        for i, v in enumerate(VOXELS[k]):
-            sel[v, STARTS[k] + i] = 1
+    sel = np.zeros((EDGE**3, len(SENT)), np.float32)
+    for i, v in enumerate(SENT):
+        sel[v, i] = 1
     return sel
 
 
@@ -107,37 +117,36 @@
 SM = pltpu.SMEM
 
 
-def project_kernel(chans, me_ref, f_ref, oct_ref, outer_ref, w_ref, *rest):
-    outs, hs_ref, part = rest[:chans], rest[chans], rest[chans + 1]
-    q = w_ref.shape[2]
+def project_kernel(chans, me_ref, f_ref, oct_ref, w_ref, *rest):
+    outs, part = rest[:chans], rest[chans]
+    q = w_ref.shape[1]
     fine = f_ref.shape[0] // q
-    x = f_ref[...]
-    picked = dot(x, oct_ref[...]).astype(BF16)
+    picked = dot(f_ref[...], oct_ref[...]).astype(BF16)
     acc = None
     for o in range(8):
         z = jnp.concatenate(
             [picked[b * q : (b + 1) * q, o * CUBE : (o + 1) * CUBE] for b in range(fine)],
             axis=1,
         )
-        term = dot(w_ref[o], z)
+        term = lax.dot_general(
+            w_ref[o], z, (((0,), (0,)), ((), ())), preferred_element_type=F32
+        )
         acc = term if acc is None else acc + term
     part[...] = acc
     me = me_ref[0]
     for s in range(chans):
         outs[s][...] = part[pl.ds(pl.multiple_of((me ^ s) * q, q), q), :].astype(BF16)
-    hs_ref[...] = dot(x, outer_ref[...]).astype(BF16)
 
 
 def project(me, features, down_weight, chans):
     fine, q, vox = features.shape
     c_out = down_weight.shape[1]
     lanes = fine * CUBE
-    res = pl.pallas_call(
+    return pl.pallas_call(
         lambda *refs: project_kernel(chans, *refs),
-        out_shape=[jax.ShapeDtypeStruct((q, lanes), BF16)] * chans
-        + [jax.ShapeDtypeStruct((fine * q, vox), BF16)],
-        in_specs=[pl.BlockSpec(memory_space=SM)] + [pl.BlockSpec(memory_space=VM)] * 4,
-        out_specs=[pl.BlockSpec(memory_space=VM)] * (chans + 1),
+        out_shape=[jax.ShapeDtypeStruct((q, lanes), BF16)] * chans,
+        in_specs=[pl.BlockSpec(memory_space=SM)] + [pl.BlockSpec(memory_space=VM)] * 3,
+        out_specs=[pl.BlockSpec(memory_space=VM)] * chans,
         scratch_shapes=[pltpu.VMEM((c_out, lanes), F32)],
         compiler_params=params(),
         cost_estimate=cost(2 * c_out * 8 * q * lanes, 2 * 1024 * 1024),
@@ -146,52 +155,99 @@
         me,
         features.reshape(fine * q, vox),
         jnp.asarray(octant_selector(), BF16),
-        jnp.asarray(outer_selector(), BF16),
-        down_weight,
+        jnp.transpose(down_weight, (0, 2, 1)),
     )
-    return res[:chans], res[chans]
-
-
-def assemble_kernel(chans, *refs):
-    slots, hs_ref, meta_ref, out_ref = refs[:chans], refs[chans], refs[chans + 1], refs[chans + 2]
+
+
+def spread_kernel(f_ref, up_ref, sel_ref, out_ref, pack_ref):
+    rows, vox = f_ref.shape
+    out_ref[...] = dot(f_ref[...], sel_ref[...]).astype(BF16)
+    pack_ref[0:rows] = f_ref[...]
+    more = up_ref.shape[0] * up_ref.shape[1] // vox
+    for i in range(vox // up_ref.shape[1]):
+        part = slice(i * up_ref.shape[1], (i + 1) * up_ref.shape[1])
+        pack_ref[rows : rows + more, part] = up_ref[i * more : (i + 1) * more]
+
+
+def spread_out(features, up_weight):
+    fine, q, vox = features.shape
+    ups = up_weight.reshape(-1, up_weight.shape[2])
+    return pl.pallas_call(
+        spread_kernel,
+        out_shape=[
+            jax.ShapeDtypeStruct((fine * q, len(SENT)), BF16),
+            jax.ShapeDtypeStruct((fine * q + ups.size // vox, vox), BF16),
+        ],
+        in_specs=[pl.BlockSpec(memory_space=VM)] * 3,
+        out_specs=[pl.BlockSpec(memory_space=VM)] * 2,
+        compiler_params=params(),
+        name="spread",
+    )(features.reshape(fine * q, vox), ups, jnp.asarray(outer_selector(), BF16))
+
+
+def assemble_kernel(owner_ref, links_ref, parents_ref, table_ref, *refs):
+    slots, outer_ref, out_ref = refs[:-2], refs[-2], refs[-1]
+    count, ways = links_ref.shape
     total = slots[0][...].astype(F32)
     for s in slots[1:]:
         total = total + s[...].astype(F32)
     q, lanes = slots[0].shape
-    rows = hs_ref.shape[0]
-    out_ref[0, 0:q, :] = total.astype(BF16)
-    at = q
-    for h in range(hs_ref.shape[1] // lanes):
-        out_ref[0, at : at + rows, :] = hs_ref[:, h * lanes : (h + 1) * lanes]
-        at += rows
-    out_ref[0, at : at + meta_ref.shape[0], :] = meta_ref[...]
-
-
-def assemble(slots, outer, meta, owners):
+    total = total.astype(BF16)
+    rows = count * 8
+    column, octant = table_ref[0], table_ref[1]
+    row = lax.broadcasted_iota(jnp.int32, (rows, 128), 0)
+    lane = lax.broadcasted_iota(jnp.int32, (rows, 128), 1)
+    code = jnp.zeros((rows, 128), jnp.int32)
+    for p in range(count):
+        own = row // 8 == p
+        for k in range(ways + 1):
+            brick = owner_ref[0] * count + p if k == ways else links_ref[p, k]
+            code = jnp.where(own & (column == k), jnp.where(brick >= 0, brick * 8 + octant + 1, 0), code)
+    for b in range(parents_ref.shape[0]):
+        code = jnp.where((row == b) & (lane == 27), parents_ref[b] + 1, code)
+    high = lax.shift_right_logical(code, 7)
+    digits = [high.astype(F32).astype(BF16), (code - high * 128).astype(F32).astype(BF16)]
+    for w in range(out_ref.shape[0]):
+        out_ref[w, 0:q, :] = total
+        for i in range(2):
+            out_ref[w, q : q + rows, 128 * i : 128 * i + 128] = digits[i]
+        at, n = q + rows, outer_ref.shape[0]
+        out_ref[w, at : at + n, :] = outer_ref[:, 0:256]
+        for i in range(2):
+            out_ref[w, at + n : at + n + n // 2, 128 * i : 128 * i + 128] = outer_ref[
+                i * n // 2 : (i + 1) * n // 2, 256:384
+            ]
+
+
+def assemble(slots, outer, owner, coarse_links, parents, owners):
     q, lanes = slots[0].shape
-    rows = q + outer.shape[0] * outer.shape[1] // lanes + meta.shape[0]
-    whole = lambda a: pl.BlockSpec(a.shape, lambda i: (0,) * a.ndim)
-    ins = list(slots) + [outer, meta]
+    count = coarse_links.shape[0]
+    columns, octants = octant_table()
+    table = np.full((2, count * 8, 128), -1, np.int32)
+    table[0, :, :27] = np.tile(columns, (count, 1))
+    table[1, :, :27] = np.tile(octants, (count, 1))
     return pl.pallas_call(
-        lambda *refs: assemble_kernel(len(slots), *refs),
-        out_shape=jax.ShapeDtypeStruct((owners, rows, lanes), BF16),
-        grid=(owners,),
-        in_specs=[whole(a) for a in ins],
-        out_specs=pl.BlockSpec((1, rows, lanes), lambda i: (i, 0, 0)),
+        assemble_kernel,
+        out_shape=jax.ShapeDtypeStruct((owners, q + count * 8 + outer.size // lanes, lanes), BF16),
+        in_specs=[pl.BlockSpec(memory_space=SM)] * 3 + [pl.BlockSpec(memory_space=VM)] * (len(slots) + 2),
+        out_specs=pl.BlockSpec(memory_space=VM),
         compiler_params=params(),
         name="assemble",
-    )(*ins)
-
-
-def halo_kernel(q, links_ref, recv_ref, out_ref):
+    )(owner, coarse_links, parents, jnp.asarray(table), *slots, outer)
+
+
+def exchanged(x, chans):
+    return [x] + [
+        lax.ppermute(x, "chan", [(i, i ^ s) for i in range(chans)]) for s in range(1, chans)
+    ]
+
+
+def halo_kernel(q, base, links_ref, recv_ref, out_ref):
     fine = out_ref.shape[0]
-    lanes = recv_ref.shape[2]
     lane = lax.broadcasted_iota(jnp.int32, (q, 128), 1)
     for b in range(fine):
         for chunk in range(out_ref.shape[2] // 128):
             here = jnp.zeros((q, 128), F32)
-            base = q + (chunk * 128 // lanes) * fine * q
-            col = chunk * 128 % lanes
             for k in range(len(HEADINGS)):
                 if STARTS[k] // 128 != chunk:
                     continue
@@ -199,16 +255,26 @@
                 last = first + len(VOXELS[k])
                 m = links_ref[b, k]
                 safe = jnp.maximum(m, 0)
-                row = pl.multiple_of(base + lax.rem(safe, fine) * q, 16)
-                got = recv_ref[lax.div(safe, fine), pl.ds(row, q), col : col + 128].astype(F32)
+                col = SOURCES[k] // 128
+                row = lax.rem(safe, fine)
+                if col < 2:
+                    lanes = pl.ds(128 * col, 128)
+                else:
+                    lanes = pl.ds(pl.multiple_of(lax.div(row, fine // 2) * 128, 128), 128)
+                    row = fine + lax.rem(row, fine // 2)
+                row = pl.multiple_of(base + row * q, 16)
+                got = recv_ref[lax.div(safe, fine), pl.ds(row, q), lanes].astype(F32)
+                turn = (first - SOURCES[k]) % 128
+                if turn:
+                    got = pltpu.roll(got, turn, 1)
                 got = jnp.where(m >= 0, got, 0.0)
                 here = jnp.where((lane >= first) & (lane < last), got, here)
             out_ref[b, :, chunk * 128 : (chunk + 1) * 128] = here.astype(BF16)
 
 
-def halo(links, recv, fine, q, vox):
+def halo(links, recv, base, fine, q, vox):
     return pl.pallas_call(
-        lambda *refs: halo_kernel(q, *refs),
+        lambda *refs: halo_kernel(q, base, *refs),
         out_shape=jax.ShapeDtypeStruct((fine, q, vox), BF16),
         in_specs=[pl.BlockSpec(memory_space=SM), pl.BlockSpec(memory_space=VM)],
         out_specs=pl.BlockSpec(memory_space=VM),
@@ -226,8 +292,18 @@
     return found
 
 
-def coarse_kernel(proj_ref, target_ref, parents_ref, w_ref, bias_ref, out_ref, rows_ref, sel_ref, nb_ref):
-    chans, owners, q, lanes = proj_ref.shape
+def bias_column(row):
+    n = row.shape[1]
+    square = jnp.broadcast_to(row, (n, n))
+    on = lax.broadcasted_iota(jnp.int32, (n, n), 0) == lax.broadcasted_iota(jnp.int32, (n, n), 1)
+    return jnp.sum(jnp.where(on, square, 0.0), axis=1, keepdims=True)
+
+
+def coarse_kernel(chans, codes, me_ref, *refs):
+    slots, refs = refs[:chans], refs[chans:]
+    recv_ref, w_ref, bias_ref, out_ref, proj_ref, rows_ref, sel_ref, nb_ref, parent_ref, table_ref = refs
+    owners, q, lanes = slots[0].shape
+    me = me_ref[0]
     fine = lanes // CUBE
     total = owners * fine
 
@@ -240,16 +316,29 @@
 
     @pl.when(pl.program_id(0) == 0)
     def _():
+        for w in range(owners):
+            digits = recv_ref[w, q : q + codes, :]
+            table_ref[w * codes : (w + 1) * codes, :] = digits
+            digits = digits.astype(F32)
+            value = digits[:, 0:128] * 128.0 + digits[:, 128:256] - 1.0
+            parent_ref[w * fine : (w + 1) * fine, :] = jnp.broadcast_to(value[0:fine, 27:28], (fine, 128))
+        for s in range(chans):
+            proj_ref[me ^ s] = slots[s][...]
         if owners <= 8:
             for w in range(owners):
                 spread(w, 0)
         else:
             lax.fori_loop(0, owners, spread, 0)
 
+    mine = parent_ref[pl.ds(pl.program_id(0) * NBLK, NBLK), :]
+    row = lax.broadcasted_iota(jnp.int32, (NBLK, table_ref.shape[0]), 1).astype(F32)
+    own = (mine[:, 0:1] == row).astype(F32).astype(BF16)
+    digits = dot(own, table_ref[...])
+    target = digits[:, 0:128] * 128.0 + digits[:, 128:256] - 1.0
+    on = lax.broadcasted_iota(jnp.int32, (total, total), 0) == lax.broadcasted_iota(jnp.int32, (total, total), 1)
+    parents = jnp.sum(jnp.where(on, parent_ref[:, 0:1], 0.0), axis=0, keepdims=True)
     for d in range(27):
-        sel_ref[d * NBLK : (d + 1) * NBLK, :] = (
-            (target_ref[:, d : d + 1] == parents_ref[0:1, :]).astype(F32).astype(BF16)
-        )
+        sel_ref[d * NBLK : (d + 1) * NBLK, :] = (target[:, d : d + 1] == parents).astype(F32).astype(BF16)
     for ux in range(HALF):
         for uy in range(HALF):
             for uz in range(HALF):
@@ -276,7 +365,7 @@
     step = HALF * HALF * NBLK
     n = HALF * step
     res = acc[0:q, 0:n] + acc[q : 2 * q, step : step + n] + acc[2 * q : 3 * q, 2 * step : 2 * step + n]
-    out_ref[0] = jnp.maximum(res + bias_ref[...], 0.0).astype(BF16)
+    out_ref[0] = jnp.maximum(res + bias_column(bias_ref[...]), 0.0).astype(BF16)
 
 
 def conv_rows(w_ref, rows_of):
@@ -297,33 +386,37 @@
     return acc
 
 
-def coarse(proj, target, parents, weight, bias):
-    chans, owners, q, lanes = proj.shape
+def coarse(me, slots, recv, codes, weight, bias):
+    chans = len(slots)
+    owners, q, lanes = slots[0].shape
     total = owners * lanes // CUBE
     blocks = total // NBLK
     c_in = weight.shape[2]
     whole = lambda a: pl.BlockSpec(a.shape, lambda i: (0,) * a.ndim)
     return pl.pallas_call(
-        coarse_kernel,
+        lambda *refs: coarse_kernel(chans, codes, *refs),
         out_shape=jax.ShapeDtypeStruct((blocks, q, CUBE * NBLK), BF16),
         grid=(blocks,),
-        in_specs=[
-            whole(proj),
-            pl.BlockSpec((NBLK, target.shape[1]), lambda i: (i, 0)),
-            whole(parents),
+        in_specs=[pl.BlockSpec(memory_space=SM)]
+        + [whole(a) for a in slots]
+        + [
+            pl.BlockSpec((owners, q + codes, recv.shape[2]), lambda i: (0, 0, 0)),
             whole(weight),
             whole(bias),
         ],
         out_specs=pl.BlockSpec((1, q, CUBE * NBLK), lambda i: (i, 0, 0)),
         scratch_shapes=[
+            pltpu.VMEM((chans, owners, q, lanes), BF16),
             pltpu.VMEM((CUBE * total, c_in), F32),
             pltpu.VMEM((27 * NBLK, total), BF16),
             pltpu.VMEM((HALF + 2, HALF + 2, HALF + 2, NBLK, c_in), BF16),
+            pltpu.VMEM((total, 128), F32),
+            pltpu.VMEM((owners * codes, 256), BF16),
         ],
         compiler_params=params(),
         cost_estimate=cost(2 * 27 * c_in * q * CUBE * total, 2 * 1024 * 1024),
         name="coarse",
-    )(proj, target, parents, weight, bias)
+    )(me, *slots, recv, weight, bias)
 
 
 def frame_axis(f):
@@ -334,13 +427,23 @@
     return 0, f - 1
 
 
-def frame_kernel(owner_ref, links_ref, fi_ref, fh_ref, ff_ref, sel_ref, inner, outer, plane):
-    chans, fine, q, vox = fi_ref.shape
-    span = 8 * fine
+def frame_kernel(chans, me_ref, owner_ref, links_ref, *refs):
+    packs, halos, refs = refs[:chans], refs[chans : 2 * chans], refs[2 * chans :]
+    ff_ref, sel_ref, up_ref, both, inner, outer, plane = refs
+    fine, q, vox = halos[0].shape
     owner = owner_ref[0]
+    me = me_ref[0]
+    for s in range(chans):
+        at = pl.ds(pl.multiple_of((me ^ s) * q, q), q)
+        for b in range(fine):
+            both[0, b, at, :] = packs[s][b * q : (b + 1) * q, :]
+            both[1, b, at, :] = halos[s][b]
+        for o in range(8):
+            row = (fine + o % 2) * q
+            up_ref[o, at, :] = packs[s][row : row + q, o // 2 * 128 : o // 2 * 128 + 128]
     for b in range(fine):
-        inner[b] = jnp.concatenate([fi_ref[c, b] for c in range(chans)], axis=0).astype(F32).T
-        outer[b] = jnp.concatenate([fh_ref[c, b] for c in range(chans)], axis=0).astype(F32).T
+        inner[b] = both[0, b].astype(F32).T
+        outer[b] = both[1, b].astype(F32).T
     for b in range(fine):
         for s in range(2):
             dz = 2 * s - 1
@@ -369,10 +472,10 @@
                 else:
                     start = STARTS[HEADING_INDEX[(dx, dy, 0)]]
                     if dx == 0:
-                        start += vx * EDGE
-                    elif dy == 0:
-                        start += vy * EDGE
-                    tiles.append(outer[b, start : start + EDGE, :])
+                        tiles.append(outer[b, pl.ds(start + vx, EDGE, stride=EDGE), :])
+                    else:
+                        start += 0 if dy else vy * EDGE
+                        tiles.append(outer[b, start : start + EDGE, :])
             tiles.append(plane[(fx * FRAME + fy) * 8 : (fx * FRAME + fy) * 8 + 8, :])
             tiles.append(jnp.zeros((8, plane.shape[1]), F32))
             ff_ref[at] = jnp.concatenate(tiles, axis=0).astype(BF16)
@@ -408,30 +511,38 @@
         lax.fori_loop(0, blocks, pick, 0)
 
 
-def frames(owner, links, inner, outer, blocks):
-    chans, fine, q, vox = inner.shape
+def frames(me, owner, links, packs, halos, blocks):
+    chans = len(packs)
+    fine, q, vox = halos[0].shape
     rows = 8 * fine + 16
+    c_all = chans * q
     return pl.pallas_call(
-        frame_kernel,
+        lambda *refs: frame_kernel(chans, *refs),
         out_shape=[
-            jax.ShapeDtypeStruct((FRAME * FRAME, rows, chans * q), BF16),
+            jax.ShapeDtypeStruct((FRAME * FRAME, rows, c_all), BF16),
             jax.ShapeDtypeStruct((blocks, 9, rows, 128), BF16),
+            jax.ShapeDtypeStruct((8, c_all, c_all), BF16),
         ],
-        in_specs=[pl.BlockSpec(memory_space=SM)] * 2 + [pl.BlockSpec(memory_space=VM)] * 2,
-        out_specs=[pl.BlockSpec(memory_space=VM)] * 2,
+        in_specs=[pl.BlockSpec(memory_space=SM)] * 3 + [pl.BlockSpec(memory_space=VM)] * (2 * chans),
+        out_specs=[pl.BlockSpec(memory_space=VM)] * 3,
         scratch_shapes=[
-            pltpu.VMEM((fine, vox, chans * q), F32),
-            pltpu.VMEM((fine, vox, chans * q), F32),
-            pltpu.VMEM((FRAME * FRAME * 8, chans * q), F32),
+            pltpu.VMEM((2, fine, c_all, vox), BF16),
+            pltpu.VMEM((fine, vox, c_all), F32),
+            pltpu.VMEM((fine, vox, c_all), F32),
+            pltpu.VMEM((FRAME * FRAME * 8, c_all), F32),
         ],
         compiler_params=params(),
         name="frames",
-    )(owner, links, inner, outer)
-
-
-def fine_kernel(co_ref, ff_ref, sel_ref, up_ref, w_ref, bias_ref, pair_ref, out_ref, cr, g3):
-    chans, blocks, q, _ = co_ref.shape
+    )(me, owner, links, *packs, *halos)
+
+
+def fine_kernel(chans, me_ref, *refs):
+    slots, refs = refs[:chans], refs[chans:]
+    ff_ref, sel_ref, up_ref, w_ref, bias_ref, pair_ref, out_ref, co_ref, cr, g3 = refs
+    blocks, q, _ = slots[0].shape
     c_all = chans * q
+    for s in range(chans):
+        co_ref[me_ref[0] ^ s] = slots[s][...]
     fine = out_ref.shape[0]
     rows = ff_ref.shape[1]
     for ux in range(HALF):
@@ -503,37 +614,40 @@
                             g3[a3, pair, fx, 2 * j + 1 - py] = tile[j]
     step = EDGE * 2 * EDGE
     n = EDGE * step
+    bias = bias_column(bias_ref[...])
     for pair in range(fine // 2):
         acc = conv_rows(
             w_ref,
             lambda a2, a3: g3[a3, pair, :, a2 : a2 + EDGE].reshape(FRAME * step, c_all),
         )
         res = acc[0:q, 0:n] + acc[q : 2 * q, step : step + n] + acc[2 * q : 3 * q, 2 * step : 2 * step + n]
-        res = jnp.maximum(res + bias_ref[...], 0.0).astype(BF16)
+        res = jnp.maximum(res + bias, 0.0).astype(BF16)
         for h in range(n // 256):
             turned = dot(res[:, 256 * h : 256 * h + 256], pair_ref[...]).astype(BF16)
             for b in range(2):
                 out_ref[2 * pair + b, :, 128 * h : 128 * h + 128] = turned[:, 128 * b : 128 * b + 128]
 
 
-def refine(co, ff, sel, up_weight, weight, bias):
-    chans, blocks, q, _ = co.shape
+def refine(me, slots, ff, sel, up_weight, weight, bias):
+    chans = len(slots)
+    blocks, q, wide = slots[0].shape
     rows = ff.shape[1]
     fine = (rows - 16) // 8
     c_all = chans * q
     return pl.pallas_call(
-        fine_kernel,
+        lambda *refs: fine_kernel(chans, *refs),
         out_shape=jax.ShapeDtypeStruct((fine, q, EDGE**3), BF16),
-        in_specs=[pl.BlockSpec(memory_space=VM)] * 7,
+        in_specs=[pl.BlockSpec(memory_space=SM)] + [pl.BlockSpec(memory_space=VM)] * (chans + 6),
         out_specs=pl.BlockSpec(memory_space=VM),
         scratch_shapes=[
+            pltpu.VMEM((chans, blocks, q, wide), BF16),
             pltpu.VMEM((HALF + 2, HALF + 2, rows, c_all), BF16),
             pltpu.VMEM((3, fine // 2, FRAME, FRAME, 2 * EDGE, c_all), BF16),
         ],
         compiler_params=params(),
         cost_estimate=cost(2 * 27 * c_all * q * fine * EDGE**3, 4 * 1024 * 1024),
         name="refine",
-    )(co, ff, sel, up_weight, weight, bias, jnp.asarray(pair_selector(), BF16))
+    )(me, *slots, ff, sel, up_weight, weight, bias, jnp.asarray(pair_selector(), BF16))
 
 
 def octant_table():
@@ -551,27 +665,6 @@
             columns[o, d] = HEADING_INDEX[tuple(cross)]
             octants[o, d] = land[0] * 4 + land[1] * 2 + land[2]
     return columns, octants
-
-
-def described(coarse_links, parents, owner, lanes):
-    count = coarse_links.shape[0]
-    columns, octants = octant_table()
-    mine = owner * count + jnp.arange(count, dtype=jnp.int32)
-    links = jnp.concatenate([coarse_links, mine[:, None]], axis=1)
-    there = links[:, columns.reshape(-1)].reshape(count, 8, 27)
-    codes = jnp.where(there >= 0, there * 8 + octants[None], -1).reshape(count * 8, 27) + 1
-    ups = jnp.pad(parents[:, None] + 1, ((0, count * 8 - parents.shape[0]), (0, 0)))
-    both = jnp.concatenate([codes, ups], axis=1)
-    digits = jnp.concatenate([both // 128, both % 128], axis=1)
-    return jnp.pad(digits, ((0, 0), (0, lanes - digits.shape[1]))).astype(BF16)
-
-
-def understood(meta, fine):
-    value = meta[:, :, :56].astype(jnp.int32)
-    value = value[:, :, :28] * 128 + value[:, :, 28:] - 1
-    table = value[:, :, :27].reshape(-1, 27)
-    parents = value[:, :fine, 27].reshape(-1)
-    return jnp.take(table, parents, axis=0), parents[None, :]
 
 
 def per_device(
@@ -591,25 +684,24 @@
     owner = lax.axis_index("brick").astype(jnp.int32)
     me = lax.axis_index("chan").astype(jnp.int32)
     fine, q, vox = features.shape
-    lanes = fine * CUBE
-    meta = described(coarse_links, parents, owner, lanes)
-    slots, outer = project(me[None], features, down_weight, chans)
-    arrived = [slots[0]] + [
-        lax.ppermute(slots[s], "chan", [(i, i ^ s) for i in range(chans)])
+    parts = project(me[None], features, down_weight, chans)
+    arrived = [parts[0]] + [
+        lax.ppermute(parts[s], "chan", [(i, i ^ s) for i in range(chans)])
         for s in range(1, chans)
     ]
-    sending = assemble(arrived, outer, meta, owners)
+    early, _ = lax.optimization_barrier((features, parts[0]))
+    outer, packed = spread_out(early, up_weight)
+    codes = 8 * coarse_links.shape[0]
+    sending = assemble(arrived, outer, owner[None], coarse_links, parents, owners)
     recv = lax.all_to_all(sending, "brick", split_axis=0, concat_axis=0, tiled=True)
-    proj = lax.all_gather(recv[:, :q], "chan", axis=0)
-    target, all_parents = understood(recv[:, recv.shape[1] - meta.shape[0] :], fine)
-    co = coarse(proj, target, all_parents, coarse_weight, coarse_bias[:, None])
-    co = lax.all_gather(co, "chan", axis=0)
-    around = halo(fine_links, recv, fine, q, vox)
-    fi = lax.all_gather(features, "chan", axis=0)
-    fh = lax.all_gather(around, "chan", axis=0)
-    up_all = lax.all_gather(up_weight, "chan", axis=1, tiled=True)
-    ff, sel = frames(owner[None], fine_links, fi, fh, co.shape[1])
-    return refine(co, ff, sel, up_all, fine_weight, fine_bias[:, None])
+    packs = exchanged(packed, chans)
+    recv, packs = lax.optimization_barrier((recv, packs))
+    slots = exchanged(recv[:, :q], chans)
+    co = coarse(me[None], slots, recv, codes, coarse_weight, coarse_bias[None])
+    halos = exchanged(halo(fine_links, recv, q + codes, fine, q, vox), chans)
+    cos = exchanged(co, chans)
+    ff, sel, up_all = frames(me[None], owner[None], fine_links, packs, halos, co.shape[0])
+    return refine(me[None], cos, ff, sel, up_all, fine_weight, fine_bias[None])
 
 
 def solution(mesh):

time: 95.4 us -> 71.9 us (0.75)
  blocking collectives: 38.3 us -> 0 us
  waiting for transfers between devices: 16 us -> 27.2 us
  starting transfers between devices: 9.07 us -> 17 us
  local copies, waits for them, and re-layouts: 6.68 us -> 3.35 us
  other arithmetic: 1.66 us -> 0 us
    all_gather x5 -> x0, blocking collectives: 38.3 us -> none  [the longest x1 8.87 us: per_device(): co = lax.all_gather(co, 'chan', axis=0)]
    ppermute x3 -> x15, waiting for transfers between devices: 1.04 us -> 13.9 us  [the longest x12 12.7 us: exchanged(): lax.ppermute(x, 'chan', [(i, i ^ s) for i in range(chans)])]
    ppermute x3 -> x15, starting transfers between devices: 3.12 us -> 11.1 us  [the longest x12 7.93 us: exchanged(): lax.ppermute(x, 'chan', [(i, i ^ s) for i in range(chans)])]
    all_to_all x1, waiting for transfers between devices: 15 us -> 13.3 us  [per_device(): lax.all_to_all(sending, 'brick', split_axis=0, concat_axis=0, tiled=True)]
    broadcast_in_dim x2 -> x0, local copies, waits for them, and re-layouts: 1.37 us -> none  [the longest x1 0.69 us: per_device(): return refine(co, ff, sel, up_all, fine_weight, fine_bias[:, None])]
    gather x2 -> x0, local copies, waits for them, and re-layouts: 1.28 us -> none  [the longest x1 0.71 us: described(): there = links[:, columns.reshape(-1)].reshape(count, 8, 27)]
    pallas_call x5 -> x6, Pallas kernels: 20.4 us -> 21.6 us  [the longest x1 6.48 us: refine(): pl.pallas_call(lambda *refs: fine_kernel(chans, *refs), out_shape=jax.Sha...]
    unnamed x25 -> x36, local copies, waits for them, and re-layouts: 2.37 us -> 3.34 us
  transfers between devices with their start and end apart: 4 -> 16, of which waited for: 2 -> 6; matrix products, arithmetic and copies ran while one was open for 4% -> 0% of each run, Pallas kernels for 0% -> 18%
where the time goes in v1:
time: 71.9 us; the launch traced here: 71.6 us
  waiting for transfers between devices  27.2 us (38%)
  Pallas kernels  23.9 us (33%)
  starting transfers between devices  17 us (24%)
  local copies, waits for them, and re-layouts  3.35 us (5%)
    all_to_all x1, waiting for transfers between devices, per_device(): lax.all_to_all(sending, 'brick', split_axis=0, concat_axis=0, tiled=True)  13.3 us
    ppermute x12, waiting for transfers between devices, exchanged(): lax.ppermute(x, 'chan', [(i, i ^ s) for i in range(chans)])  12.7 us
    ppermute x12, starting transfers between devices, exchanged(): lax.ppermute(x, 'chan', [(i, i ^ s) for i in range(chans)])  7.93 us
    pallas_call x1, Pallas kernels, refine(): pl.pallas_call(lambda *refs: fine_kernel(chans, *refs), out_shape=jax.Sha...  6.48 us
    all_to_all x1, starting transfers between devices, per_device(): lax.all_to_all(sending, 'brick', split_axis=0, concat_axis=0, tiled=True)  5.94 us
    pallas_call x1, Pallas kernels, coarse(): pl.pallas_call(lambda *refs: coarse_kernel(chans, codes, *refs), out_shap...  5.45 us
    unnamed x36, local copies, waits for them, and re-layouts  3.34 us
    pallas_call x1, Pallas kernels, frames(): pl.pallas_call(lambda *refs: frame_kernel(chans, *refs), out_shape=[jax.S...  3.14 us
  transfers between devices with their start and end apart: 16, of which 6 were waited for; matrix products, arithmetic and copies ran while one was open for 0% of the time, Pallas kernels for 18%

profile of v1, /device:TPU:0, one launch (start us, length us, event | category | flops | bytes accessed | tf_op | source)
XLA Modules:
  0.0 71.6 jit_solution(6768683682440990736)
XLA Ops:
  0.0 2.3 %project.1 = (bf16[32,256]{1,0:T(8,128)(2,1)}, bf16[32,256]{1,0:T(8,128)(2,1)}, bf16[32,256]{1,0:T(8,128)(2,1)}, bf16[32,256]{1,0:T(8,128)(2,1)}) custom-call(s32[1]{0:T(128)} %bitcast.refs_0_, bf16[128,512]{1,0:T(8,128)(2,1)} %bitcast.8, bf16[512,512]{1,0:T(8,128)(2,1)} %constant.17.clone.refs_2_, bf16[8,32,128]{2,1,0:T(8,128)(2,1)} %bitcast.10), custom_call_target="tpu_custom_call" | custom-call | flops 16777216 | bytes 2097152 | tf_op jit(solution)/shard_map/project/pallas_call | solution.py:145
  2.3 0.5 collective-permute-start
  2.8 2.5 %collective-permute-start.1 = (bf16[32,256]{1,0:T(8,128)(2,1)}, bf16[32,256]{1,0:T(8,128)(2,1)S(1)}, u32[]{:S(2)}, u32[]{:S(2)}) collective-permute-start(bf16[32,256]{1,0:T(8,128)(2,1)} %get-tuple-element.22), channel_id=1, source_target_pairs={{0,2},{1,3},{2,0},{3,1},{4,6},{5,7},{6,4},{7,5},{8,10},{9,11},{10,... | collective-permute-start | bytes 49160 | tf_op jit(solution)/shard_map/ppermute | solution.py:689
  5.3 0.1 collective-permute-start.2
  5.4 2.0 %spread.1 = (bf16[128,384]{1,0:T(8,128)(2,1)}, bf16[192,512]{1,0:T(8,128)(2,1)}) custom-call(bf16[128,512]{1,0:T(8,128)(2,1)} %bitcast.9, bf16[256,128]{1,0:T(8,128)(2,1)} %bitcast.11, bf16[512,384]{1,0:T(8,128)(2,1)} %constant.18.clone.sel_ref), custom_call_target="tpu_custom_call" | custom-call | tf_op jit(solution)/shard_map/spread/pallas_call | solution.py:175
  7.4 0.0 collective-permute-done.refs_1_
  7.4 0.0 collective-permute-done.1.refs_2_
  7.4 1.2 %collective-permute-done.2.refs_3_ = bf16[32,256]{1,0:T(8,128)(2,1)S(1)} collective-permute-done((bf16[32,256]{1,0:T(8,128)(2,1)}, bf16[32,256]{1,0:T(8,128)(2,1)S(1)}, u32[]{:S(2)}, u32[]{:S(2)}) %collective-permute-start.2) | collective-permute-done | bytes 16416 | tf_op jit(solution)/shard_map/ppermute | solution.py:689
  8.7 0.6 copy-done.17
  9.3 2.1 %assemble.1 = bf16[8,240,256]{2,1,0:T(8,128)(2,1)} custom-call(s32[1]{0:T(128)} %bitcast.1.owner_ref.refs_1_, s32[2,26]{1,0:T(2,128)} %links_ref.1, s32[4]{0:T(128)} %parents_ref.1, s32[2,16,128]{2,1,0:T(8,128)} %constant.19.clone.table_ref, bf16[32,256]{1,0:T(8,128)(2,1)} %get-tuple-element.20.refs_0_, bf16[32,256]{1,0:T(8,128)(2,1)} %copy-done.15, ...), custom_call_target="tpu_custom_call" | custom-call | tf_op jit(solution)/shard_map/assemble/pallas_call | solution.py:229
  11.3 5.9 %all-to-all-start = ((bf16[8,240,256]{2,1,0:T(8,128)(2,1)}), bf16[8,240,256]{2,1,0:T(8,128)(2,1)S(1)}, u32[]{:S(2)}, u32[]{:S(2)}) async-start(bf16[8,240,256]{2,1,0:T(8,128)(2,1)} %assemble.1), calls=%async_computation | async-start | bytes 1966080 | tf_op jit(solution)/shard_map/all_to_all | solution.py:696
  17.3 0.2 collective-permute-start.5
  17.5 1.5 %collective-permute-start.4 = (bf16[192,512]{1,0:T(8,128)(2,1)S(1)}, bf16[192,512]{1,0:T(8,128)(2,1)S(1)}, u32[]{:S(2)}, u32[]{:S(2)}) collective-permute-start(bf16[192,512]{1,0:T(8,128)(2,1)S(1)} %copy-done.2), channel_id=1, source_target_pairs={{0,2},{1,3},{2,0},{3,1},{4,6},{5,7},{6,4},{7,5},{8,10},{9,11},{10,... | collective-permute-start | bytes 589832 | tf_op jit(solution)/shard_map/ppermute | solution.py:241
  18.9 0.3 collective-permute-start.3
  19.2 5.2 %collective-permute-done.5.refs_6_ = bf16[192,512]{1,0:T(8,128)(2,1)S(1)} collective-permute-done((bf16[192,512]{1,0:T(8,128)(2,1)S(1)}, bf16[192,512]{1,0:T(8,128)(2,1)S(1)}, u32[]{:S(2)}, u32[]{:S(2)}) %collective-permute-start.5) | collective-permute-done | bytes 196640 | tf_op jit(solution)/shard_map/ppermute | solution.py:241
  24.4 4.3 %collective-permute-done.4.refs_5_ = bf16[192,512]{1,0:T(8,128)(2,1)S(1)} collective-permute-done((bf16[192,512]{1,0:T(8,128)(2,1)S(1)}, bf16[192,512]{1,0:T(8,128)(2,1)S(1)}, u32[]{:S(2)}, u32[]{:S(2)}) %collective-permute-start.4) | collective-permute-done | bytes 196640 | tf_op jit(solution)/shard_map/ppermute | solution.py:241
  28.8 0.0 collective-permute-done.3.refs_4_
  28.8 13.3 %all-to-all-done.refs_5_.refs_1_ = bf16[8,240,256]{2,1,0:T(8,128)(2,1)S(1)} async-done(((bf16[8,240,256]{2,1,0:T(8,128)(2,1)}), bf16[8,240,256]{2,1,0:T(8,128)(2,1)S(1)}, u32[]{:S(2)}, u32[]{:S(2)}) %all-to-all-start) | async-done | bytes 983072 | tf_op jit(solution)/shard_map/all_to_all | solution.py:696
  42.1 0.0 copy-start.1
  42.1 0.1 collective-permute-start.8
  42.1 0.8 %collective-permute-start.7 = (bf16[8,32,256]{2,1,0:T(8,128)(2,1)S(1)}, bf16[8,32,256]{2,1,0:T(8,128)(2,1)S(1)}, u32[]{:S(2)}, u32[]{:S(2)}) collective-permute-start(bf16[8,32,256]{2,1,0:T(8,128)(2,1)S(1)} %slice.3.refs_1_), channel_id=1, source_target_pairs={{0,2},{1,3},{2,0},{3,1},{4,6},{5,7},{6,4},{7,5},{8,10},{9,11},{10,... | collective-permute-start | bytes 393224 | tf_op jit(solution)/shard_map/ppermute | solution.py:241
  42.9 1.1 %collective-permute-start.6 = (bf16[8,32,256]{2,1,0:T(8,128)(2,1)S(1)}, bf16[8,32,256]{2,1,0:T(8,128)(2,1)S(1)}, u32[]{:S(2)}, u32[]{:S(2)}) collective-permute-start(bf16[8,32,256]{2,1,0:T(8,128)(2,1)S(1)} %slice.3.refs_1_), channel_id=1, source_target_pairs={{0,1},{1,0},{2,3},{3,2},{4,5},{5,4},{6,7},{7,6},{8,9},{9,8},{10,11... | collective-permute-start | bytes 393224 | tf_op jit(solution)/shard_map/ppermute | solution.py:241
  44.0 2.5 %halo.1.refs_7_ = bf16[4,32,512]{2,1,0:T(8,128)(2,1)} custom-call(s32[4,26]{1,0:T(4,128)} %refs_2_.2, bf16[8,240,256]{2,1,0:T(8,128)(2,1)} %copy-done), custom_call_target="tpu_custom_call" | custom-call | tf_op jit(solution)/shard_map/halo/pallas_call | solution.py:276
  46.5 0.4 collective-permute-start.14
  46.8 1.3 %collective-permute-start.13 = (bf16[4,32,512]{2,1,0:T(8,128)(2,1)}, bf16[4,32,512]{2,1,0:T(8,128)(2,1)S(1)}, u32[]{:S(2)}, u32[]{:S(2)}) collective-permute-start(bf16[4,32,512]{2,1,0:T(8,128)(2,1)} %halo.1.refs_7_), channel_id=1, source_target_pairs={{0,2},{1,3},{2,0},{3,1},{4,6},{5,7},{6,4},{7,5},{8,10},{9,11},{10,... | collective-permute-start | bytes 393224 | tf_op jit(solution)/shard_map/ppermute | solution.py:241
  48.1 0.0 collective-permute-done.8.refs_4_
  48.1 0.2 collective-permute-start.12
  48.3 1.1 %collective-permute-done.7.refs_3_ = bf16[8,32,256]{2,1,0:T(8,128)(2,1)S(1)} collective-permute-done((bf16[8,32,256]{2,1,0:T(8,128)(2,1)S(1)}, bf16[8,32,256]{2,1,0:T(8,128)(2,1)S(1)}, u32[]{:S(2)}, u32[]{:S(2)}) %collective-permute-start.7) | collective-permute-done | bytes 131104 | tf_op jit(solution)/shard_map/ppermute | solution.py:241
  49.4 0.0 collective-permute-done.6.refs_2_
  49.4 0.6 copy-done.13
  50.1 0.0 copy-done.14
  50.1 5.4 %coarse.1.refs_1_ = bf16[1,32,2048]{2,1,0:T(8,128)(2,1)} custom-call(s32[1]{0:T(128)} %bitcast.refs_0_, bf16[8,32,256]{2,1,0:T(8,128)(2,1)} %copy-done.1, bf16[8,32,256]{2,1,0:T(8,128)(2,1)} %copy-done.14, bf16[8,32,256]{2,1,0:T(8,128)(2,1)} %copy-done.13, bf16[8,32,256]{2,1,0:T(8,128)(2,1)} %copy-done.12, bf16[8,240,256]{2,1,0:T(8,128)(2,1)} %copy-done, ...), custom_call_target="tpu_custom_call" | custom-call | flops 452984832 | bytes 2097152 | tf_op jit(solution)/shard_map/coarse/pallas_call | solution.py:396
  55.6 1.6 %collective-permute-start.11 = (bf16[1,32,2048]{2,1,0:T(8,128)(2,1)}, bf16[1,32,2048]{2,1,0:T(8,128)(2,1)S(1)}, u32[]{:S(2)}, u32[]{:S(2)}) collective-permute-start(bf16[1,32,2048]{2,1,0:T(8,128)(2,1)} %coarse.1.refs_1_), channel_id=1, source_target_pairs={{0,3},{1,2},{2,1},{3,0},{4,7},{5,6},{6,5},{7,4},{8,11},{9,10},{10,... | collective-permute-start | bytes 393224 | tf_op jit(solution)/shard_map/ppermute | solution.py:241
  57.2 0.6 collective-permute-start.10
  57.8 0.0 collective-permute-done.14.refs_10_
  57.8 0.0 collective-permute-start.9
  57.8 0.0 collective-permute-done.13.refs_9_
  57.8 0.0 collective-permute-done.12.refs_8_
  57.8 0.6 copy-done.6
  58.4 0.1 copy-done.7
  58.5 0.7 copy-done.8
  59.2 3.1 %frames.1 = (bf16[100,48,128]{2,1,0:T(8,128)(2,1)}, bf16[1,9,48,128]{3,2,1,0:T(8,128)(2,1)}, bf16[8,128,128]{2,1,0:T(8,128)(2,1)}) custom-call(s32[1]{0:T(128)} %bitcast.refs_0_, s32[1]{0:T(128)} %bitcast.1.owner_ref.refs_1_, s32[4,26]{1,0:T(4,128)} %refs_2_.2, bf16[192,512]{1,0:T(8,128)(2,1)} %get-tuple-element.28.refs_3_, bf16[192,512]{1,0:T(8,128)(2,1)} %copy-done.5, ...), custom_call_target="tpu_custom_call" | custom-call | tf_op jit(solution)/shard_map/frames/pallas_call | solution.py:519
  62.3 0.0 collective-permute-done.11.refs_4_
  62.3 2.1 %collective-permute-done.10.refs_3_ = bf16[1,32,2048]{2,1,0:T(8,128)(2,1)S(1)} collective-permute-done((bf16[1,32,2048]{2,1,0:T(8,128)(2,1)}, bf16[1,32,2048]{2,1,0:T(8,128)(2,1)S(1)}, u32[]{:S(2)}, u32[]{:S(2)}) %collective-permute-start.10) | collective-permute-done | bytes 131104 | tf_op jit(solution)/shard_map/ppermute | solution.py:241
  64.4 0.0 collective-permute-done.9.refs_2_
  64.4 0.6 copy-done.10
  65.0 0.1 copy-done.11
  65.1 6.5 %refine.1 = bf16[4,32,512]{2,1,0:T(8,128)(2,1)} custom-call(s32[1]{0:T(128)} %bitcast.refs_0_, bf16[1,32,2048]{2,1,0:T(8,128)(2,1)} %coarse.1.refs_1_, bf16[1,32,2048]{2,1,0:T(8,128)(2,1)} %copy-done.11, bf16[1,32,2048]{2,1,0:T(8,128)(2,1)} %copy-done.10, bf16[1,32,2048]{2,1,0:T(8,128)(2,1)} %copy-done.9, bf16[100,48,128]{2,1,0:T(8,128)(2,1)} %get-tuple-element.32.refs_5_, ...), custom_call_target="tpu_custom_call" | custom-call | flops 452984832 | bytes 4194304 | tf_op jit(solution)/shard_map/refine/pallas_call | solution.py:637
  (28 shorter events, 0.1 us)
Async XLA Ops:
  2.3 5.1 %collective-permute-start = (bf16[32,256]{1,0:T(8,128)(2,1)}, bf16[32,256]{1,0:T(8,128)(2,1)S(1)}, u32[]{:S(2)}, u32[]{:S(2)}) collective-permute-start(bf16[32,256]{1,0:T(8,128)(2,1)} %get-tuple-element.21), channel_id=1, source_target_pairs={{0,1},{1,0},{2,3},{3,2},{4,5},{5,4},{6,7},{7,6},{8,9},{9,8},{10,11... | collective-permute-start | bytes 49160 | tf_op jit(solution)/shard_map/ppermute | solution.py:689
  2.8 4.6 %collective-permute-start.1 = (bf16[32,256]{1,0:T(8,128)(2,1)}, bf16[32,256]{1,0:T(8,128)(2,1)S(1)}, u32[]{:S(2)}, u32[]{:S(2)}) collective-permute-start(bf16[32,256]{1,0:T(8,128)(2,1)} %get-tuple-element.22), channel_id=1, source_target_pairs={{0,2},{1,3},{2,0},{3,1},{4,6},{5,7},{6,4},{7,5},{8,10},{9,11},{10,... | collective-permute-start | bytes 49160 | tf_op jit(solution)/shard_map/ppermute | solution.py:689
  5.3 3.4 %collective-permute-start.2 = (bf16[32,256]{1,0:T(8,128)(2,1)}, bf16[32,256]{1,0:T(8,128)(2,1)S(1)}, u32[]{:S(2)}, u32[]{:S(2)}) collective-permute-start(bf16[32,256]{1,0:T(8,128)(2,1)} %get-tuple-element.23), channel_id=1, source_target_pairs={{0,3},{1,2},{2,1},{3,0},{4,7},{5,6},{6,5},{7,4},{8,11},{9,10},{10,... | collective-permute-start | bytes 49160 | tf_op jit(solution)/shard_map/ppermute | solution.py:689
  7.4 1.3 %copy-start.15 = (bf16[32,256]{1,0:T(8,128)(2,1)}, bf16[32,256]{1,0:T(8,128)(2,1)S(1)}, u32[]{:S(2)}) copy-start(bf16[32,256]{1,0:T(8,128)(2,1)S(1)} %collective-permute-done.refs_1_) | copy-start | bytes 49156
  7.4 1.3 %copy-start.16 = (bf16[32,256]{1,0:T(8,128)(2,1)}, bf16[32,256]{1,0:T(8,128)(2,1)S(1)}, u32[]{:S(2)}) copy-start(bf16[32,256]{1,0:T(8,128)(2,1)S(1)} %collective-permute-done.1.refs_2_) | copy-start | bytes 49156
  8.7 0.6 copy-start.17
  11.3 5.9 %copy-start.2 = (bf16[192,512]{1,0:T(8,128)(2,1)S(1)}, bf16[192,512]{1,0:T(8,128)(2,1)}, u32[]{:S(2)}) copy-start(bf16[192,512]{1,0:T(8,128)(2,1)} %get-tuple-element.28.refs_3_) | copy-start | bytes 589828
  11.3 30.7 %all-to-all-start = ((bf16[8,240,256]{2,1,0:T(8,128)(2,1)}), bf16[8,240,256]{2,1,0:T(8,128)(2,1)S(1)}, u32[]{:S(2)}, u32[]{:S(2)}) async-start(bf16[8,240,256]{2,1,0:T(8,128)(2,1)} %assemble.1), calls=%async_computation | async-start | bytes 1966080 | tf_op jit(solution)/shard_map/all_to_all | solution.py:696
  17.3 7.1 %collective-permute-start.5 = (bf16[192,512]{1,0:T(8,128)(2,1)S(1)}, bf16[192,512]{1,0:T(8,128)(2,1)S(1)}, u32[]{:S(2)}, u32[]{:S(2)}) collective-permute-start(bf16[192,512]{1,0:T(8,128)(2,1)S(1)} %copy-done.2), channel_id=1, source_target_pairs={{0,3},{1,2},{2,1},{3,0},{4,7},{5,6},{6,5},{7,4},{8,11},{9,10},{10,... | collective-permute-start | bytes 589832 | tf_op jit(solution)/shard_map/ppermute | solution.py:241
  17.5 11.3 %collective-permute-start.4 = (bf16[192,512]{1,0:T(8,128)(2,1)S(1)}, bf16[192,512]{1,0:T(8,128)(2,1)S(1)}, u32[]{:S(2)}, u32[]{:S(2)}) collective-permute-start(bf16[192,512]{1,0:T(8,128)(2,1)S(1)} %copy-done.2), channel_id=1, source_target_pairs={{0,2},{1,3},{2,0},{3,1},{4,6},{5,7},{6,4},{7,5},{8,10},{9,11},{10,... | collective-permute-start | bytes 589832 | tf_op jit(solution)/shard_map/ppermute | solution.py:241
  18.9 9.8 %collective-permute-start.3 = (bf16[192,512]{1,0:T(8,128)(2,1)S(1)}, bf16[192,512]{1,0:T(8,128)(2,1)S(1)}, u32[]{:S(2)}, u32[]{:S(2)}) collective-permute-start(bf16[192,512]{1,0:T(8,128)(2,1)S(1)} %copy-done.2), channel_id=1, source_target_pairs={{0,1},{1,0},{2,3},{3,2},{4,5},{5,4},{6,7},{7,6},{8,9},{9,8},{10,11... | collective-permute-start | bytes 589832 | tf_op jit(solution)/shard_map/ppermute | solution.py:241
  24.4 31.1 %copy-start.3 = (bf16[192,512]{1,0:T(8,128)(2,1)}, bf16[192,512]{1,0:T(8,128)(2,1)S(1)}, u32[]{:S(2)}) copy-start(bf16[192,512]{1,0:T(8,128)(2,1)S(1)} %collective-permute-done.5.refs_6_) | copy-start | bytes 589828
  28.8 29.1 %copy-start.4 = (bf16[192,512]{1,0:T(8,128)(2,1)}, bf16[192,512]{1,0:T(8,128)(2,1)S(1)}, u32[]{:S(2)}) copy-start(bf16[192,512]{1,0:T(8,128)(2,1)S(1)} %collective-permute-done.4.refs_5_) | copy-start | bytes 589828
  28.8 29.1 %copy-start.5 = (bf16[192,512]{1,0:T(8,128)(2,1)}, bf16[192,512]{1,0:T(8,128)(2,1)S(1)}, u32[]{:S(2)}) copy-start(bf16[192,512]{1,0:T(8,128)(2,1)S(1)} %collective-permute-done.3.refs_4_) | copy-start | bytes 589828
  42.0 2.0 %copy-start = (bf16[8,240,256]{2,1,0:T(8,128)(2,1)}, bf16[8,240,256]{2,1,0:T(8,128)(2,1)S(1)}, u32[]{:S(2)}) copy-start(bf16[8,240,256]{2,1,0:T(8,128)(2,1)S(1)} %all-to-all-done.refs_5_.refs_1_) | copy-start | bytes 2949124
  42.1 7.4 %copy-start.1 = (bf16[8,32,256]{2,1,0:T(8,128)(2,1)}, bf16[8,32,256]{2,1,0:T(8,128)(2,1)S(1)}, u32[]{:S(2)}) copy-start(bf16[8,32,256]{2,1,0:T(8,128)(2,1)S(1)} %slice.3.refs_1_) | copy-start | bytes 393220
  42.1 6.0 %collective-permute-start.8 = (bf16[8,32,256]{2,1,0:T(8,128)(2,1)S(1)}, bf16[8,32,256]{2,1,0:T(8,128)(2,1)S(1)}, u32[]{:S(2)}, u32[]{:S(2)}) collective-permute-start(bf16[8,32,256]{2,1,0:T(8,128)(2,1)S(1)} %slice.3.refs_1_), channel_id=1, source_target_pairs={{0,3},{1,2},{2,1},{3,0},{4,7},{5,6},{6,5},{7,4},{8,11},{9,10},{10,... | collective-permute-start | bytes 393224 | tf_op jit(solution)/shard_map/ppermute | solution.py:241
  42.1 7.3 %collective-permute-start.7 = (bf16[8,32,256]{2,1,0:T(8,128)(2,1)S(1)}, bf16[8,32,256]{2,1,0:T(8,128)(2,1)S(1)}, u32[]{:S(2)}, u32[]{:S(2)}) collective-permute-start(bf16[8,32,256]{2,1,0:T(8,128)(2,1)S(1)} %slice.3.refs_1_), channel_id=1, source_target_pairs={{0,2},{1,3},{2,0},{3,1},{4,6},{5,7},{6,4},{7,5},{8,10},{9,11},{10,... | collective-permute-start | bytes 393224 | tf_op jit(solution)/shard_map/ppermute | solution.py:241
  42.9 6.5 %collective-permute-start.6 = (bf16[8,32,256]{2,1,0:T(8,128)(2,1)S(1)}, bf16[8,32,256]{2,1,0:T(8,128)(2,1)S(1)}, u32[]{:S(2)}, u32[]{:S(2)}) collective-permute-start(bf16[8,32,256]{2,1,0:T(8,128)(2,1)S(1)} %slice.3.refs_1_), channel_id=1, source_target_pairs={{0,1},{1,0},{2,3},{3,2},{4,5},{5,4},{6,7},{7,6},{8,9},{9,8},{10,11... | collective-permute-start | bytes 393224 | tf_op jit(solution)/shard_map/ppermute | solution.py:241
  46.5 11.3 %collective-permute-start.14 = (bf16[4,32,512]{2,1,0:T(8,128)(2,1)}, bf16[4,32,512]{2,1,0:T(8,128)(2,1)S(1)}, u32[]{:S(2)}, u32[]{:S(2)}) collective-permute-start(bf16[4,32,512]{2,1,0:T(8,128)(2,1)} %halo.1.refs_7_), channel_id=1, source_target_pairs={{0,3},{1,2},{2,1},{3,0},{4,7},{5,6},{6,5},{7,4},{8,11},{9,10},{10,... | collective-permute-start | bytes 393224 | tf_op jit(solution)/shard_map/ppermute | solution.py:241
  46.8 11.0 %collective-permute-start.13 = (bf16[4,32,512]{2,1,0:T(8,128)(2,1)}, bf16[4,32,512]{2,1,0:T(8,128)(2,1)S(1)}, u32[]{:S(2)}, u32[]{:S(2)}) collective-permute-start(bf16[4,32,512]{2,1,0:T(8,128)(2,1)} %halo.1.refs_7_), channel_id=1, source_target_pairs={{0,2},{1,3},{2,0},{3,1},{4,6},{5,7},{6,4},{7,5},{8,10},{9,11},{10,... | collective-permute-start | bytes 393224 | tf_op jit(solution)/shard_map/ppermute | solution.py:241
  48.1 1.3 %copy-start.12 = (bf16[8,32,256]{2,1,0:T(8,128)(2,1)}, bf16[8,32,256]{2,1,0:T(8,128)(2,1)S(1)}, u32[]{:S(2)}) copy-start(bf16[8,32,256]{2,1,0:T(8,128)(2,1)S(1)} %collective-permute-done.8.refs_4_) | copy-start | bytes 393220
  48.1 9.7 %collective-permute-start.12 = (bf16[4,32,512]{2,1,0:T(8,128)(2,1)}, bf16[4,32,512]{2,1,0:T(8,128)(2,1)S(1)}, u32[]{:S(2)}, u32[]{:S(2)}) collective-permute-start(bf16[4,32,512]{2,1,0:T(8,128)(2,1)} %halo.1.refs_7_), channel_id=1, source_target_pairs={{0,1},{1,0},{2,3},{3,2},{4,5},{5,4},{6,7},{7,6},{8,9},{9,8},{10,11... | collective-permute-start | bytes 393224 | tf_op jit(solution)/shard_map/ppermute | solution.py:241
  49.4 0.7 copy-start.13
  49.4 0.7 copy-start.14
  55.6 6.7 %collective-permute-start.11 = (bf16[1,32,2048]{2,1,0:T(8,128)(2,1)}, bf16[1,32,2048]{2,1,0:T(8,128)(2,1)S(1)}, u32[]{:S(2)}, u32[]{:S(2)}) collective-permute-start(bf16[1,32,2048]{2,1,0:T(8,128)(2,1)} %coarse.1.refs_1_), channel_id=1, source_target_pairs={{0,3},{1,2},{2,1},{3,0},{4,7},{5,6},{6,5},{7,4},{8,11},{9,10},{10,... | collective-permute-start | bytes 393224 | tf_op jit(solution)/shard_map/ppermute | solution.py:241
  57.2 7.2 %collective-permute-start.10 = (bf16[1,32,2048]{2,1,0:T(8,128)(2,1)}, bf16[1,32,2048]{2,1,0:T(8,128)(2,1)S(1)}, u32[]{:S(2)}, u32[]{:S(2)}) collective-permute-start(bf16[1,32,2048]{2,1,0:T(8,128)(2,1)} %coarse.1.refs_1_), channel_id=1, source_target_pairs={{0,2},{1,3},{2,0},{3,1},{4,6},{5,7},{6,4},{7,5},{8,10},{9,11},{10,... | collective-permute-start | bytes 393224 | tf_op jit(solution)/shard_map/ppermute | solution.py:241
  57.8 0.6 copy-start.6
  57.8 6.6 %collective-permute-start.9 = (bf16[1,32,2048]{2,1,0:T(8,128)(2,1)}, bf16[1,32,2048]{2,1,0:T(8,128)(2,1)S(1)}, u32[]{:S(2)}, u32[]{:S(2)}) collective-permute-start(bf16[1,32,2048]{2,1,0:T(8,128)(2,1)} %coarse.1.refs_1_), channel_id=1, source_target_pairs={{0,1},{1,0},{2,3},{3,2},{4,5},{5,4},{6,7},{7,6},{8,9},{9,8},{10,11... | collective-permute-start | bytes 393224 | tf_op jit(solution)/shard_map/ppermute | solution.py:241
  57.8 0.7 copy-start.7
  58.5 0.7 copy-start.8
  62.3 2.1 %copy-start.9 = (bf16[1,32,2048]{2,1,0:T(8,128)(2,1)}, bf16[1,32,2048]{2,1,0:T(8,128)(2,1)S(1)}, u32[]{:S(2)}) copy-start(bf16[1,32,2048]{2,1,0:T(8,128)(2,1)S(1)} %collective-permute-done.11.refs_4_) | copy-start | bytes 393220
  64.4 0.7 copy-start.10
  64.4 0.7 %copy-start.11 = (bf16[1,32,2048]{2,1,0:T(8,128)(2,1)}, bf16[1,32,2048]{2,1,0:T(8,128)(2,1)S(1)}, u32[]{:S(2)}) copy-start(bf16[1,32,2048]{2,1,0:T(8,128)(2,1)S(1)} %collective-permute-done.9.refs_2_) | copy-start | bytes 393220

commit v2 on v1

--- a/solution.py
+++ b/solution.py
@@ -56,19 +56,6 @@
 STARTS, VOXELS = piece_lanes()
 for k in (2, 3):
     VOXELS[k] = [VOXELS[k][x * EDGE + z] for z in range(EDGE) for x in range(EDGE)]
-SENT = [v for k in range(6) for v in VOXELS[k]]
-SOURCES = []
-for k, heading in enumerate(HEADINGS):
-    for f in range(6):
-        run = VOXELS[f]
-        want = VOXELS[k]
-        first = run.index(want[0]) if want[0] in run else -1
-        if first >= 0 and run[first : first + len(want)] == want:
-            SOURCES.append(EDGE**2 * f + first)
-            break
-assert len(SOURCES) == len(HEADINGS)
-
-
 def octant_selector():
     sel = np.zeros((EDGE**3, EDGE**3), np.float32)
     for x in range(EDGE):
@@ -80,11 +67,34 @@
     return sel
 
 
+FACE = EDGE**2
+FACES = 6
+RIMS = len(HEADINGS) - FACES
+
+
 def outer_selector():
-    sel = np.zeros((EDGE**3, len(SENT)), np.float32)
-    for i, v in enumerate(SENT):
-        sel[v, i] = 1
+    sel = np.zeros((EDGE**3, FACES * FACE + -(-RIMS * EDGE // 128) * 128), np.float32)
+    for k in range(len(HEADINGS)):
+        first = k * FACE if k < FACES else FACES * FACE + (k - FACES) * EDGE
+        for i, v in enumerate(VOXELS[k]):
+            sel[v, first + i] = 1
     return sel
+
+
+def entry_tables(fine):
+    wide = 128 // fine
+    lanes = np.zeros((2, 128), np.int32)
+    for b in range(fine):
+        for k in range(len(HEADINGS)):
+            face = k < FACES
+            lanes[:, b * wide + k] = k * 128 if face else FACES * 128 + (k - FACES) * EDGE, face
+    kind = lanes[1]
+    earlier = (np.arange(128)[:, None] < np.arange(128)[None]) & (kind[:, None] == kind[None])
+    return lanes, earlier.astype(np.float32)
+
+
+def capacities(fine, owners):
+    return -(-fine * FACES // owners), -(-fine * RIMS // owners)
 
 
 def pair_selector():
@@ -117,11 +127,13 @@
 SM = pltpu.SMEM
 
 
-def project_kernel(chans, me_ref, f_ref, oct_ref, w_ref, *rest):
-    outs, part = rest[:chans], rest[chans]
+def project_kernel(chans, me_ref, f_ref, sel_ref, w_ref, up_ref, *rest):
+    outs, (chunk_ref, pack_ref, part) = rest[:chans], rest[chans:]
     q = w_ref.shape[1]
-    fine = f_ref.shape[0] // q
-    picked = dot(f_ref[...], oct_ref[...]).astype(BF16)
+    rows, vox = f_ref.shape
+    fine = rows // q
+    x = f_ref[...]
+    picked = dot(x, sel_ref[:, :vox]).astype(BF16)
     acc = None
     for o in range(8):
         z = jnp.concatenate(
@@ -136,57 +148,124 @@
     me = me_ref[0]
     for s in range(chans):
         outs[s][...] = part[pl.ds(pl.multiple_of((me ^ s) * q, q), q), :].astype(BF16)
-
-
-def project(me, features, down_weight, chans):
+    got = dot(x, sel_ref[:, vox:])
+    low = lax.broadcasted_iota(jnp.int32, (rows, 128), 1) < FACE
+    for i in range(FACES // 2):
+        pair = got[:, 128 * i : 128 * i + 128]
+        turned = pltpu.roll(pair, FACE, 1)
+        chunk_ref[2 * i] = jnp.where(low, pair, turned).astype(BF16)
+        chunk_ref[2 * i + 1] = jnp.where(low, turned, pair).astype(BF16)
+    for i in range(FACES, chunk_ref.shape[0]):
+        at = 128 * (i - FACES // 2)
+        chunk_ref[i] = got[:, at : at + 128].astype(BF16)
+    pack_ref[0:rows] = x
+    more = up_ref.shape[0] * up_ref.shape[1] // vox
+    for i in range(vox // up_ref.shape[1]):
+        part_lanes = slice(i * up_ref.shape[1], (i + 1) * up_ref.shape[1])
+        pack_ref[rows : rows + more, part_lanes] = up_ref[i * more : (i + 1) * more]
+
+
+def project(me, features, down_weight, up_weight, chans):
     fine, q, vox = features.shape
     c_out = down_weight.shape[1]
     lanes = fine * CUBE
-    return pl.pallas_call(
+    ups = up_weight.reshape(-1, up_weight.shape[2])
+    sel = np.concatenate([octant_selector(), outer_selector()], axis=1)
+    chunks = (sel.shape[1] - vox) // 128 + FACES // 2
+    res = pl.pallas_call(
         lambda *refs: project_kernel(chans, *refs),
-        out_shape=[jax.ShapeDtypeStruct((q, lanes), BF16)] * chans,
-        in_specs=[pl.BlockSpec(memory_space=SM)] + [pl.BlockSpec(memory_space=VM)] * 3,
-        out_specs=[pl.BlockSpec(memory_space=VM)] * chans,
+        out_shape=[jax.ShapeDtypeStruct((q, lanes), BF16)] * chans
+        + [
+            jax.ShapeDtypeStruct((chunks, fine * q, 128), BF16),
+            jax.ShapeDtypeStruct((fine * q + ups.size // vox, vox), BF16),
+        ],
+        in_specs=[pl.BlockSpec(memory_space=SM)] + [pl.BlockSpec(memory_space=VM)] * 4,
+        out_specs=[pl.BlockSpec(memory_space=VM)] * (chans + 2),
         scratch_shapes=[pltpu.VMEM((c_out, lanes), F32)],
         compiler_params=params(),
-        cost_estimate=cost(2 * c_out * 8 * q * lanes, 2 * 1024 * 1024),
         name="project",
     )(
         me,
         features.reshape(fine * q, vox),
-        jnp.asarray(octant_selector(), BF16),
+        jnp.asarray(sel, BF16),
         jnp.transpose(down_weight, (0, 2, 1)),
+        ups,
     )
-
-
-def spread_kernel(f_ref, up_ref, sel_ref, out_ref, pack_ref):
-    rows, vox = f_ref.shape
-    out_ref[...] = dot(f_ref[...], sel_ref[...]).astype(BF16)
-    pack_ref[0:rows] = f_ref[...]
-    more = up_ref.shape[0] * up_ref.shape[1] // vox
-    for i in range(vox // up_ref.shape[1]):
-        part = slice(i * up_ref.shape[1], (i + 1) * up_ref.shape[1])
-        pack_ref[rows : rows + more, part] = up_ref[i * more : (i + 1) * more]
-
-
-def spread_out(features, up_weight):
-    fine, q, vox = features.shape
-    ups = up_weight.reshape(-1, up_weight.shape[2])
-    return pl.pallas_call(
-        spread_kernel,
-        out_shape=[
-            jax.ShapeDtypeStruct((fine * q, len(SENT)), BF16),
-            jax.ShapeDtypeStruct((fine * q + ups.size // vox, vox), BF16),
+    return res[:chans], res[chans], res[chans + 1]
+
+
+def choose(
+    fine, q, faces, rims, base, owner_ref, asked_refs, own_ref, lanes_ref, earlier_ref, chunk_ref,
+    out_ref, from_ref, table, scalars, sem,
+):
+    owners = out_ref.shape[0]
+    place = lanes_ref[0:1, :]
+    is_face = lanes_ref[1:2, :] == 1
+    wide = 128 // fine
+    asked = jnp.concatenate(
+        [
+            jnp.concatenate([ref[:, b, :][:, :wide] for ref in asked_refs], axis=0)
+            for b in range(fine)
         ],
-        in_specs=[pl.BlockSpec(memory_space=VM)] * 3,
-        out_specs=[pl.BlockSpec(memory_space=VM)] * 2,
-        compiler_params=params(),
-        name="spread",
-    )(features.reshape(fine * q, vox), ups, jnp.asarray(outer_selector(), BF16))
-
-
-def assemble_kernel(owner_ref, links_ref, parents_ref, table_ref, *refs):
-    slots, outer_ref, out_ref = refs[:-2], refs[-2], refs[-1]
+        axis=1,
+    )
+    mask = (asked >= 0) & (lax.div(jnp.maximum(asked, 0), fine) == owner_ref[0])
+    rank = dot(mask.astype(F32).astype(BF16), earlier_ref[...])
+    slot = jnp.where(is_face, rank, rank + faces)
+    code = (lax.rem(jnp.maximum(asked, 0), fine) * 1024 + place + 1).astype(F32)
+    lane = lax.broadcasted_iota(jnp.int32, (owners, 128), 1)
+    found = jnp.zeros((owners, 128), F32)
+    for r in range(faces + rims):
+        value = jnp.sum(jnp.where(mask & (slot == r), code, 0.0), axis=1, keepdims=True)
+        found = jnp.where(lane == r, value, found)
+    table[...] = found.astype(jnp.int32) - 1
+    copy = pltpu.make_async_copy(table, scalars, sem)
+    copy.start()
+    own = jnp.concatenate([own_ref[b : b + 1, :wide] for b in range(fine)], axis=1)
+    own = jnp.broadcast_to(own, (owners, 128))
+    theirs = lax.div(jnp.maximum(own, 0), fine)
+    mask = (own >= 0) & (theirs == lax.broadcasted_iota(jnp.int32, (owners, 128), 0))
+    rank = dot(mask.astype(F32).astype(BF16), earlier_ref[...])
+    at = jnp.where(is_face, rank * FACE, rank * EDGE + faces * FACE) + theirs.astype(F32) * 1024.0 + 1.0
+    from_ref[...] = jnp.sum(jnp.where(mask, at, 0.0), axis=0, keepdims=True).astype(jnp.int32) - 1
+    copy.wait()
+    side = lax.broadcasted_iota(jnp.int32, (q, 128), 1)
+    half = q // 2
+
+    def one(r_owner, _):
+        w = owner_ref[0] ^ r_owner
+        for block in range((out_ref.shape[1] - base) // half):
+            here = jnp.zeros((q, 128), F32)
+            for r in range(faces + rims):
+                pos = r * FACE if r < faces else faces * FACE + (r - faces) * EDGE
+                if pos // 128 != block:
+                    continue
+                v = scalars[r_owner, r]
+                safe = jnp.maximum(v, 0)
+                b = lax.shift_right_logical(safe, 10)
+                chunk = lax.shift_right_logical(safe, 7) & 7
+                got = chunk_ref[chunk, pl.ds(pl.multiple_of(b * q, q), q), :].astype(F32)
+                first = pos % 128
+                size = FACE
+                if r >= faces:
+                    got = pltpu.roll(got, (first + 128 - (safe & 127)) & 127, 1)
+                    size = EDGE
+                here = jnp.where((side >= first) & (side < first + size) & (v >= 0), got, here)
+            here = here.astype(BF16)
+            for i in range(2):
+                out_ref[w, base + block * half : base + (block + 1) * half, 128 * i : 128 * i + 128] = here[i * half : (i + 1) * half]
+        return 0
+
+    if owners <= 8:
+        for w in range(owners):
+            one(w, 0)
+    else:
+        lax.fori_loop(0, owners, one, 0)
+
+
+def assemble_kernel(chans, asks, fine, faces, rims, owner_ref, links_ref, parents_ref, table_ref, *refs):
+    slots, asked_refs, refs = refs[:chans], refs[chans : chans + asks], refs[chans + asks :]
+    out_ref = refs[4]
     count, ways = links_ref.shape
     total = slots[0][...].astype(F32)
     for s in slots[1:]:
@@ -211,39 +290,78 @@
         out_ref[w, 0:q, :] = total
         for i in range(2):
             out_ref[w, q : q + rows, 128 * i : 128 * i + 128] = digits[i]
-        at, n = q + rows, outer_ref.shape[0]
-        out_ref[w, at : at + n, :] = outer_ref[:, 0:256]
-        for i in range(2):
-            out_ref[w, at + n : at + n + n // 2, 128 * i : 128 * i + 128] = outer_ref[
-                i * n // 2 : (i + 1) * n // 2, 256:384
-            ]
-
-
-def assemble(slots, outer, owner, coarse_links, parents, owners):
+    choose(fine, q, faces, rims, q + rows, owner_ref, asked_refs, *refs)
+
+
+def assemble(slots, owner, coarse_links, parents, asked, own, chunks, owners):
     q, lanes = slots[0].shape
     count = coarse_links.shape[0]
+    fine = parents.shape[0]
     columns, octants = octant_table()
     table = np.full((2, count * 8, 128), -1, np.int32)
     table[0, :, :27] = np.tile(columns, (count, 1))
     table[1, :, :27] = np.tile(octants, (count, 1))
+    faces, rims = capacities(fine, owners)
+    blocks = -(-(faces * FACE + rims * EDGE) // 128)
+    entries, earlier = entry_tables(fine)
     return pl.pallas_call(
-        assemble_kernel,
-        out_shape=jax.ShapeDtypeStruct((owners, q + count * 8 + outer.size // lanes, lanes), BF16),
-        in_specs=[pl.BlockSpec(memory_space=SM)] * 3 + [pl.BlockSpec(memory_space=VM)] * (len(slots) + 2),
-        out_specs=pl.BlockSpec(memory_space=VM),
+        lambda *refs: assemble_kernel(len(slots), len(asked), fine, faces, rims, *refs),
+        out_shape=[
+            jax.ShapeDtypeStruct((owners, q + count * 8 + blocks * q // 2, lanes), BF16),
+            jax.ShapeDtypeStruct((1, 128), jnp.int32),
+        ],
+        in_specs=[pl.BlockSpec(memory_space=SM)] * 3 + [pl.BlockSpec(memory_space=VM)] * (len(slots) + len(asked) + 5),
+        out_specs=[pl.BlockSpec(memory_space=VM)] * 2,
+        scratch_shapes=[
+            pltpu.VMEM((owners, 128), jnp.int32),
+            pltpu.SMEM((owners, 128), jnp.int32),
+            pltpu.SemaphoreType.DMA,
+        ],
         compiler_params=params(),
+        cost_estimate=cost(1024 * 1024, 12 * 1024 * 1024),
         name="assemble",
-    )(owner, coarse_links, parents, jnp.asarray(table), *slots, outer)
+    )(
+        owner, coarse_links, parents, jnp.asarray(table), *slots,
+        *asked, own, jnp.asarray(entries), jnp.asarray(earlier, BF16), chunks,
+    )
+
+
+def partner(x, axis, step, count):
+    return lax.ppermute(x, axis, [(i, i ^ step) for i in range(count)])
 
 
 def exchanged(x, chans):
-    return [x] + [
-        lax.ppermute(x, "chan", [(i, i ^ s) for i in range(chans)]) for s in range(1, chans)
-    ]
-
-
-def halo_kernel(q, base, links_ref, recv_ref, out_ref):
+    return [x] + [partner(x, "chan", s, chans) for s in range(1, chans)]
+
+
+def relayed(x, chans, meanwhile=lambda: None):
+    slots, step, other = {0: x}, chans // 2, None
+    while step:
+        if step == 1:
+            other = meanwhile()
+            if other is not None:
+                slots, other = lax.optimization_barrier((slots, other))
+        for s in list(slots):
+            slots[s | step] = partner(slots[s], "chan", step, chans)
+        step //= 2
+    return [slots[s] for s in range(chans)], other
+
+
+def gathered(x, owners, between):
+    have, step, count = [x], 1, 0
+    while step < owners:
+        now = jnp.concatenate(have, axis=0) if len(have) > 1 else have[0]
+        if count < len(between):
+            now = between[count](now)
+        have = [now, partner(now, "brick", step, owners)]
+        step *= 2
+        count += 1
+    return have
+
+
+def halo_kernel(q, base, from_ref, recv_ref, out_ref):
     fine = out_ref.shape[0]
+    half = q // 2
     lane = lax.broadcasted_iota(jnp.int32, (q, 128), 1)
     for b in range(fine):
         for chunk in range(out_ref.shape[2] // 128):
@@ -253,26 +371,20 @@
                     continue
                 first = STARTS[k] % 128
                 last = first + len(VOXELS[k])
-                m = links_ref[b, k]
-                safe = jnp.maximum(m, 0)
-                col = SOURCES[k] // 128
-                row = lax.rem(safe, fine)
-                if col < 2:
-                    lanes = pl.ds(128 * col, 128)
-                else:
-                    lanes = pl.ds(pl.multiple_of(lax.div(row, fine // 2) * 128, 128), 128)
-                    row = fine + lax.rem(row, fine // 2)
-                row = pl.multiple_of(base + row * q, 16)
-                got = recv_ref[lax.div(safe, fine), pl.ds(row, q), lanes].astype(F32)
-                turn = (first - SOURCES[k]) % 128
-                if turn:
-                    got = pltpu.roll(got, turn, 1)
-                got = jnp.where(m >= 0, got, 0.0)
-                here = jnp.where((lane >= first) & (lane < last), got, here)
+                v = from_ref[0, b * (128 // fine) + k]
+                safe = jnp.maximum(v, 0)
+                w = lax.shift_right_logical(safe, 10)
+                block = lax.shift_right_logical(safe, 7) & 7
+                row = pl.multiple_of(base + block * half, 16)
+                got = jnp.concatenate(
+                    [recv_ref[w, pl.ds(row, half), 0:128], recv_ref[w, pl.ds(row, half), 128:256]], axis=0
+                ).astype(F32)
+                got = pltpu.roll(got, (first + 128 - (safe & 127)) & 127, 1)
+                here = jnp.where((lane >= first) & (lane < last) & (v >= 0), got, here)
             out_ref[b, :, chunk * 128 : (chunk + 1) * 128] = here.astype(BF16)
 
 
-def halo(links, recv, base, fine, q, vox):
+def halo(places, recv, base, fine, q, vox):
     return pl.pallas_call(
         lambda *refs: halo_kernel(q, base, *refs),
         out_shape=jax.ShapeDtypeStruct((fine, q, vox), BF16),
@@ -280,7 +392,7 @@
         out_specs=pl.BlockSpec(memory_space=VM),
         compiler_params=params(),
         name="halo",
-    )(links, recv)
+    )(places, recv)
 
 
 def axis_places(u):
@@ -684,23 +796,40 @@
     owner = lax.axis_index("brick").astype(jnp.int32)
     me = lax.axis_index("chan").astype(jnp.int32)
     fine, q, vox = features.shape
-    parts = project(me[None], features, down_weight, chans)
-    arrived = [parts[0]] + [
-        lax.ppermute(parts[s], "chan", [(i, i ^ s) for i in range(chans)])
-        for s in range(1, chans)
-    ]
-    early, _ = lax.optimization_barrier((features, parts[0]))
-    outer, packed = spread_out(early, up_weight)
+    own = jnp.pad(fine_links, ((0, -fine % 8), (0, 128 - fine_links.shape[1])), constant_values=-1)
+    parts, chunks, packed = project(me[None], features, down_weight, up_weight, chans)
+    done = {}
+
+    def projected(now):
+        now, done["parts"] = lax.optimization_barrier((now, parts))
+        return now
+
+    def reduced(now):
+        blocks = done["parts"]
+        arrived = [blocks[0]] + [partner(blocks[s], "chan", s, chans) for s in range(1, chans)]
+        now, arrived[1] = lax.optimization_barrier((now, arrived[1]))
+        done["arrived"] = arrived
+        return now
+
+    asked = gathered(own[None], owners, [lambda now: now, projected, reduced])
+    arrived = done["arrived"]
     codes = 8 * coarse_links.shape[0]
-    sending = assemble(arrived, outer, owner[None], coarse_links, parents, owners)
+    sending, places = assemble(arrived, owner[None], coarse_links, parents, asked, own, chunks, owners)
     recv = lax.all_to_all(sending, "brick", split_axis=0, concat_axis=0, tiled=True)
-    packs = exchanged(packed, chans)
+    packs, _ = relayed(packed, chans)
     recv, packs = lax.optimization_barrier((recv, packs))
-    slots = exchanged(recv[:, :q], chans)
-    co = coarse(me[None], slots, recv, codes, coarse_weight, coarse_bias[None])
-    halos = exchanged(halo(fine_links, recv, q + codes, fine, q, vox), chans)
-    cos = exchanged(co, chans)
-    ff, sel, up_all = frames(me[None], owner[None], fine_links, packs, halos, co.shape[0])
+    slots, around = relayed(recv[:, :q], chans, lambda: halo(places, recv, q + codes, fine, q, vox))
+    slots, around = lax.optimization_barrier((slots, around))
+    halos, co = relayed(
+        around,
+        chans,
+        lambda: coarse(me[None], slots, recv, codes, coarse_weight, coarse_bias[None]),
+    )
+    cos, (ff, sel, up_all) = relayed(
+        co,
+        chans,
+        lambda: frames(me[None], owner[None], fine_links, packs, halos, co.shape[0]),
+    )
     return refine(me[None], cos, ff, sel, up_all, fine_weight, fine_bias[None])
 
 

time: 71.9 us -> 63.1 us (0.88)
  waiting for transfers between devices: 27.2 us -> 14.3 us
  starting transfers between devices: 17 us -> 21.3 us
    all_to_all x1, waiting for transfers between devices: 13.3 us -> 2.5 us  [per_device(): lax.all_to_all(sending, 'brick', split_axis=0, concat_axis=0, tiled=True)]
    ppermute x15 -> x18, starting transfers between devices: 11.1 us -> 16 us  [partner(): return lax.ppermute(x, axis, [(i, i ^ step) for i in range(count)])]
    ppermute x15 -> x18, waiting for transfers between devices: 13.9 us -> 11.8 us  [partner(): return lax.ppermute(x, axis, [(i, i ^ step) for i in range(count)])]
    pad x0 -> x1, local copies, waits for them, and re-layouts: none -> 1.27 us  [per_device(): jnp.pad(fine_links, ((0, -fine % 8), (0, 128 - fine_links.shape[1])), con...]
    unnamed x36 -> x44, local copies, waits for them, and re-layouts: 3.34 us -> 2.43 us
    pallas_call x2 -> x1, Pallas kernels: 4.05 us -> 3.29 us  [assemble(): pl.pallas_call(lambda *refs: assemble_kernel(len(slots), len(asked), fine...]
  transfers between devices with their start and end apart: 16 -> 19, of which waited for: 6 -> 14; matrix products, arithmetic and copies ran while one was open for 0% -> 0% of each run, Pallas kernels for 18% -> 22%
where the time goes in v2:
time: 63.1 us; the launch traced here: 62.8 us
  Pallas kernels  23.4 us (37%)
  starting transfers between devices  21.3 us (34%)
  waiting for transfers between devices  14.3 us (23%)
  local copies, waits for them, and re-layouts  3.71 us (6%)
    ppermute x18, starting transfers between devices, partner(): return lax.ppermute(x, axis, [(i, i ^ step) for i in range(count)])  16 us
    ppermute x18, waiting for transfers between devices, partner(): return lax.ppermute(x, axis, [(i, i ^ step) for i in range(count)])  11.8 us
    pallas_call x1, Pallas kernels, refine(): pl.pallas_call(lambda *refs: fine_kernel(chans, *refs), out_shape=jax.Sha...  6.47 us
    pallas_call x1, Pallas kernels, coarse(): pl.pallas_call(lambda *refs: coarse_kernel(chans, codes, *refs), out_shap...  5.48 us
    all_to_all x1, starting transfers between devices, per_device(): lax.all_to_all(sending, 'brick', split_axis=0, concat_axis=0, tiled=True)  5.27 us
    pallas_call x1, Pallas kernels, assemble(): pl.pallas_call(lambda *refs: assemble_kernel(len(slots), len(asked), fine...  3.29 us
    pallas_call x1, Pallas kernels, frames(): pl.pallas_call(lambda *refs: frame_kernel(chans, *refs), out_shape=[jax.S...  3.16 us
    pallas_call x1, Pallas kernels, project(): pl.pallas_call(lambda *refs: project_kernel(chans, *refs), out_shape=[jax...  2.64 us
  transfers between devices with their start and end apart: 19, of which 14 were waited for; matrix products, arithmetic and copies ran while one was open for 0% of the time, Pallas kernels for 22%

profile of v2, /device:TPU:0, one launch (start us, length us, event | category | flops | bytes accessed | tf_op | source)
XLA Modules:
  0.0 62.8 jit_solution(1790651112799173486)
XLA Ops:
  0.0 1.3 %fusion = (s32[8,128]{1,0:T(8,128)}, s32[1,8,128]{2,1,0:T(8,128)S(1)}) fusion(s32[4,26]{1,0:T(4,128)} %refs_2_.4), kind=kLoop, calls=%fused_computation.3 | loop fusion | bytes 8608 | tf_op jit(solution)/shard_map/jit(_pad)/pad | solution.py:799
  1.3 2.9 %collective-permute-start = (s32[1,8,128]{2,1,0:T(8,128)S(1)}, s32[1,8,128]{2,1,0:T(8,128)S(1)}, u32[]{:S(2)}, u32[]{:S(2)}) collective-permute-start(s32[1,8,128]{2,1,0:T(8,128)S(1)} %get-tuple-element.84), channel_id=1, source_target_pairs={{0,4},{4,0},{8,12},{12,8},{16,20},{20,16},{24,28},{28,24},{1,5},{5... | collective-permute-start | bytes 12296 | tf_op jit(solution)/shard_map/ppermute | solution.py:330
  4.2 2.6 %project.1 = (bf16[32,256]{1,0:T(8,128)(2,1)}, bf16[32,256]{1,0:T(8,128)(2,1)}, bf16[32,256]{1,0:T(8,128)(2,1)}, bf16[32,256]{1,0:T(8,128)(2,1)}, bf16[8,128,128...) custom-call(s32[1]{0:T(128)} %bitcast.refs_0_, bf16[128,512]{1,0:T(8,128)(2,1)} %bitcast.9, ...), custom_call_target="tpu_custom_call" | custom-call | tf_op jit(solution)/shard_map/project/pallas_call | solution.py:175
  6.9 0.0 collective-permute-done
  6.9 1.6 %collective-permute-start.1 = (s32[2,8,128]{2,1,0:T(8,128)S(1)}, s32[2,8,128]{2,1,0:T(8,128)S(1)}, u32[]{:S(2)}, u32[]{:S(2)}) collective-permute-start(s32[2,8,128]{2,1,0:T(8,128)S(1)} %pad_add_fusion.1), channel_id=1, source_target_pairs={{0,8},{4,12},{8,0},{12,4},{16,24},{20,28},{24,16},{28,20},{1,9},{5... | collective-permute-start | bytes 24584 | tf_op jit(solution)/shard_map/ppermute | solution.py:330
  8.5 0.0 collective-permute-start.2
  8.5 1.5 %collective-permute-start.3 = (bf16[32,256]{1,0:T(8,128)(2,1)}, bf16[32,256]{1,0:T(8,128)(2,1)S(1)}, u32[]{:S(2)}, u32[]{:S(2)}) collective-permute-start(bf16[32,256]{1,0:T(8,128)(2,1)} %get-tuple-element.52), channel_id=1, source_target_pairs={{0,2},{1,3},{2,0},{3,1},{4,6},{5,7},{6,4},{7,5},{8,10},{9,11},{10,... | collective-permute-start | bytes 49160 | tf_op jit(solution)/shard_map/ppermute | solution.py:330
  10.0 0.3 collective-permute-start.4
  10.4 0.2 collective-permute-done.1
  10.6 0.0 collective-permute-done.2.refs_5_
  10.6 2.7 %collective-permute-start.5 = (s32[4,8,128]{2,1,0:T(8,128)S(1)}, s32[4,8,128]{2,1,0:T(8,128)S(1)}, u32[]{:S(2)}, u32[]{:S(2)}) collective-permute-start(s32[4,8,128]{2,1,0:T(8,128)S(1)} %pad_add_fusion.refs_8_), channel_id=1, source_target_pairs={{0,16},{4,20},{8,24},{12,28},{16,0},{20,4},{24,8},{28,12},{1,17},{... | collective-permute-start | bytes 49160 | tf_op jit(solution)/shard_map/ppermute | solution.py:330
  13.3 0.0 collective-permute-done.3.refs_6_
  13.3 0.1 collective-permute-done.4.refs_7_
  13.4 1.9 %collective-permute-done.5.refs_9_ = s32[4,8,128]{2,1,0:T(8,128)S(1)} collective-permute-done((s32[4,8,128]{2,1,0:T(8,128)S(1)}, s32[4,8,128]{2,1,0:T(8,128)S(1)}, u32[]{:S(2)}, u32[]{:S(2)}) %collective-permute-start.5) | collective-permute-done | bytes 16416 | tf_op jit(solution)/shard_map/ppermute | solution.py:330
  15.3 0.6 copy-done.18
  15.9 3.3 %assemble.1 = (bf16[8,96,256]{2,1,0:T(8,128)(2,1)}, s32[1,128]{1,0:T(1,128)}) custom-call(s32[1]{0:T(128)} %bitcast.1.refs_0_.refs_1_, s32[2,26]{1,0:T(2,128)} %refs_1_.1, s32[4]{0:T(128)} %refs_2_.3, s32[2,16,128]{2,1,0:T(8,128)} %constant.22.clone.refs_3_, bf16[32,256]{1,0:T(8,128)(2,1)} %get-tuple-element.48.refs_4_, bf16[32,256]{1,0:T(8,128)(2,1)} %copy-done.15, ...), custom_call_target="tpu_custom_call" | custom-call | flops 1048576 | bytes 12582912 | tf_op jit(solution)/shard_map/assemble/pallas_call | solution.py:307
  19.2 5.3 %all-to-all-start = ((bf16[8,96,256]{2,1,0:T(8,128)(2,1)}), bf16[8,96,256]{2,1,0:T(8,128)(2,1)S(1)}, u32[]{:S(2)}, u32[]{:S(2)}) async-start(bf16[8,96,256]{2,1,0:T(8,128)(2,1)} %get-tuple-element.56), calls=%async_computation | async-start | bytes 786432 | tf_op jit(solution)/shard_map/all_to_all | solution.py:818
  24.5 1.6 %collective-permute-start.7 = (bf16[192,512]{1,0:T(8,128)(2,1)S(1)}, bf16[192,512]{1,0:T(8,128)(2,1)S(1)}, u32[]{:S(2)}, u32[]{:S(2)}) collective-permute-start(bf16[192,512]{1,0:T(8,128)(2,1)S(1)} %copy-done.2), channel_id=1, source_target_pairs={{0,2},{1,3},{2,0},{3,1},{4,6},{5,7},{6,4},{7,5},{8,10},{9,11},{10,... | collective-permute-start | bytes 589832 | tf_op jit(solution)/shard_map/ppermute | solution.py:330
  26.1 4.1 %collective-permute-done.7.refs_5_ = bf16[192,512]{1,0:T(8,128)(2,1)S(1)} collective-permute-done((bf16[192,512]{1,0:T(8,128)(2,1)S(1)}, bf16[192,512]{1,0:T(8,128)(2,1)S(1)}, u32[]{:S(2)}, u32[]{:S(2)}) %collective-permute-start.7) | collective-permute-done | bytes 196640 | tf_op jit(solution)/shard_map/ppermute | solution.py:330
  30.2 0.0 collective-permute-start.8
  30.2 0.0 collective-permute-done.6.refs_4_
  30.2 1.4 %collective-permute-done.8.refs_6_ = bf16[192,512]{1,0:T(8,128)(2,1)S(1)} collective-permute-done((bf16[192,512]{1,0:T(8,128)(2,1)S(1)}, bf16[192,512]{1,0:T(8,128)(2,1)S(1)}, u32[]{:S(2)}, u32[]{:S(2)}) %collective-permute-start.8) | collective-permute-done | bytes 196640 | tf_op jit(solution)/shard_map/ppermute | solution.py:330
  31.7 2.5 %all-to-all-done.refs_1_.refs_5_ = bf16[8,96,256]{2,1,0:T(8,128)(2,1)S(1)} async-done(((bf16[8,96,256]{2,1,0:T(8,128)(2,1)}), bf16[8,96,256]{2,1,0:T(8,128)(2,1)S(1)}, u32[]{:S(2)}, u32[]{:S(2)}) %all-to-all-start) | async-done | bytes 393248 | tf_op jit(solution)/shard_map/all_to_all | solution.py:818
  34.2 0.0 copy-start.13
  34.2 1.6 %collective-permute-start.9 = (bf16[8,32,256]{2,1,0:T(8,128)(2,1)S(1)}, bf16[8,32,256]{2,1,0:T(8,128)(2,1)S(1)}, u32[]{:S(2)}, u32[]{:S(2)}) collective-permute-start(bf16[8,32,256]{2,1,0:T(8,128)(2,1)S(1)} %slice.3.refs_1_), channel_id=1, source_target_pairs={{0,2},{1,3},{2,0},{3,1},{4,6},{5,7},{6,4},{7,5},{8,10},{9,11},{10,... | collective-permute-start | bytes 393224 | tf_op jit(solution)/shard_map/ppermute | solution.py:330
  35.8 2.3 %halo.1.refs_7_ = bf16[4,32,512]{2,1,0:T(8,128)(2,1)} custom-call(s32[1,128]{1,0:T(1,128)} %get-tuple-element.59.refs_0_, bf16[8,96,256]{2,1,0:T(8,128)(2,1)} %copy-done), custom_call_target="tpu_custom_call" | custom-call | tf_op jit(solution)/shard_map/halo/pallas_call | solution.py:388
  38.1 1.1 %collective-permute-done.9.refs_3_ = bf16[8,32,256]{2,1,0:T(8,128)(2,1)S(1)} collective-permute-done((bf16[8,32,256]{2,1,0:T(8,128)(2,1)S(1)}, bf16[8,32,256]{2,1,0:T(8,128)(2,1)S(1)}, u32[]{:S(2)}, u32[]{:S(2)}) %collective-permute-start.9) | collective-permute-done | bytes 131104 | tf_op jit(solution)/shard_map/ppermute | solution.py:330
  39.2 0.0 collective-permute-start.10
  39.2 0.5 collective-permute-start.11
  39.7 0.8 %collective-permute-done.10.refs_2_ = bf16[8,32,256]{2,1,0:T(8,128)(2,1)S(1)} collective-permute-done((bf16[8,32,256]{2,1,0:T(8,128)(2,1)S(1)}, bf16[8,32,256]{2,1,0:T(8,128)(2,1)S(1)}, u32[]{:S(2)}, u32[]{:S(2)}) %collective-permute-start.10) | collective-permute-done | bytes 131104 | tf_op jit(solution)/shard_map/ppermute | solution.py:330
  40.6 0.2 collective-permute-done.11.refs_4_
  40.8 1.5 %collective-permute-start.12 = (bf16[4,32,512]{2,1,0:T(8,128)(2,1)}, bf16[4,32,512]{2,1,0:T(8,128)(2,1)S(1)}, u32[]{:S(2)}, u32[]{:S(2)}) collective-permute-start(bf16[4,32,512]{2,1,0:T(8,128)(2,1)} %halo.1.refs_7_), channel_id=1, source_target_pairs={{0,2},{1,3},{2,0},{3,1},{4,6},{5,7},{6,4},{7,5},{8,10},{9,11},{10,... | collective-permute-start | bytes 393224 | tf_op jit(solution)/shard_map/ppermute | solution.py:330
  42.3 5.5 %coarse.1.refs_1_ = bf16[1,32,2048]{2,1,0:T(8,128)(2,1)} custom-call(s32[1]{0:T(128)} %bitcast.refs_0_, bf16[8,32,256]{2,1,0:T(8,128)(2,1)} %copy-done.13, bf16[8,32,256]{2,1,0:T(8,128)(2,1)} %copy-done.20, bf16[8,32,256]{2,1,0:T(8,128)(2,1)} %copy-done.19, bf16[8,32,256]{2,1,0:T(8,128)(2,1)} %copy-done.21, bf16[8,96,256]{2,1,0:T(8,128)(2,1)} %copy-done, ...), custom_call_target="tpu_custom_call" | custom-call | flops 452984832 | bytes 2097152 | tf_op jit(solution)/shard_map/coarse/pallas_call | solution.py:508
  47.8 0.1 collective-permute-start.14
  47.9 0.5 collective-permute-start.15
  48.4 0.6 %collective-permute-start.13 = (bf16[1,32,2048]{2,1,0:T(8,128)(2,1)}, bf16[1,32,2048]{2,1,0:T(8,128)(2,1)S(1)}, u32[]{:S(2)}, u32[]{:S(2)}) collective-permute-start(bf16[1,32,2048]{2,1,0:T(8,128)(2,1)} %coarse.1.refs_1_), channel_id=1, source_target_pairs={{0,2},{1,3},{2,0},{3,1},{4,6},{5,7},{6,4},{7,5},{8,10},{9,11},{10,... | collective-permute-start | bytes 393224 | tf_op jit(solution)/shard_map/ppermute | solution.py:330
  49.0 0.2 collective-permute-done.14.refs_8_
  49.2 0.2 collective-permute-done.15.refs_10_
  49.4 0.5 copy-done.9
  49.9 0.7 %copy-done.10 = bf16[4,32,512]{2,1,0:T(8,128)(2,1)} copy-done((bf16[4,32,512]{2,1,0:T(8,128)(2,1)}, bf16[4,32,512]{2,1,0:T(8,128)(2,1)S(1)}, u32[]{:S(2)}) %copy-start.10) | copy-done | bytes 131096
  50.6 3.2 %frames.1 = (bf16[100,48,128]{2,1,0:T(8,128)(2,1)}, bf16[1,9,48,128]{3,2,1,0:T(8,128)(2,1)}, bf16[8,128,128]{2,1,0:T(8,128)(2,1)}) custom-call(s32[1]{0:T(128)} %bitcast.refs_0_, s32[1]{0:T(128)} %bitcast.1.refs_0_.refs_1_, s32[4,26]{1,0:T(4,128)} %refs_2_.4, bf16[192,512]{1,0:T(8,128)(2,1)} %get-tuple-element.69.refs_3_, bf16[192,512]{1,0:T(8,128)(2,1)} %copy-done.4, ...), custom_call_target="tpu_custom_call" | custom-call | tf_op jit(solution)/shard_map/frames/pallas_call | solution.py:631
  53.7 0.4 collective-permute-done.13.refs_3_
  54.1 0.5 collective-permute-start.17
  54.6 0.8 %collective-permute-done.16.refs_2_ = bf16[1,32,2048]{2,1,0:T(8,128)(2,1)S(1)} collective-permute-done((bf16[1,32,2048]{2,1,0:T(8,128)(2,1)S(1)}, bf16[1,32,2048]{2,1,0:T(8,128)(2,1)S(1)}, u32[]{:S(2)}, u32[]{:S(2)}) %collective-permute-start.16) | collective-permute-done | bytes 131104 | tf_op jit(solution)/shard_map/ppermute | solution.py:330
  55.4 0.2 collective-permute-done.17.refs_4_
  55.6 0.5 copy-done.11
  56.1 0.2 copy-done.12
  56.3 6.5 %refine.1 = bf16[4,32,512]{2,1,0:T(8,128)(2,1)} custom-call(s32[1]{0:T(128)} %bitcast.refs_0_, bf16[1,32,2048]{2,1,0:T(8,128)(2,1)} %coarse.1.refs_1_, bf16[1,32,2048]{2,1,0:T(8,128)(2,1)} %copy-done.11, bf16[1,32,2048]{2,1,0:T(8,128)(2,1)} %copy-done.7, bf16[1,32,2048]{2,1,0:T(8,128)(2,1)} %copy-done.12, bf16[100,48,128]{2,1,0:T(8,128)(2,1)} %get-tuple-element.80.refs_5_, ...), custom_call_target="tpu_custom_call" | custom-call | flops 452984832 | bytes 4194304 | tf_op jit(solution)/shard_map/refine/pallas_call | solution.py:749
  (44 shorter events, 0.1 us)
Async XLA Ops:
  1.3 5.6 %collective-permute-start = (s32[1,8,128]{2,1,0:T(8,128)S(1)}, s32[1,8,128]{2,1,0:T(8,128)S(1)}, u32[]{:S(2)}, u32[]{:S(2)}) collective-permute-start(s32[1,8,128]{2,1,0:T(8,128)S(1)} %get-tuple-element.84), channel_id=1, source_target_pairs={{0,4},{4,0},{8,12},{12,8},{16,20},{20,16},{24,28},{28,24},{1,5},{5... | collective-permute-start | bytes 12296 | tf_op jit(solution)/shard_map/ppermute | solution.py:330
  6.9 17.6 %copy-start.2 = (bf16[192,512]{1,0:T(8,128)(2,1)S(1)}, bf16[192,512]{1,0:T(8,128)(2,1)}, u32[]{:S(2)}) copy-start(bf16[192,512]{1,0:T(8,128)(2,1)} %get-tuple-element.69.refs_3_) | copy-start | bytes 589828
  6.9 3.7 %collective-permute-start.1 = (s32[2,8,128]{2,1,0:T(8,128)S(1)}, s32[2,8,128]{2,1,0:T(8,128)S(1)}, u32[]{:S(2)}, u32[]{:S(2)}) collective-permute-start(s32[2,8,128]{2,1,0:T(8,128)S(1)} %pad_add_fusion.1), channel_id=1, source_target_pairs={{0,8},{4,12},{8,0},{12,4},{16,24},{20,28},{24,16},{28,20},{1,9},{5... | collective-permute-start | bytes 24584 | tf_op jit(solution)/shard_map/ppermute | solution.py:330
  8.5 2.1 %collective-permute-start.2 = (bf16[32,256]{1,0:T(8,128)(2,1)}, bf16[32,256]{1,0:T(8,128)(2,1)S(1)}, u32[]{:S(2)}, u32[]{:S(2)}) collective-permute-start(bf16[32,256]{1,0:T(8,128)(2,1)} %get-tuple-element.50), channel_id=1, source_target_pairs={{0,1},{1,0},{2,3},{3,2},{4,5},{5,4},{6,7},{7,6},{8,9},{9,8},{10,11... | collective-permute-start | bytes 49160 | tf_op jit(solution)/shard_map/ppermute | solution.py:330
  8.5 4.8 %collective-permute-start.3 = (bf16[32,256]{1,0:T(8,128)(2,1)}, bf16[32,256]{1,0:T(8,128)(2,1)S(1)}, u32[]{:S(2)}, u32[]{:S(2)}) collective-permute-start(bf16[32,256]{1,0:T(8,128)(2,1)} %get-tuple-element.52), channel_id=1, source_target_pairs={{0,2},{1,3},{2,0},{3,1},{4,6},{5,7},{6,4},{7,5},{8,10},{9,11},{10,... | collective-permute-start | bytes 49160 | tf_op jit(solution)/shard_map/ppermute | solution.py:330
  10.0 3.4 %collective-permute-start.4 = (bf16[32,256]{1,0:T(8,128)(2,1)}, bf16[32,256]{1,0:T(8,128)(2,1)S(1)}, u32[]{:S(2)}, u32[]{:S(2)}) collective-permute-start(bf16[32,256]{1,0:T(8,128)(2,1)} %get-tuple-element.53), channel_id=1, source_target_pairs={{0,3},{1,2},{2,1},{3,0},{4,7},{5,6},{6,5},{7,4},{8,11},{9,10},{10,... | collective-permute-start | bytes 49160 | tf_op jit(solution)/shard_map/ppermute | solution.py:330
  10.6 4.7 %copy-start.14 = (s32[4,8,128]{2,1,0:T(8,128)}, s32[4,8,128]{2,1,0:T(8,128)S(1)}, u32[]{:S(2)}) copy-start(s32[4,8,128]{2,1,0:T(8,128)S(1)} %pad_add_fusion.refs_8_) | copy-start | bytes 49156
  10.6 4.7 %copy-start.15 = (bf16[32,256]{1,0:T(8,128)(2,1)}, bf16[32,256]{1,0:T(8,128)(2,1)S(1)}, u32[]{:S(2)}) copy-start(bf16[32,256]{1,0:T(8,128)(2,1)S(1)} %collective-permute-done.2.refs_5_) | copy-start | bytes 49156
  10.6 4.7 %collective-permute-start.5 = (s32[4,8,128]{2,1,0:T(8,128)S(1)}, s32[4,8,128]{2,1,0:T(8,128)S(1)}, u32[]{:S(2)}, u32[]{:S(2)}) collective-permute-start(s32[4,8,128]{2,1,0:T(8,128)S(1)} %pad_add_fusion.refs_8_), channel_id=1, source_target_pairs={{0,16},{4,20},{8,24},{12,28},{16,0},{20,4},{24,8},{28,12},{1,17},{... | collective-permute-start | bytes 49160 | tf_op jit(solution)/shard_map/ppermute | solution.py:330
  13.3 2.1 %copy-start.16 = (bf16[32,256]{1,0:T(8,128)(2,1)}, bf16[32,256]{1,0:T(8,128)(2,1)S(1)}, u32[]{:S(2)}) copy-start(bf16[32,256]{1,0:T(8,128)(2,1)S(1)} %collective-permute-done.3.refs_6_) | copy-start | bytes 49156
  13.4 1.9 %copy-start.17 = (bf16[32,256]{1,0:T(8,128)(2,1)}, bf16[32,256]{1,0:T(8,128)(2,1)S(1)}, u32[]{:S(2)}) copy-start(bf16[32,256]{1,0:T(8,128)(2,1)S(1)} %collective-permute-done.4.refs_7_) | copy-start | bytes 49156
  15.3 0.6 copy-start.18
  19.2 15.0 %all-to-all-start = ((bf16[8,96,256]{2,1,0:T(8,128)(2,1)}), bf16[8,96,256]{2,1,0:T(8,128)(2,1)S(1)}, u32[]{:S(2)}, u32[]{:S(2)}) async-start(bf16[8,96,256]{2,1,0:T(8,128)(2,1)} %get-tuple-element.56), calls=%async_computation | async-start | bytes 786432 | tf_op jit(solution)/shard_map/all_to_all | solution.py:818
  24.5 5.7 %collective-permute-start.7 = (bf16[192,512]{1,0:T(8,128)(2,1)S(1)}, bf16[192,512]{1,0:T(8,128)(2,1)S(1)}, u32[]{:S(2)}, u32[]{:S(2)}) collective-permute-start(bf16[192,512]{1,0:T(8,128)(2,1)S(1)} %copy-done.2), channel_id=1, source_target_pairs={{0,2},{1,3},{2,0},{3,1},{4,6},{5,7},{6,4},{7,5},{8,10},{9,11},{10,... | collective-permute-start | bytes 589832 | tf_op jit(solution)/shard_map/ppermute | solution.py:330
  26.1 4.2 %collective-permute-start.6 = (bf16[192,512]{1,0:T(8,128)(2,1)S(1)}, bf16[192,512]{1,0:T(8,128)(2,1)S(1)}, u32[]{:S(2)}, u32[]{:S(2)}) collective-permute-start(bf16[192,512]{1,0:T(8,128)(2,1)S(1)} %copy-done.2), channel_id=1, source_target_pairs={{0,1},{1,0},{2,3},{3,2},{4,5},{5,4},{6,7},{7,6},{8,9},{9,8},{10,11... | collective-permute-start | bytes 589832 | tf_op jit(solution)/shard_map/ppermute | solution.py:330
  30.2 17.6 %copy-start.3 = (bf16[192,512]{1,0:T(8,128)(2,1)}, bf16[192,512]{1,0:T(8,128)(2,1)S(1)}, u32[]{:S(2)}) copy-start(bf16[192,512]{1,0:T(8,128)(2,1)S(1)} %collective-permute-done.7.refs_5_) | copy-start | bytes 589828
  30.2 1.4 %collective-permute-start.8 = (bf16[192,512]{1,0:T(8,128)(2,1)S(1)}, bf16[192,512]{1,0:T(8,128)(2,1)S(1)}, u32[]{:S(2)}, u32[]{:S(2)}) collective-permute-start(bf16[192,512]{1,0:T(8,128)(2,1)S(1)} %collective-permute-done.7.refs_5_), channel_id=1, source_target_pairs={{0,1},{1,0},{2,3},{3,2},{4,5},{5,4},{6,7},{7,6},{8,9},{9,8},{10,11... | collective-permute-start | bytes 589832 | tf_op jit(solution)/shard_map/ppermute | solution.py:330
  30.2 19.2 %copy-start.4 = (bf16[192,512]{1,0:T(8,128)(2,1)}, bf16[192,512]{1,0:T(8,128)(2,1)S(1)}, u32[]{:S(2)}) copy-start(bf16[192,512]{1,0:T(8,128)(2,1)S(1)} %collective-permute-done.6.refs_4_) | copy-start | bytes 589828
  31.7 17.8 %copy-start.5 = (bf16[192,512]{1,0:T(8,128)(2,1)}, bf16[192,512]{1,0:T(8,128)(2,1)S(1)}, u32[]{:S(2)}) copy-start(bf16[192,512]{1,0:T(8,128)(2,1)S(1)} %collective-permute-done.8.refs_6_) | copy-start | bytes 589828
  34.2 1.6 %copy-start = (bf16[8,96,256]{2,1,0:T(8,128)(2,1)}, bf16[8,96,256]{2,1,0:T(8,128)(2,1)S(1)}, u32[]{:S(2)}) copy-start(bf16[8,96,256]{2,1,0:T(8,128)(2,1)S(1)} %all-to-all-done.refs_1_.refs_5_) | copy-start | bytes 1179652
  34.2 8.1 %copy-start.13 = (bf16[8,32,256]{2,1,0:T(8,128)(2,1)}, bf16[8,32,256]{2,1,0:T(8,128)(2,1)S(1)}, u32[]{:S(2)}) copy-start(bf16[8,32,256]{2,1,0:T(8,128)(2,1)S(1)} %slice.3.refs_1_) | copy-start | bytes 393220
  34.2 5.0 %collective-permute-start.9 = (bf16[8,32,256]{2,1,0:T(8,128)(2,1)S(1)}, bf16[8,32,256]{2,1,0:T(8,128)(2,1)S(1)}, u32[]{:S(2)}, u32[]{:S(2)}) collective-permute-start(bf16[8,32,256]{2,1,0:T(8,128)(2,1)S(1)} %slice.3.refs_1_), channel_id=1, source_target_pairs={{0,2},{1,3},{2,0},{3,1},{4,6},{5,7},{6,4},{7,5},{8,10},{9,11},{10,... | collective-permute-start | bytes 393224 | tf_op jit(solution)/shard_map/ppermute | solution.py:330
  38.1 9.7 %copy-start.1 = (bf16[4,32,512]{2,1,0:T(8,128)(2,1)S(1)}, bf16[4,32,512]{2,1,0:T(8,128)(2,1)}, u32[]{:S(2)}) copy-start(bf16[4,32,512]{2,1,0:T(8,128)(2,1)} %halo.1.refs_7_) | copy-start | bytes 393220
  39.2 3.1 %copy-start.19 = (bf16[8,32,256]{2,1,0:T(8,128)(2,1)}, bf16[8,32,256]{2,1,0:T(8,128)(2,1)S(1)}, u32[]{:S(2)}) copy-start(bf16[8,32,256]{2,1,0:T(8,128)(2,1)S(1)} %collective-permute-done.9.refs_3_) | copy-start | bytes 393220
  39.2 1.3 %collective-permute-start.10 = (bf16[8,32,256]{2,1,0:T(8,128)(2,1)S(1)}, bf16[8,32,256]{2,1,0:T(8,128)(2,1)S(1)}, u32[]{:S(2)}, u32[]{:S(2)}) collective-permute-start(bf16[8,32,256]{2,1,0:T(8,128)(2,1)S(1)} %slice.3.refs_1_), channel_id=1, source_target_pairs={{0,1},{1,0},{2,3},{3,2},{4,5},{5,4},{6,7},{7,6},{8,9},{9,8},{10,11... | collective-permute-start | bytes 393224 | tf_op jit(solution)/shard_map/ppermute | solution.py:330
  39.2 1.5 %collective-permute-start.11 = (bf16[8,32,256]{2,1,0:T(8,128)(2,1)S(1)}, bf16[8,32,256]{2,1,0:T(8,128)(2,1)S(1)}, u32[]{:S(2)}, u32[]{:S(2)}) collective-permute-start(bf16[8,32,256]{2,1,0:T(8,128)(2,1)S(1)} %collective-permute-done.9.refs_3_), channel_id=1, source_target_pairs={{0,1},{1,0},{2,3},{3,2},{4,5},{5,4},{6,7},{7,6},{8,9},{9,8},{10,11... | collective-permute-start | bytes 393224 | tf_op jit(solution)/shard_map/ppermute | solution.py:330
  40.6 1.7 %copy-start.20 = (bf16[8,32,256]{2,1,0:T(8,128)(2,1)}, bf16[8,32,256]{2,1,0:T(8,128)(2,1)S(1)}, u32[]{:S(2)}) copy-start(bf16[8,32,256]{2,1,0:T(8,128)(2,1)S(1)} %collective-permute-done.10.refs_2_) | copy-start | bytes 393220
  40.8 1.5 %copy-start.21 = (bf16[8,32,256]{2,1,0:T(8,128)(2,1)}, bf16[8,32,256]{2,1,0:T(8,128)(2,1)S(1)}, u32[]{:S(2)}) copy-start(bf16[8,32,256]{2,1,0:T(8,128)(2,1)S(1)} %collective-permute-done.11.refs_4_) | copy-start | bytes 393220
  40.8 7.0 %collective-permute-start.12 = (bf16[4,32,512]{2,1,0:T(8,128)(2,1)}, bf16[4,32,512]{2,1,0:T(8,128)(2,1)S(1)}, u32[]{:S(2)}, u32[]{:S(2)}) collective-permute-start(bf16[4,32,512]{2,1,0:T(8,128)(2,1)} %halo.1.refs_7_), channel_id=1, source_target_pairs={{0,2},{1,3},{2,0},{3,1},{4,6},{5,7},{6,4},{7,5},{8,10},{9,11},{10,... | collective-permute-start | bytes 393224 | tf_op jit(solution)/shard_map/ppermute | solution.py:330
  47.8 6.3 %copy-start.6 = (bf16[1,32,2048]{2,1,0:T(8,128)(2,1)S(1)}, bf16[1,32,2048]{2,1,0:T(8,128)(2,1)}, u32[]{:S(2)}) copy-start(bf16[1,32,2048]{2,1,0:T(8,128)(2,1)} %coarse.1.refs_1_) | copy-start | bytes 393220
  47.8 1.6 %copy-start.8 = (bf16[4,32,512]{2,1,0:T(8,128)(2,1)}, bf16[4,32,512]{2,1,0:T(8,128)(2,1)S(1)}, u32[]{:S(2)}) copy-start(bf16[4,32,512]{2,1,0:T(8,128)(2,1)S(1)} %collective-permute-done.12.refs_9_) | copy-start | bytes 393220
  47.8 1.4 %collective-permute-start.14 = (bf16[4,32,512]{2,1,0:T(8,128)(2,1)S(1)}, bf16[4,32,512]{2,1,0:T(8,128)(2,1)S(1)}, u32[]{:S(2)}, u32[]{:S(2)}) collective-permute-start(bf16[4,32,512]{2,1,0:T(8,128)(2,1)S(1)} %copy-done.1), channel_id=1, source_target_pairs={{0,1},{1,0},{2,3},{3,2},{4,5},{5,4},{6,7},{7,6},{8,9},{9,8},{10,11... | collective-permute-start | bytes 393224 | tf_op jit(solution)/shard_map/ppermute | solution.py:330
  47.9 1.5 %collective-permute-start.15 = (bf16[4,32,512]{2,1,0:T(8,128)(2,1)S(1)}, bf16[4,32,512]{2,1,0:T(8,128)(2,1)S(1)}, u32[]{:S(2)}, u32[]{:S(2)}) collective-permute-start(bf16[4,32,512]{2,1,0:T(8,128)(2,1)S(1)} %collective-permute-done.12.refs_9_), channel_id=1, source_target_pairs={{0,1},{1,0},{2,3},{3,2},{4,5},{5,4},{6,7},{7,6},{8,9},{9,8},{10,11... | collective-permute-start | bytes 393224 | tf_op jit(solution)/shard_map/ppermute | solution.py:330
  48.4 5.7 %collective-permute-start.13 = (bf16[1,32,2048]{2,1,0:T(8,128)(2,1)}, bf16[1,32,2048]{2,1,0:T(8,128)(2,1)S(1)}, u32[]{:S(2)}, u32[]{:S(2)}) collective-permute-start(bf16[1,32,2048]{2,1,0:T(8,128)(2,1)} %coarse.1.refs_1_), channel_id=1, source_target_pairs={{0,2},{1,3},{2,0},{3,1},{4,6},{5,7},{6,4},{7,5},{8,10},{9,11},{10,... | collective-permute-start | bytes 393224 | tf_op jit(solution)/shard_map/ppermute | solution.py:330
  49.2 0.7 %copy-start.9 = (bf16[4,32,512]{2,1,0:T(8,128)(2,1)}, bf16[4,32,512]{2,1,0:T(8,128)(2,1)S(1)}, u32[]{:S(2)}) copy-start(bf16[4,32,512]{2,1,0:T(8,128)(2,1)S(1)} %collective-permute-done.14.refs_8_) | copy-start | bytes 393220
  49.9 0.7 %copy-start.10 = (bf16[4,32,512]{2,1,0:T(8,128)(2,1)}, bf16[4,32,512]{2,1,0:T(8,128)(2,1)S(1)}, u32[]{:S(2)}) copy-start(bf16[4,32,512]{2,1,0:T(8,128)(2,1)S(1)} %collective-permute-done.15.refs_10_) | copy-start | bytes 393220
  54.1 1.5 %copy-start.7 = (bf16[1,32,2048]{2,1,0:T(8,128)(2,1)}, bf16[1,32,2048]{2,1,0:T(8,128)(2,1)S(1)}, u32[]{:S(2)}) copy-start(bf16[1,32,2048]{2,1,0:T(8,128)(2,1)S(1)} %collective-permute-done.13.refs_3_) | copy-start | bytes 393220
  54.1 1.3 %collective-permute-start.16 = (bf16[1,32,2048]{2,1,0:T(8,128)(2,1)S(1)}, bf16[1,32,2048]{2,1,0:T(8,128)(2,1)S(1)}, u32[]{:S(2)}, u32[]{:S(2)}) collective-permute-start(bf16[1,32,2048]{2,1,0:T(8,128)(2,1)S(1)} %copy-done.6), channel_id=1, source_target_pairs={{0,1},{1,0},{2,3},{3,2},{4,5},{5,4},{6,7},{7,6},{8,9},{9,8},{10,11... | collective-permute-start | bytes 393224 | tf_op jit(solution)/shard_map/ppermute | solution.py:330
  54.1 1.5 %collective-permute-start.17 = (bf16[1,32,2048]{2,1,0:T(8,128)(2,1)S(1)}, bf16[1,32,2048]{2,1,0:T(8,128)(2,1)S(1)}, u32[]{:S(2)}, u32[]{:S(2)}) collective-permute-start(bf16[1,32,2048]{2,1,0:T(8,128)(2,1)S(1)} %collective-permute-done.13.refs_3_), channel_id=1, source_target_pairs={{0,1},{1,0},{2,3},{3,2},{4,5},{5,4},{6,7},{7,6},{8,9},{9,8},{10,11... | collective-permute-start | bytes 393224 | tf_op jit(solution)/shard_map/ppermute | solution.py:330
  55.4 0.7 %copy-start.11 = (bf16[1,32,2048]{2,1,0:T(8,128)(2,1)}, bf16[1,32,2048]{2,1,0:T(8,128)(2,1)S(1)}, u32[]{:S(2)}) copy-start(bf16[1,32,2048]{2,1,0:T(8,128)(2,1)S(1)} %collective-permute-done.16.refs_2_) | copy-start | bytes 393220
  55.6 0.7 %copy-start.12 = (bf16[1,32,2048]{2,1,0:T(8,128)(2,1)}, bf16[1,32,2048]{2,1,0:T(8,128)(2,1)S(1)}, u32[]{:S(2)}) copy-start(bf16[1,32,2048]{2,1,0:T(8,128)(2,1)S(1)} %collective-permute-done.17.refs_4_) | copy-start | bytes 393220

commit v3 on v2

--- a/solution.py
+++ b/solution.py
@@ -13,6 +13,7 @@
 NBLK = 32
 F32 = jnp.float32
 BF16 = jnp.bfloat16
+META = 96
 VMEM_LIMIT = 56 * 1024 * 1024
 
 
@@ -194,17 +195,22 @@
     return res[:chans], res[chans], res[chans + 1]
 
 
+def padded(rows, wide):
+    return jnp.concatenate([rows, jnp.full((rows.shape[0], wide - rows.shape[1]), -1, jnp.int32)], axis=1)
+
+
 def choose(
-    fine, q, faces, rims, base, owner_ref, asked_refs, own_ref, lanes_ref, earlier_ref, chunk_ref,
+    fine, q, faces, rims, digits, owner_ref, asked_refs, own_ref, lanes_ref, earlier_ref, chunk_ref,
     out_ref, from_ref, table, scalars, sem,
 ):
+    order = xor_order(out_ref.shape[0])
     owners = out_ref.shape[0]
     place = lanes_ref[0:1, :]
     is_face = lanes_ref[1:2, :] == 1
     wide = 128 // fine
     asked = jnp.concatenate(
         [
-            jnp.concatenate([ref[:, b, :][:, :wide] for ref in asked_refs], axis=0)
+            jnp.concatenate([padded(ref[:, b, :], wide) for ref in asked_refs], axis=0)
             for b in range(fine)
         ],
         axis=1,
@@ -221,7 +227,7 @@
     table[...] = found.astype(jnp.int32) - 1
     copy = pltpu.make_async_copy(table, scalars, sem)
     copy.start()
-    own = jnp.concatenate([own_ref[b : b + 1, :wide] for b in range(fine)], axis=1)
+    own = jnp.concatenate([padded(own_ref[b : b + 1, :], wide) for b in range(fine)], axis=1)
     own = jnp.broadcast_to(own, (owners, 128))
     theirs = lax.div(jnp.maximum(own, 0), fine)
     mask = (own >= 0) & (theirs == lax.broadcasted_iota(jnp.int32, (owners, 128), 0))
@@ -233,8 +239,9 @@
     half = q // 2
 
     def one(r_owner, _):
-        w = owner_ref[0] ^ r_owner
-        for block in range((out_ref.shape[1] - base) // half):
+        w = owner_ref[0] ^ (order[r_owner] if owners <= 8 else reversed_bits(r_owner, owners))
+        blocks = (out_ref.shape[1] - q) // half
+        for block in range(blocks):
             here = jnp.zeros((q, 128), F32)
             for r in range(faces + rims):
                 pos = r * FACE if r < faces else faces * FACE + (r - faces) * EDGE
@@ -251,9 +258,12 @@
                     got = pltpu.roll(got, (first + 128 - (safe & 127)) & 127, 1)
                     size = EDGE
                 here = jnp.where((side >= first) & (side < first + size) & (v >= 0), got, here)
-            here = here.astype(BF16)
+            at = q + block * half
             for i in range(2):
-                out_ref[w, base + block * half : base + (block + 1) * half, 128 * i : 128 * i + 128] = here[i * half : (i + 1) * half]
+                part = here[i * half : (i + 1) * half]
+                if block == blocks - 1:
+                    part = part + digits[i]
+                out_ref[w, at : at + half, 128 * i : 128 * i + 128] = part.astype(BF16)
         return 0
 
     if owners <= 8:
@@ -283,14 +293,12 @@
             brick = owner_ref[0] * count + p if k == ways else links_ref[p, k]
             code = jnp.where(own & (column == k), jnp.where(brick >= 0, brick * 8 + octant + 1, 0), code)
     for b in range(parents_ref.shape[0]):
-        code = jnp.where((row == b) & (lane == 27), parents_ref[b] + 1, code)
+        code = jnp.where((row == b) & (lane == META + 27), parents_ref[b] + 1, code)
     high = lax.shift_right_logical(code, 7)
-    digits = [high.astype(F32).astype(BF16), (code - high * 128).astype(F32).astype(BF16)]
+    digits = [high.astype(F32), (code - high * 128).astype(F32)]
     for w in range(out_ref.shape[0]):
         out_ref[w, 0:q, :] = total
-        for i in range(2):
-            out_ref[w, q : q + rows, 128 * i : 128 * i + 128] = digits[i]
-    choose(fine, q, faces, rims, q + rows, owner_ref, asked_refs, *refs)
+    choose(fine, q, faces, rims, digits, owner_ref, asked_refs, *refs)
 
 
 def assemble(slots, owner, coarse_links, parents, asked, own, chunks, owners):
@@ -299,15 +307,16 @@
     fine = parents.shape[0]
     columns, octants = octant_table()
     table = np.full((2, count * 8, 128), -1, np.int32)
-    table[0, :, :27] = np.tile(columns, (count, 1))
-    table[1, :, :27] = np.tile(octants, (count, 1))
+    table[0, :, META : META + 27] = np.tile(columns, (count, 1))
+    table[1, :, META : META + 27] = np.tile(octants, (count, 1))
     faces, rims = capacities(fine, owners)
     blocks = -(-(faces * FACE + rims * EDGE) // 128)
+    assert count * 8 == q // 2 and (faces * FACE + rims * EDGE - 1) % 128 < META
     entries, earlier = entry_tables(fine)
     return pl.pallas_call(
         lambda *refs: assemble_kernel(len(slots), len(asked), fine, faces, rims, *refs),
         out_shape=[
-            jax.ShapeDtypeStruct((owners, q + count * 8 + blocks * q // 2, lanes), BF16),
+            jax.ShapeDtypeStruct((owners, q + blocks * q // 2, lanes), BF16),
             jax.ShapeDtypeStruct((1, 128), jnp.int32),
         ],
         in_specs=[pl.BlockSpec(memory_space=SM)] * 3 + [pl.BlockSpec(memory_space=VM)] * (len(slots) + len(asked) + 5),
@@ -347,14 +356,27 @@
     return [slots[s] for s in range(chans)], other
 
 
+def reversed_bits(r, count):
+    out, bit = 0, 1
+    while bit < count:
+        out = out * 2 + r % 2
+        r = r // 2
+        bit *= 2
+    return out
+
+
+def xor_order(count):
+    return [reversed_bits(r, count) for r in range(count)]
+
+
 def gathered(x, owners, between):
-    have, step, count = [x], 1, 0
-    while step < owners:
+    have, step, count = [x], owners // 2, 0
+    while step:
         now = jnp.concatenate(have, axis=0) if len(have) > 1 else have[0]
         if count < len(between):
             now = between[count](now)
         have = [now, partner(now, "brick", step, owners)]
-        step *= 2
+        step //= 2
         count += 1
     return have
 
@@ -429,11 +451,11 @@
     @pl.when(pl.program_id(0) == 0)
     def _():
         for w in range(owners):
-            digits = recv_ref[w, q : q + codes, :]
+            digits = recv_ref[w]
             table_ref[w * codes : (w + 1) * codes, :] = digits
             digits = digits.astype(F32)
             value = digits[:, 0:128] * 128.0 + digits[:, 128:256] - 1.0
-            parent_ref[w * fine : (w + 1) * fine, :] = jnp.broadcast_to(value[0:fine, 27:28], (fine, 128))
+            parent_ref[w * fine : (w + 1) * fine, :] = jnp.broadcast_to(value[0:fine, META + 27 : META + 28], (fine, 128))
         for s in range(chans):
             proj_ref[me ^ s] = slots[s][...]
         if owners <= 8:
@@ -450,7 +472,7 @@
     on = lax.broadcasted_iota(jnp.int32, (total, total), 0) == lax.broadcasted_iota(jnp.int32, (total, total), 1)
     parents = jnp.sum(jnp.where(on, parent_ref[:, 0:1], 0.0), axis=0, keepdims=True)
     for d in range(27):
-        sel_ref[d * NBLK : (d + 1) * NBLK, :] = (target[:, d : d + 1] == parents).astype(F32).astype(BF16)
+        sel_ref[d * NBLK : (d + 1) * NBLK, :] = (target[:, META + d : META + d + 1] == parents).astype(F32).astype(BF16)
     for ux in range(HALF):
         for uy in range(HALF):
             for uz in range(HALF):
@@ -473,6 +495,7 @@
     acc = conv_rows(
         w_ref,
         lambda a2, a3: nb_ref[:, a2 : a2 + HALF, a3 : a3 + HALF].reshape(size, nb_ref.shape[4]),
+        2,
     )
     step = HALF * HALF * NBLK
     n = HALF * step
@@ -480,11 +503,11 @@
     out_ref[0] = jnp.maximum(res + bias_column(bias_ref[...]), 0.0).astype(BF16)
 
 
-def conv_rows(w_ref, rows_of):
+def conv_rows(w_ref, rows_of, together):
     taps = [(a2, a3) for a2 in range(3) for a3 in range(3)]
     acc = None
-    for i in range(0, 9, 2):
-        some = taps[i : i + 2]
+    for i in range(0, 9, together):
+        some = taps[i : i + together]
         lhs = jnp.concatenate(
             [
                 jnp.concatenate([w_ref[9 * a1 + 3 * a2 + a3] for a1 in range(3)], axis=0)
@@ -512,7 +535,7 @@
         in_specs=[pl.BlockSpec(memory_space=SM)]
         + [whole(a) for a in slots]
         + [
-            pl.BlockSpec((owners, q + codes, recv.shape[2]), lambda i: (0, 0, 0)),
+            pl.BlockSpec((owners, codes, recv.shape[2]), lambda i: (0, recv.shape[1] // codes - 1, 0)),
             whole(weight),
             whole(bias),
         ],
@@ -731,6 +754,7 @@
         acc = conv_rows(
             w_ref,
             lambda a2, a3: g3[a3, pair, :, a2 : a2 + EDGE].reshape(FRAME * step, c_all),
+            9,
         )
         res = acc[0:q, 0:n] + acc[q : 2 * q, step : step + n] + acc[2 * q : 3 * q, 2 * step : 2 * step + n]
         res = jnp.maximum(res + bias, 0.0).astype(BF16)
@@ -796,7 +820,6 @@
     owner = lax.axis_index("brick").astype(jnp.int32)
     me = lax.axis_index("chan").astype(jnp.int32)
     fine, q, vox = features.shape
-    own = jnp.pad(fine_links, ((0, -fine % 8), (0, 128 - fine_links.shape[1])), constant_values=-1)
     parts, chunks, packed = project(me[None], features, down_weight, up_weight, chans)
     done = {}
 
@@ -811,15 +834,14 @@
         done["arrived"] = arrived
         return now
 
-    asked = gathered(own[None], owners, [lambda now: now, projected, reduced])
+    asked = gathered(fine_links[None], owners, [lambda now: now, projected, reduced])
     arrived = done["arrived"]
     codes = 8 * coarse_links.shape[0]
-    sending, places = assemble(arrived, owner[None], coarse_links, parents, asked, own, chunks, owners)
+    sending, places = assemble(arrived, owner[None], coarse_links, parents, asked, fine_links, chunks, owners)
     recv = lax.all_to_all(sending, "brick", split_axis=0, concat_axis=0, tiled=True)
     packs, _ = relayed(packed, chans)
     recv, packs = lax.optimization_barrier((recv, packs))
-    slots, around = relayed(recv[:, :q], chans, lambda: halo(places, recv, q + codes, fine, q, vox))
-    slots, around = lax.optimization_barrier((slots, around))
+    slots, around = relayed(recv[:, :q], chans, lambda: halo(places, recv, q, fine, q, vox))
     halos, co = relayed(
         around,
         chans,

time: 63.1 us -> 59.8 us (0.948)
  waiting for transfers between devices: 14.3 us -> 12.3 us
  Pallas kernels: 23.4 us -> 22.6 us
    pad x1 -> x0, local copies, waits for them, and re-layouts: 1.27 us -> none  [per_device(): jnp.pad(fine_links, ((0, -fine % 8), (0, 128 - fine_links.shape[1])), con...]
    all_to_all x1, waiting for transfers between devices: 2.5 us -> 1.49 us  [per_device(): lax.all_to_all(sending, 'brick', split_axis=0, concat_axis=0, tiled=True)]
    ppermute x18, waiting for transfers between devices: 11.8 us -> 10.8 us  [partner(): return lax.ppermute(x, axis, [(i, i ^ step) for i in range(count)])]
    unnamed x44, local copies, waits for them, and re-layouts: 2.43 us -> 3.2 us
    pallas_call x1, Pallas kernels: 6.47 us -> 5.84 us  [refine(): pl.pallas_call(lambda *refs: fine_kernel(chans, *refs), out_shape=jax.Sha...]
  transfers between devices with their start and end apart: 19 -> 19, of which waited for: 14 -> 12; matrix products, arithmetic and copies ran while one was open for 0% -> 0% of each run, Pallas kernels for 22% -> 23%
where the time goes in v3:
time: 59.8 us; the launch traced here: 59.4 us
  Pallas kernels  22.6 us (38%)
  starting transfers between devices  21.1 us (35%)
  waiting for transfers between devices  12.3 us (21%)
  local copies, waits for them, and re-layouts  3.21 us (5%)
    ppermute x18, starting transfers between devices, partner(): return lax.ppermute(x, axis, [(i, i ^ step) for i in range(count)])  16 us
    ppermute x18, waiting for transfers between devices, partner(): return lax.ppermute(x, axis, [(i, i ^ step) for i in range(count)])  10.8 us
    pallas_call x1, Pallas kernels, refine(): pl.pallas_call(lambda *refs: fine_kernel(chans, *refs), out_shape=jax.Sha...  5.84 us
    pallas_call x1, Pallas kernels, coarse(): pl.pallas_call(lambda *refs: coarse_kernel(chans, codes, *refs), out_shap...  5.42 us
    all_to_all x1, starting transfers between devices, per_device(): lax.all_to_all(sending, 'brick', split_axis=0, concat_axis=0, tiled=True)  5.19 us
    pallas_call x1, Pallas kernels, assemble(): pl.pallas_call(lambda *refs: assemble_kernel(len(slots), len(asked), fine...  3.28 us
    unnamed x44, local copies, waits for them, and re-layouts  3.2 us
    pallas_call x1, Pallas kernels, frames(): pl.pallas_call(lambda *refs: frame_kernel(chans, *refs), out_shape=[jax.S...  3.14 us
  transfers between devices with their start and end apart: 19, of which 12 were waited for; matrix products, arithmetic and copies ran while one was open for 0% of the time, Pallas kernels for 23%

profile of v3, /device:TPU:0, one launch (start us, length us, event | category | flops | bytes accessed | tf_op | source)
XLA Modules:
  0.0 59.4 jit_solution(14958447365586966506)
XLA Ops:
  0.0 4.0 %collective-permute-start = (s32[1,4,26]{2,1,0:T(4,128)}, s32[1,4,26]{2,1,0:T(4,128)S(1)}, u32[]{:S(2)}, u32[]{:S(2)}) collective-permute-start(s32[1,4,26]{2,1,0:T(4,128)} %bitcast.11), channel_id=1, source_target_pairs={{0,16},{4,20},{8,24},{12,28},{16,0},{20,4},{24,8},{28,12},{1,17},{... | collective-permute-start | bytes 1256 | tf_op jit(solution)/shard_map/ppermute | solution.py:339
  4.0 2.7 %project.1 = (bf16[32,256]{1,0:T(8,128)(2,1)}, bf16[32,256]{1,0:T(8,128)(2,1)}, bf16[32,256]{1,0:T(8,128)(2,1)}, bf16[32,256]{1,0:T(8,128)(2,1)}, bf16[8,128,128...) custom-call(s32[1]{0:T(128)} %bitcast.refs_0_, bf16[128,512]{1,0:T(8,128)(2,1)} %bitcast.8, ...), custom_call_target="tpu_custom_call" | custom-call | tf_op jit(solution)/shard_map/project/pallas_call | solution.py:176
  6.7 0.0 collective-permute-done
  6.7 1.6 %collective-permute-start.1 = (s32[2,4,26]{2,1,0:T(4,128)S(1)}, s32[2,4,26]{2,1,0:T(4,128)S(1)}, u32[]{:S(2)}, u32[]{:S(2)}) collective-permute-start(s32[2,4,26]{2,1,0:T(4,128)S(1)} %pad_add_fusion.1), channel_id=1, source_target_pairs={{0,8},{4,12},{8,0},{12,4},{16,24},{20,28},{24,16},{28,20},{1,9},{5... | collective-permute-start | bytes 2504 | tf_op jit(solution)/shard_map/ppermute | solution.py:339
  8.4 0.0 collective-permute-start.2
  8.4 1.5 %collective-permute-start.3 = (bf16[32,256]{1,0:T(8,128)(2,1)}, bf16[32,256]{1,0:T(8,128)(2,1)S(1)}, u32[]{:S(2)}, u32[]{:S(2)}) collective-permute-start(bf16[32,256]{1,0:T(8,128)(2,1)} %get-tuple-element.47), channel_id=1, source_target_pairs={{0,2},{1,3},{2,0},{3,1},{4,6},{5,7},{6,4},{7,5},{8,10},{9,11},{10,... | collective-permute-start | bytes 49160 | tf_op jit(solution)/shard_map/ppermute | solution.py:339
  9.9 0.3 collective-permute-start.4
  10.2 0.2 collective-permute-done.1
  10.4 0.0 collective-permute-done.2.refs_5_
  10.4 1.6 %collective-permute-start.5 = (s32[4,4,26]{2,1,0:T(4,128)S(1)}, s32[4,4,26]{2,1,0:T(4,128)S(1)}, u32[]{:S(2)}, u32[]{:S(2)}) collective-permute-start(s32[4,4,26]{2,1,0:T(4,128)S(1)} %pad_add_fusion.refs_8_), channel_id=1, source_target_pairs={{0,4},{4,0},{8,12},{12,8},{16,20},{20,16},{24,28},{28,24},{1,5},{5... | collective-permute-start | bytes 5000 | tf_op jit(solution)/shard_map/ppermute | solution.py:339
  12.0 0.3 collective-permute-done.3.refs_6_
  12.3 0.9 %collective-permute-done.4.refs_7_ = bf16[32,256]{1,0:T(8,128)(2,1)S(1)} collective-permute-done((bf16[32,256]{1,0:T(8,128)(2,1)}, bf16[32,256]{1,0:T(8,128)(2,1)S(1)}, u32[]{:S(2)}, u32[]{:S(2)}) %collective-permute-start.4) | collective-permute-done | bytes 16416 | tf_op jit(solution)/shard_map/ppermute | solution.py:339
  13.3 0.9 %collective-permute-done.5.refs_9_ = s32[4,4,26]{2,1,0:T(4,128)S(1)} collective-permute-done((s32[4,4,26]{2,1,0:T(4,128)S(1)}, s32[4,4,26]{2,1,0:T(4,128)S(1)}, u32[]{:S(2)}, u32[]{:S(2)}) %collective-permute-start.5) | collective-permute-done | bytes 1696 | tf_op jit(solution)/shard_map/ppermute | solution.py:339
  14.2 0.6 copy-done.18
  14.7 3.3 %assemble.1 = (bf16[8,80,256]{2,1,0:T(8,128)(2,1)}, s32[1,128]{1,0:T(1,128)}) custom-call(s32[1]{0:T(128)} %bitcast.1.refs_0_.refs_1_, s32[2,26]{1,0:T(2,128)} %refs_1_.1, s32[4]{0:T(128)} %refs_2_.3, s32[2,16,128]{2,1,0:T(8,128)} %constant.20.clone.refs_3_, bf16[32,256]{1,0:T(8,128)(2,1)} %get-tuple-element.43.refs_4_, bf16[32,256]{1,0:T(8,128)(2,1)} %copy-done.15, ...), custom_call_target="tpu_custom_call" | custom-call | flops 1048576 | bytes 12582912 | tf_op jit(solution)/shard_map/assemble/pallas_call | solution.py:316
  18.0 5.2 %all-to-all-start = ((bf16[8,80,256]{2,1,0:T(8,128)(2,1)}), bf16[8,80,256]{2,1,0:T(8,128)(2,1)S(1)}, u32[]{:S(2)}, u32[]{:S(2)}) async-start(bf16[8,80,256]{2,1,0:T(8,128)(2,1)} %get-tuple-element.51), calls=%async_computation | async-start | bytes 655360 | tf_op jit(solution)/shard_map/all_to_all | solution.py:841
  23.2 1.5 %collective-permute-start.7 = (bf16[192,512]{1,0:T(8,128)(2,1)}, bf16[192,512]{1,0:T(8,128)(2,1)S(1)}, u32[]{:S(2)}, u32[]{:S(2)}) collective-permute-start(bf16[192,512]{1,0:T(8,128)(2,1)} %get-tuple-element.59.refs_3_), channel_id=1, source_target_pairs={{0,2},{1,3},{2,0},{3,1},{4,6},{5,7},{6,4},{7,5},{8,10},{9,11},{10,... | collective-permute-start | bytes 589832 | tf_op jit(solution)/shard_map/ppermute | solution.py:339
  24.7 0.0 collective-permute-start.6
  24.7 4.4 %collective-permute-done.7.refs_5_ = bf16[192,512]{1,0:T(8,128)(2,1)S(1)} collective-permute-done((bf16[192,512]{1,0:T(8,128)(2,1)}, bf16[192,512]{1,0:T(8,128)(2,1)S(1)}, u32[]{:S(2)}, u32[]{:S(2)}) %collective-permute-start.7) | collective-permute-done | bytes 196640 | tf_op jit(solution)/shard_map/ppermute | solution.py:339
  29.1 0.0 collective-permute-start.8
  29.1 1.4 %collective-permute-done.8.refs_6_ = bf16[192,512]{1,0:T(8,128)(2,1)S(1)} collective-permute-done((bf16[192,512]{1,0:T(8,128)(2,1)S(1)}, bf16[192,512]{1,0:T(8,128)(2,1)S(1)}, u32[]{:S(2)}, u32[]{:S(2)}) %collective-permute-start.8) | collective-permute-done | bytes 196640 | tf_op jit(solution)/shard_map/ppermute | solution.py:339
  30.5 1.5 %all-to-all-done.refs_1_.refs_5_ = bf16[8,80,256]{2,1,0:T(8,128)(2,1)S(1)} async-done(((bf16[8,80,256]{2,1,0:T(8,128)(2,1)}), bf16[8,80,256]{2,1,0:T(8,128)(2,1)S(1)}, u32[]{:S(2)}, u32[]{:S(2)}) %all-to-all-start) | async-done | bytes 327712 | tf_op jit(solution)/shard_map/all_to_all | solution.py:841
  32.0 0.0 copy-start.12
  32.0 1.4 %collective-permute-start.9 = (bf16[8,32,256]{2,1,0:T(8,128)(2,1)S(1)}, bf16[8,32,256]{2,1,0:T(8,128)(2,1)S(1)}, u32[]{:S(2)}, u32[]{:S(2)}) collective-permute-start(bf16[8,32,256]{2,1,0:T(8,128)(2,1)S(1)} %slice.3.refs_1_), channel_id=1, source_target_pairs={{0,2},{1,3},{2,0},{3,1},{4,6},{5,7},{6,4},{7,5},{8,10},{9,11},{10,... | collective-permute-start | bytes 393224 | tf_op jit(solution)/shard_map/ppermute | solution.py:339
  33.5 2.3 %halo.1.refs_7_ = bf16[4,32,512]{2,1,0:T(8,128)(2,1)} custom-call(s32[1,128]{1,0:T(1,128)} %get-tuple-element.54.refs_0_, bf16[8,80,256]{2,1,0:T(8,128)(2,1)} %copy-done), custom_call_target="tpu_custom_call" | custom-call | tf_op jit(solution)/shard_map/halo/pallas_call | solution.py:410
  35.8 1.3 %collective-permute-done.9.refs_3_ = bf16[8,32,256]{2,1,0:T(8,128)(2,1)S(1)} collective-permute-done((bf16[8,32,256]{2,1,0:T(8,128)(2,1)S(1)}, bf16[8,32,256]{2,1,0:T(8,128)(2,1)S(1)}, u32[]{:S(2)}, u32[]{:S(2)}) %collective-permute-start.9) | collective-permute-done | bytes 131104 | tf_op jit(solution)/shard_map/ppermute | solution.py:339
  37.1 0.5 collective-permute-start.12
  37.6 1.4 %collective-permute-start.10 = (bf16[4,32,512]{2,1,0:T(8,128)(2,1)}, bf16[4,32,512]{2,1,0:T(8,128)(2,1)S(1)}, u32[]{:S(2)}, u32[]{:S(2)}) collective-permute-start(bf16[4,32,512]{2,1,0:T(8,128)(2,1)} %halo.1.refs_7_), channel_id=1, source_target_pairs={{0,2},{1,3},{2,0},{3,1},{4,6},{5,7},{6,4},{7,5},{8,10},{9,11},{10,... | collective-permute-start | bytes 393224 | tf_op jit(solution)/shard_map/ppermute | solution.py:339
  39.0 0.6 %copy-done.20 = bf16[8,32,256]{2,1,0:T(8,128)(2,1)} copy-done((bf16[8,32,256]{2,1,0:T(8,128)(2,1)}, bf16[8,32,256]{2,1,0:T(8,128)(2,1)S(1)}, u32[]{:S(2)}) %copy-start.20) | copy-done | bytes 131096
  39.6 0.1 copy-done.21
  39.7 5.4 %coarse.1.refs_1_ = bf16[1,32,2048]{2,1,0:T(8,128)(2,1)} custom-call(s32[1]{0:T(128)} %bitcast.refs_0_, bf16[8,32,256]{2,1,0:T(8,128)(2,1)} %copy-done.12, bf16[8,32,256]{2,1,0:T(8,128)(2,1)} %copy-done.20, bf16[8,32,256]{2,1,0:T(8,128)(2,1)} %copy-done.19, bf16[8,32,256]{2,1,0:T(8,128)(2,1)} %copy-done.21, bf16[8,80,256]{2,1,0:T(8,128)(2,1)} %copy-done, ...), custom_call_target="tpu_custom_call" | custom-call | flops 452984832 | bytes 2097152 | tf_op jit(solution)/shard_map/coarse/pallas_call | solution.py:531
  45.1 0.0 collective-permute-done.10.refs_9_
  45.1 0.1 collective-permute-start.14
  45.2 0.5 collective-permute-start.15
  45.7 1.0 %collective-permute-start.13 = (bf16[1,32,2048]{2,1,0:T(8,128)(2,1)}, bf16[1,32,2048]{2,1,0:T(8,128)(2,1)S(1)}, u32[]{:S(2)}, u32[]{:S(2)}) collective-permute-start(bf16[1,32,2048]{2,1,0:T(8,128)(2,1)} %coarse.1.refs_1_), channel_id=1, source_target_pairs={{0,2},{1,3},{2,0},{3,1},{4,6},{5,7},{6,4},{7,5},{8,10},{9,11},{10,... | collective-permute-start | bytes 393224 | tf_op jit(solution)/shard_map/ppermute | solution.py:339
  46.7 0.0 collective-permute-done.14.refs_8_
  46.7 0.1 collective-permute-done.15.refs_10_
  46.7 0.6 copy-done.8
  47.3 0.7 %copy-done.9 = bf16[4,32,512]{2,1,0:T(8,128)(2,1)} copy-done((bf16[4,32,512]{2,1,0:T(8,128)(2,1)}, bf16[4,32,512]{2,1,0:T(8,128)(2,1)S(1)}, u32[]{:S(2)}) %copy-start.9) | copy-done | bytes 131096
  48.0 3.1 %frames.1 = (bf16[100,48,128]{2,1,0:T(8,128)(2,1)}, bf16[1,9,48,128]{3,2,1,0:T(8,128)(2,1)}, bf16[8,128,128]{2,1,0:T(8,128)(2,1)}) custom-call(s32[1]{0:T(128)} %bitcast.refs_0_, s32[1]{0:T(128)} %bitcast.1.refs_0_.refs_1_, s32[4,26]{1,0:T(4,128)} %refs_2_.4, bf16[192,512]{1,0:T(8,128)(2,1)} %get-tuple-element.59.refs_3_, bf16[192,512]{1,0:T(8,128)(2,1)} %copy-done.3, ...), custom_call_target="tpu_custom_call" | custom-call | tf_op jit(solution)/shard_map/frames/pallas_call | solution.py:654
  51.1 0.3 collective-permute-done.13.refs_3_
  51.4 0.0 collective-permute-start.16
  51.4 0.5 collective-permute-start.17
  51.9 0.8 %collective-permute-done.16.refs_2_ = bf16[1,32,2048]{2,1,0:T(8,128)(2,1)S(1)} collective-permute-done((bf16[1,32,2048]{2,1,0:T(8,128)(2,1)S(1)}, bf16[1,32,2048]{2,1,0:T(8,128)(2,1)S(1)}, u32[]{:S(2)}, u32[]{:S(2)}) %collective-permute-start.16) | collective-permute-done | bytes 131104 | tf_op jit(solution)/shard_map/ppermute | solution.py:339
  52.7 0.2 collective-permute-done.17.refs_4_
  52.9 0.5 copy-done.10
  53.4 0.2 copy-done.11
  53.6 5.8 %refine.1 = bf16[4,32,512]{2,1,0:T(8,128)(2,1)} custom-call(s32[1]{0:T(128)} %bitcast.refs_0_, bf16[1,32,2048]{2,1,0:T(8,128)(2,1)} %coarse.1.refs_1_, bf16[1,32,2048]{2,1,0:T(8,128)(2,1)} %copy-done.10, bf16[1,32,2048]{2,1,0:T(8,128)(2,1)} %copy-done.7, bf16[1,32,2048]{2,1,0:T(8,128)(2,1)} %copy-done.11, bf16[100,48,128]{2,1,0:T(8,128)(2,1)} %get-tuple-element.70.refs_5_, ...), custom_call_target="tpu_custom_call" | custom-call | flops 452984832 | bytes 4194304 | tf_op jit(solution)/shard_map/refine/pallas_call | solution.py:773
  (43 shorter events, 0.1 us)
Async XLA Ops:
  0.0 6.7 %copy-start.14 = (s32[4,26]{1,0:T(4,128)S(1)}, s32[4,26]{1,0:T(4,128)}, u32[]{:S(2)}) copy-start(s32[4,26]{1,0:T(4,128)} %refs_2_.4) | copy-start | bytes 1252
  0.0 6.7 %collective-permute-start = (s32[1,4,26]{2,1,0:T(4,128)}, s32[1,4,26]{2,1,0:T(4,128)S(1)}, u32[]{:S(2)}, u32[]{:S(2)}) collective-permute-start(s32[1,4,26]{2,1,0:T(4,128)} %bitcast.11), channel_id=1, source_target_pairs={{0,16},{4,20},{8,24},{12,28},{16,0},{20,4},{24,8},{28,12},{1,17},{... | collective-permute-start | bytes 1256 | tf_op jit(solution)/shard_map/ppermute | solution.py:339
  6.7 3.7 %collective-permute-start.1 = (s32[2,4,26]{2,1,0:T(4,128)S(1)}, s32[2,4,26]{2,1,0:T(4,128)S(1)}, u32[]{:S(2)}, u32[]{:S(2)}) collective-permute-start(s32[2,4,26]{2,1,0:T(4,128)S(1)} %pad_add_fusion.1), channel_id=1, source_target_pairs={{0,8},{4,12},{8,0},{12,4},{16,24},{20,28},{24,16},{28,20},{1,9},{5... | collective-permute-start | bytes 2504 | tf_op jit(solution)/shard_map/ppermute | solution.py:339
  8.4 2.0 %collective-permute-start.2 = (bf16[32,256]{1,0:T(8,128)(2,1)}, bf16[32,256]{1,0:T(8,128)(2,1)S(1)}, u32[]{:S(2)}, u32[]{:S(2)}) collective-permute-start(bf16[32,256]{1,0:T(8,128)(2,1)} %get-tuple-element.45), channel_id=1, source_target_pairs={{0,1},{1,0},{2,3},{3,2},{4,5},{5,4},{6,7},{7,6},{8,9},{9,8},{10,11... | collective-permute-start | bytes 49160 | tf_op jit(solution)/shard_map/ppermute | solution.py:339
  8.4 3.9 %collective-permute-start.3 = (bf16[32,256]{1,0:T(8,128)(2,1)}, bf16[32,256]{1,0:T(8,128)(2,1)S(1)}, u32[]{:S(2)}, u32[]{:S(2)}) collective-permute-start(bf16[32,256]{1,0:T(8,128)(2,1)} %get-tuple-element.47), channel_id=1, source_target_pairs={{0,2},{1,3},{2,0},{3,1},{4,6},{5,7},{6,4},{7,5},{8,10},{9,11},{10,... | collective-permute-start | bytes 49160 | tf_op jit(solution)/shard_map/ppermute | solution.py:339
  9.9 3.4 %collective-permute-start.4 = (bf16[32,256]{1,0:T(8,128)(2,1)}, bf16[32,256]{1,0:T(8,128)(2,1)S(1)}, u32[]{:S(2)}, u32[]{:S(2)}) collective-permute-start(bf16[32,256]{1,0:T(8,128)(2,1)} %get-tuple-element.48), channel_id=1, source_target_pairs={{0,3},{1,2},{2,1},{3,0},{4,7},{5,6},{6,5},{7,4},{8,11},{9,10},{10,... | collective-permute-start | bytes 49160 | tf_op jit(solution)/shard_map/ppermute | solution.py:339
  10.4 3.7 %copy-start.13 = (s32[4,4,26]{2,1,0:T(4,128)}, s32[4,4,26]{2,1,0:T(4,128)S(1)}, u32[]{:S(2)}) copy-start(s32[4,4,26]{2,1,0:T(4,128)S(1)} %pad_add_fusion.refs_8_) | copy-start | bytes 4996
  10.4 3.7 %copy-start.15 = (bf16[32,256]{1,0:T(8,128)(2,1)}, bf16[32,256]{1,0:T(8,128)(2,1)S(1)}, u32[]{:S(2)}) copy-start(bf16[32,256]{1,0:T(8,128)(2,1)S(1)} %collective-permute-done.2.refs_5_) | copy-start | bytes 49156
  10.4 3.7 %collective-permute-start.5 = (s32[4,4,26]{2,1,0:T(4,128)S(1)}, s32[4,4,26]{2,1,0:T(4,128)S(1)}, u32[]{:S(2)}, u32[]{:S(2)}) collective-permute-start(s32[4,4,26]{2,1,0:T(4,128)S(1)} %pad_add_fusion.refs_8_), channel_id=1, source_target_pairs={{0,4},{4,0},{8,12},{12,8},{16,20},{20,16},{24,28},{28,24},{1,5},{5... | collective-permute-start | bytes 5000 | tf_op jit(solution)/shard_map/ppermute | solution.py:339
  12.3 1.8 %copy-start.16 = (bf16[32,256]{1,0:T(8,128)(2,1)}, bf16[32,256]{1,0:T(8,128)(2,1)S(1)}, u32[]{:S(2)}) copy-start(bf16[32,256]{1,0:T(8,128)(2,1)S(1)} %collective-permute-done.3.refs_6_) | copy-start | bytes 49156
  13.3 0.9 %copy-start.17 = (bf16[32,256]{1,0:T(8,128)(2,1)}, bf16[32,256]{1,0:T(8,128)(2,1)S(1)}, u32[]{:S(2)}) copy-start(bf16[32,256]{1,0:T(8,128)(2,1)S(1)} %collective-permute-done.4.refs_7_) | copy-start | bytes 49156
  14.1 0.6 %copy-start.18 = (s32[4,4,26]{2,1,0:T(4,128)}, s32[4,4,26]{2,1,0:T(4,128)S(1)}, u32[]{:S(2)}) copy-start(s32[4,4,26]{2,1,0:T(4,128)S(1)} %collective-permute-done.5.refs_9_) | copy-start | bytes 4996
  18.0 14.0 %all-to-all-start = ((bf16[8,80,256]{2,1,0:T(8,128)(2,1)}), bf16[8,80,256]{2,1,0:T(8,128)(2,1)S(1)}, u32[]{:S(2)}, u32[]{:S(2)}) async-start(bf16[8,80,256]{2,1,0:T(8,128)(2,1)} %get-tuple-element.51), calls=%async_computation | async-start | bytes 655360 | tf_op jit(solution)/shard_map/all_to_all | solution.py:841
  23.2 5.9 %collective-permute-start.7 = (bf16[192,512]{1,0:T(8,128)(2,1)}, bf16[192,512]{1,0:T(8,128)(2,1)S(1)}, u32[]{:S(2)}, u32[]{:S(2)}) collective-permute-start(bf16[192,512]{1,0:T(8,128)(2,1)} %get-tuple-element.59.refs_3_), channel_id=1, source_target_pairs={{0,2},{1,3},{2,0},{3,1},{4,6},{5,7},{6,4},{7,5},{8,10},{9,11},{10,... | collective-permute-start | bytes 589832 | tf_op jit(solution)/shard_map/ppermute | solution.py:339
  24.7 4.4 %collective-permute-start.6 = (bf16[192,512]{1,0:T(8,128)(2,1)}, bf16[192,512]{1,0:T(8,128)(2,1)S(1)}, u32[]{:S(2)}, u32[]{:S(2)}) collective-permute-start(bf16[192,512]{1,0:T(8,128)(2,1)} %get-tuple-element.59.refs_3_), channel_id=1, source_target_pairs={{0,1},{1,0},{2,3},{3,2},{4,5},{5,4},{6,7},{7,6},{8,9},{9,8},{10,11... | collective-permute-start | bytes 589832 | tf_op jit(solution)/shard_map/ppermute | solution.py:339
  29.1 17.6 %copy-start.2 = (bf16[192,512]{1,0:T(8,128)(2,1)}, bf16[192,512]{1,0:T(8,128)(2,1)S(1)}, u32[]{:S(2)}) copy-start(bf16[192,512]{1,0:T(8,128)(2,1)S(1)} %collective-permute-done.7.refs_5_) | copy-start | bytes 589828
  29.1 1.4 %collective-permute-start.8 = (bf16[192,512]{1,0:T(8,128)(2,1)S(1)}, bf16[192,512]{1,0:T(8,128)(2,1)S(1)}, u32[]{:S(2)}, u32[]{:S(2)}) collective-permute-start(bf16[192,512]{1,0:T(8,128)(2,1)S(1)} %collective-permute-done.7.refs_5_), channel_id=1, source_target_pairs={{0,1},{1,0},{2,3},{3,2},{4,5},{5,4},{6,7},{7,6},{8,9},{9,8},{10,11... | collective-permute-start | bytes 589832 | tf_op jit(solution)/shard_map/ppermute | solution.py:339
  29.1 17.6 %copy-start.3 = (bf16[192,512]{1,0:T(8,128)(2,1)}, bf16[192,512]{1,0:T(8,128)(2,1)S(1)}, u32[]{:S(2)}) copy-start(bf16[192,512]{1,0:T(8,128)(2,1)S(1)} %collective-permute-done.6.refs_4_) | copy-start | bytes 589828
  30.5 16.2 %copy-start.4 = (bf16[192,512]{1,0:T(8,128)(2,1)}, bf16[192,512]{1,0:T(8,128)(2,1)S(1)}, u32[]{:S(2)}) copy-start(bf16[192,512]{1,0:T(8,128)(2,1)S(1)} %collective-permute-done.8.refs_6_) | copy-start | bytes 589828
  32.0 1.5 %copy-start = (bf16[8,80,256]{2,1,0:T(8,128)(2,1)}, bf16[8,80,256]{2,1,0:T(8,128)(2,1)S(1)}, u32[]{:S(2)}) copy-start(bf16[8,80,256]{2,1,0:T(8,128)(2,1)S(1)} %all-to-all-done.refs_1_.refs_5_) | copy-start | bytes 983044
  32.0 6.9 %copy-start.12 = (bf16[8,32,256]{2,1,0:T(8,128)(2,1)}, bf16[8,32,256]{2,1,0:T(8,128)(2,1)S(1)}, u32[]{:S(2)}) copy-start(bf16[8,32,256]{2,1,0:T(8,128)(2,1)S(1)} %slice.3.refs_1_) | copy-start | bytes 393220
  32.0 5.0 %collective-permute-start.9 = (bf16[8,32,256]{2,1,0:T(8,128)(2,1)S(1)}, bf16[8,32,256]{2,1,0:T(8,128)(2,1)S(1)}, u32[]{:S(2)}, u32[]{:S(2)}) collective-permute-start(bf16[8,32,256]{2,1,0:T(8,128)(2,1)S(1)} %slice.3.refs_1_), channel_id=1, source_target_pairs={{0,2},{1,3},{2,0},{3,1},{4,6},{5,7},{6,4},{7,5},{8,10},{9,11},{10,... | collective-permute-start | bytes 393224 | tf_op jit(solution)/shard_map/ppermute | solution.py:339
  35.8 9.3 %copy-start.1 = (bf16[4,32,512]{2,1,0:T(8,128)(2,1)S(1)}, bf16[4,32,512]{2,1,0:T(8,128)(2,1)}, u32[]{:S(2)}) copy-start(bf16[4,32,512]{2,1,0:T(8,128)(2,1)} %halo.1.refs_7_) | copy-start | bytes 393220
  37.1 1.9 %copy-start.19 = (bf16[8,32,256]{2,1,0:T(8,128)(2,1)}, bf16[8,32,256]{2,1,0:T(8,128)(2,1)S(1)}, u32[]{:S(2)}) copy-start(bf16[8,32,256]{2,1,0:T(8,128)(2,1)S(1)} %collective-permute-done.9.refs_3_) | copy-start | bytes 393220
  37.1 1.9 %collective-permute-start.11 = (bf16[8,32,256]{2,1,0:T(8,128)(2,1)S(1)}, bf16[8,32,256]{2,1,0:T(8,128)(2,1)S(1)}, u32[]{:S(2)}, u32[]{:S(2)}) collective-permute-start(bf16[8,32,256]{2,1,0:T(8,128)(2,1)S(1)} %slice.3.refs_1_), channel_id=1, source_target_pairs={{0,1},{1,0},{2,3},{3,2},{4,5},{5,4},{6,7},{7,6},{8,9},{9,8},{10,11... | collective-permute-start | bytes 393224 | tf_op jit(solution)/shard_map/ppermute | solution.py:339
  37.1 1.9 %collective-permute-start.12 = (bf16[8,32,256]{2,1,0:T(8,128)(2,1)S(1)}, bf16[8,32,256]{2,1,0:T(8,128)(2,1)S(1)}, u32[]{:S(2)}, u32[]{:S(2)}) collective-permute-start(bf16[8,32,256]{2,1,0:T(8,128)(2,1)S(1)} %collective-permute-done.9.refs_3_), channel_id=1, source_target_pairs={{0,1},{1,0},{2,3},{3,2},{4,5},{5,4},{6,7},{7,6},{8,9},{9,8},{10,11... | collective-permute-start | bytes 393224 | tf_op jit(solution)/shard_map/ppermute | solution.py:339
  37.6 7.5 %collective-permute-start.10 = (bf16[4,32,512]{2,1,0:T(8,128)(2,1)}, bf16[4,32,512]{2,1,0:T(8,128)(2,1)S(1)}, u32[]{:S(2)}, u32[]{:S(2)}) collective-permute-start(bf16[4,32,512]{2,1,0:T(8,128)(2,1)} %halo.1.refs_7_), channel_id=1, source_target_pairs={{0,2},{1,3},{2,0},{3,1},{4,6},{5,7},{6,4},{7,5},{8,10},{9,11},{10,... | collective-permute-start | bytes 393224 | tf_op jit(solution)/shard_map/ppermute | solution.py:339
  39.0 0.7 %copy-start.20 = (bf16[8,32,256]{2,1,0:T(8,128)(2,1)}, bf16[8,32,256]{2,1,0:T(8,128)(2,1)S(1)}, u32[]{:S(2)}) copy-start(bf16[8,32,256]{2,1,0:T(8,128)(2,1)S(1)} %collective-permute-done.11.refs_2_) | copy-start | bytes 393220
  39.0 0.7 %copy-start.21 = (bf16[8,32,256]{2,1,0:T(8,128)(2,1)}, bf16[8,32,256]{2,1,0:T(8,128)(2,1)S(1)}, u32[]{:S(2)}) copy-start(bf16[8,32,256]{2,1,0:T(8,128)(2,1)S(1)} %collective-permute-done.12.refs_4_) | copy-start | bytes 393220
  45.1 6.3 %copy-start.5 = (bf16[1,32,2048]{2,1,0:T(8,128)(2,1)S(1)}, bf16[1,32,2048]{2,1,0:T(8,128)(2,1)}, u32[]{:S(2)}) copy-start(bf16[1,32,2048]{2,1,0:T(8,128)(2,1)} %coarse.1.refs_1_) | copy-start | bytes 393220
  45.1 1.6 %copy-start.6 = (bf16[4,32,512]{2,1,0:T(8,128)(2,1)}, bf16[4,32,512]{2,1,0:T(8,128)(2,1)S(1)}, u32[]{:S(2)}) copy-start(bf16[4,32,512]{2,1,0:T(8,128)(2,1)S(1)} %collective-permute-done.10.refs_9_) | copy-start | bytes 393220
  45.1 1.5 %collective-permute-start.14 = (bf16[4,32,512]{2,1,0:T(8,128)(2,1)S(1)}, bf16[4,32,512]{2,1,0:T(8,128)(2,1)S(1)}, u32[]{:S(2)}, u32[]{:S(2)}) collective-permute-start(bf16[4,32,512]{2,1,0:T(8,128)(2,1)S(1)} %copy-done.1), channel_id=1, source_target_pairs={{0,1},{1,0},{2,3},{3,2},{4,5},{5,4},{6,7},{7,6},{8,9},{9,8},{10,11... | collective-permute-start | bytes 393224 | tf_op jit(solution)/shard_map/ppermute | solution.py:339
  45.2 1.5 %collective-permute-start.15 = (bf16[4,32,512]{2,1,0:T(8,128)(2,1)S(1)}, bf16[4,32,512]{2,1,0:T(8,128)(2,1)S(1)}, u32[]{:S(2)}, u32[]{:S(2)}) collective-permute-start(bf16[4,32,512]{2,1,0:T(8,128)(2,1)S(1)} %collective-permute-done.10.refs_9_), channel_id=1, source_target_pairs={{0,1},{1,0},{2,3},{3,2},{4,5},{5,4},{6,7},{7,6},{8,9},{9,8},{10,11... | collective-permute-start | bytes 393224 | tf_op jit(solution)/shard_map/ppermute | solution.py:339
  45.7 5.7 %collective-permute-start.13 = (bf16[1,32,2048]{2,1,0:T(8,128)(2,1)}, bf16[1,32,2048]{2,1,0:T(8,128)(2,1)S(1)}, u32[]{:S(2)}, u32[]{:S(2)}) collective-permute-start(bf16[1,32,2048]{2,1,0:T(8,128)(2,1)} %coarse.1.refs_1_), channel_id=1, source_target_pairs={{0,2},{1,3},{2,0},{3,1},{4,6},{5,7},{6,4},{7,5},{8,10},{9,11},{10,... | collective-permute-start | bytes 393224 | tf_op jit(solution)/shard_map/ppermute | solution.py:339
  46.7 0.7 %copy-start.8 = (bf16[4,32,512]{2,1,0:T(8,128)(2,1)}, bf16[4,32,512]{2,1,0:T(8,128)(2,1)S(1)}, u32[]{:S(2)}) copy-start(bf16[4,32,512]{2,1,0:T(8,128)(2,1)S(1)} %collective-permute-done.14.refs_8_) | copy-start | bytes 393220
  47.3 0.7 %copy-start.9 = (bf16[4,32,512]{2,1,0:T(8,128)(2,1)}, bf16[4,32,512]{2,1,0:T(8,128)(2,1)S(1)}, u32[]{:S(2)}) copy-start(bf16[4,32,512]{2,1,0:T(8,128)(2,1)S(1)} %collective-permute-done.15.refs_10_) | copy-start | bytes 393220
  51.4 1.5 %copy-start.7 = (bf16[1,32,2048]{2,1,0:T(8,128)(2,1)}, bf16[1,32,2048]{2,1,0:T(8,128)(2,1)S(1)}, u32[]{:S(2)}) copy-start(bf16[1,32,2048]{2,1,0:T(8,128)(2,1)S(1)} %collective-permute-done.13.refs_3_) | copy-start | bytes 393220
  51.4 1.3 %collective-permute-start.16 = (bf16[1,32,2048]{2,1,0:T(8,128)(2,1)S(1)}, bf16[1,32,2048]{2,1,0:T(8,128)(2,1)S(1)}, u32[]{:S(2)}, u32[]{:S(2)}) collective-permute-start(bf16[1,32,2048]{2,1,0:T(8,128)(2,1)S(1)} %copy-done.5), channel_id=1, source_target_pairs={{0,1},{1,0},{2,3},{3,2},{4,5},{5,4},{6,7},{7,6},{8,9},{9,8},{10,11... | collective-permute-start | bytes 393224 | tf_op jit(solution)/shard_map/ppermute | solution.py:339
  51.4 1.5 %collective-permute-start.17 = (bf16[1,32,2048]{2,1,0:T(8,128)(2,1)S(1)}, bf16[1,32,2048]{2,1,0:T(8,128)(2,1)S(1)}, u32[]{:S(2)}, u32[]{:S(2)}) collective-permute-start(bf16[1,32,2048]{2,1,0:T(8,128)(2,1)S(1)} %collective-permute-done.13.refs_3_), channel_id=1, source_target_pairs={{0,1},{1,0},{2,3},{3,2},{4,5},{5,4},{6,7},{7,6},{8,9},{9,8},{10,11... | collective-permute-start | bytes 393224 | tf_op jit(solution)/shard_map/ppermute | solution.py:339
  52.7 0.6 %copy-start.10 = (bf16[1,32,2048]{2,1,0:T(8,128)(2,1)}, bf16[1,32,2048]{2,1,0:T(8,128)(2,1)S(1)}, u32[]{:S(2)}) copy-start(bf16[1,32,2048]{2,1,0:T(8,128)(2,1)S(1)} %collective-permute-done.16.refs_2_) | copy-start | bytes 393220
  52.9 0.7 %copy-start.11 = (bf16[1,32,2048]{2,1,0:T(8,128)(2,1)}, bf16[1,32,2048]{2,1,0:T(8,128)(2,1)S(1)}, u32[]{:S(2)}) copy-start(bf16[1,32,2048]{2,1,0:T(8,128)(2,1)S(1)} %collective-permute-done.17.refs_4_) | copy-start | bytes 393220

commit v4 on v3

--- a/solution.py
+++ b/solution.py
@@ -14,7 +14,7 @@
 F32 = jnp.float32
 BF16 = jnp.bfloat16
 META = 96
-VMEM_LIMIT = 56 * 1024 * 1024
+MIB = 1024 * 1024
 
 
 def headings():
@@ -117,7 +117,7 @@
 
 
 def params():
-    return pltpu.CompilerParams(vmem_limit_bytes=VMEM_LIMIT)
+    return pltpu.CompilerParams(vmem_limit_bytes=min(56, 12 + lax.axis_size("brick")) * MIB)
 
 
 def cost(flops, moved):
@@ -247,8 +247,7 @@
                 pos = r * FACE if r < faces else faces * FACE + (r - faces) * EDGE
                 if pos // 128 != block:
                     continue
-                v = scalars[r_owner, r]
-                safe = jnp.maximum(v, 0)
+                safe = jnp.maximum(scalars[r_owner, r], 0)
                 b = lax.shift_right_logical(safe, 10)
                 chunk = lax.shift_right_logical(safe, 7) & 7
                 got = chunk_ref[chunk, pl.ds(pl.multiple_of(b * q, q), q), :].astype(F32)
@@ -257,7 +256,7 @@
                 if r >= faces:
                     got = pltpu.roll(got, (first + 128 - (safe & 127)) & 127, 1)
                     size = EDGE
-                here = jnp.where((side >= first) & (side < first + size) & (v >= 0), got, here)
+                here = jnp.where((side >= first) & (side < first + size), got, here)
             at = q + block * half
             for i in range(2):
                 part = here[i * half : (i + 1) * half]

time: 59.8 us -> 55 us (0.920)
  Pallas kernels: 22.6 us -> 13.4 us
  waiting for transfers between devices: 12.3 us -> 17.1 us
  starting transfers between devices: 21.1 us -> 20.1 us
  local copies, waits for them, and re-layouts: 3.21 us -> 3.92 us
    ppermute x18, waiting for transfers between devices: 10.8 us -> 14.8 us  [partner(): return lax.ppermute(x, axis, [(i, i ^ step) for i in range(count)])]
    pallas_call x1, Pallas kernels: 2.66 us -> 0.66 us  [project(): pl.pallas_call(lambda *refs: project_kernel(chans, *refs), out_shape=[jax...]
    pallas_call x1, Pallas kernels: 3.14 us -> 1.19 us  [frames(): pl.pallas_call(lambda *refs: frame_kernel(chans, *refs), out_shape=[jax.S...]
    pallas_call x1, Pallas kernels: 5.42 us -> 3.55 us  [coarse(): pl.pallas_call(lambda *refs: coarse_kernel(chans, codes, *refs), out_shap...]
    pallas_call x1, Pallas kernels: 5.84 us -> 4.13 us  [refine(): pl.pallas_call(lambda *refs: fine_kernel(chans, *refs), out_shape=jax.Sha...]
    all_to_all x1, starting transfers between devices: 5.19 us -> 3.79 us  [per_device(): lax.all_to_all(sending, 'brick', split_axis=0, concat_axis=0, tiled=True)]
    pallas_call x1, Pallas kernels: 2.3 us -> 1.21 us  [halo(): pl.pallas_call(lambda *refs: halo_kernel(q, base, *refs), out_shape=jax.S...]
    all_to_all x1, waiting for transfers between devices: 1.49 us -> 2.35 us  [per_device(): lax.all_to_all(sending, 'brick', split_axis=0, concat_axis=0, tiled=True)]
  transfers between devices with their start and end apart: 19 -> 19, of which waited for: 12 -> 12; matrix products, arithmetic and copies ran while one was open for 0% -> 0% of each run, Pallas kernels for 23% -> 12%
where the time goes in v4:
time: 55 us; the launch traced here: 54.6 us
  starting transfers between devices  20.1 us (37%)
  waiting for transfers between devices  17.1 us (31%)
  Pallas kernels  13.4 us (24%)
  local copies, waits for them, and re-layouts  3.92 us (7%)
    ppermute x18, starting transfers between devices, partner(): return lax.ppermute(x, axis, [(i, i ^ step) for i in range(count)])  16.3 us
    ppermute x18, waiting for transfers between devices, partner(): return lax.ppermute(x, axis, [(i, i ^ step) for i in range(count)])  14.8 us
    pallas_call x1, Pallas kernels, refine(): pl.pallas_call(lambda *refs: fine_kernel(chans, *refs), out_shape=jax.Sha...  4.13 us
    unnamed x30, local copies, waits for them, and re-layouts  3.91 us
    all_to_all x1, starting transfers between devices, per_device(): lax.all_to_all(sending, 'brick', split_axis=0, concat_axis=0, tiled=True)  3.79 us
    pallas_call x1, Pallas kernels, coarse(): pl.pallas_call(lambda *refs: coarse_kernel(chans, codes, *refs), out_shap...  3.55 us
    pallas_call x1, Pallas kernels, assemble(): pl.pallas_call(lambda *refs: assemble_kernel(len(slots), len(asked), fine...  2.63 us
    all_to_all x1, waiting for transfers between devices, per_device(): lax.all_to_all(sending, 'brick', split_axis=0, concat_axis=0, tiled=True)  2.35 us
  transfers between devices with their start and end apart: 19, of which 12 were waited for; matrix products, arithmetic and copies ran while one was open for 0% of the time, Pallas kernels for 12%

profile of v4, /device:TPU:0, one launch (start us, length us, event | category | flops | bytes accessed | tf_op | source)
XLA Modules:
  0.0 54.6 jit_solution(7860372697532046567)
XLA Ops:
  0.0 4.1 %collective-permute-start = (s32[1,4,26]{2,1,0:T(4,128)}, s32[1,4,26]{2,1,0:T(4,128)S(1)}, u32[]{:S(2)}, u32[]{:S(2)}) collective-permute-start(s32[1,4,26]{2,1,0:T(4,128)} %bitcast.11), channel_id=1, source_target_pairs={{0,16},{4,20},{8,24},{12,28},{16,0},{20,4},{24,8},{28,12},{1,17},{... | collective-permute-start | bytes 1256 | tf_op jit(solution)/shard_map/ppermute | solution.py:338
  4.1 1.3 %copy-done = bf16[512,1152]{1,0:T(8,128)(2,1)S(1)} copy-done((bf16[512,1152]{1,0:T(8,128)(2,1)S(1)}, bf16[512,1152]{1,0:T(8,128)(2,1)}, u32[]{:S(2)}) %copy-start) | copy-done | bytes 1179672
  5.4 0.9 %copy-done.3 = bf16[4,32,512]{2,1,0:T(8,128)(2,1)S(1)} copy-done((bf16[4,32,512]{2,1,0:T(8,128)(2,1)S(1)}, bf16[4,32,512]{2,1,0:T(8,128)(2,1)}, u32[]{:S(2)}) %copy-start.3) | copy-done | bytes 131096
  6.3 0.8 %copy-done.4 = bf16[8,128,32]{1,2,0:T(8,128)(2,1)S(1)} copy-done((bf16[8,128,32]{1,2,0:T(8,128)(2,1)S(1)}, bf16[8,128,32]{1,2,0:T(8,128)(2,1)}, u32[]{:S(2)}) %copy-start.4) | copy-done | bytes 65560
  7.1 0.8 %copy-done.5 = bf16[8,32,128]{2,1,0:T(8,128)(2,1)S(1)} copy-done((bf16[8,32,128]{2,1,0:T(8,128)(2,1)S(1)}, bf16[8,32,128]{2,1,0:T(8,128)(2,1)}, u32[]{:S(2)}) %copy-start.5) | copy-done | bytes 65560
  8.0 0.7 %project.1 = (bf16[32,256]{1,0:T(8,128)(2,1)S(1)}, bf16[32,256]{1,0:T(8,128)(2,1)S(1)}, bf16[32,256]{1,0:T(8,128)(2,1)S(1)}, bf16[32,256]{1,0:T(8,128)(2,1)S(1)}...) custom-call(s32[1]{0:T(128)} %bitcast.refs_0_, bf16[128,512]{1,0:T(8,128)(2,1)S(1)} %bitcast.8, ...), custom_call_target="tpu_custom_call" | custom-call | tf_op jit(solution)/shard_map/project/pallas_call | solution.py:176
  8.7 0.0 copy-start.13
  8.7 0.0 copy-start.14
  8.7 1.6 %collective-permute-start.1 = (s32[2,4,26]{2,1,0:T(4,128)S(1)}, s32[2,4,26]{2,1,0:T(4,128)S(1)}, u32[]{:S(2)}, u32[]{:S(2)}) collective-permute-start(s32[2,4,26]{2,1,0:T(4,128)S(1)} %pad_add_fusion.1), channel_id=1, source_target_pairs={{0,8},{4,12},{8,0},{12,4},{16,24},{20,28},{24,16},{28,20},{1,9},{5... | collective-permute-start | bytes 2504 | tf_op jit(solution)/shard_map/ppermute | solution.py:338
  10.4 0.0 collective-permute-start.2
  10.4 1.5 %collective-permute-start.3 = (bf16[32,256]{1,0:T(8,128)(2,1)S(1)}, bf16[32,256]{1,0:T(8,128)(2,1)S(1)}, u32[]{:S(2)}, u32[]{:S(2)}) collective-permute-start(bf16[32,256]{1,0:T(8,128)(2,1)S(1)} %get-tuple-element.47), channel_id=1, source_target_pairs={{0,2},{1,3},{2,0},{3,1},{4,6},{5,7},{6,4},{7,5},{8,10},{9,11},{10,... | collective-permute-start | bytes 49160 | tf_op jit(solution)/shard_map/ppermute | solution.py:338
  11.9 0.3 collective-permute-start.4
  12.2 0.2 collective-permute-done.1
  12.4 1.6 %collective-permute-start.5 = (s32[4,4,26]{2,1,0:T(4,128)S(1)}, s32[4,4,26]{2,1,0:T(4,128)S(1)}, u32[]{:S(2)}, u32[]{:S(2)}) collective-permute-start(s32[4,4,26]{2,1,0:T(4,128)S(1)} %pad_add_fusion.refs_8_), channel_id=1, source_target_pairs={{0,4},{4,0},{8,12},{12,8},{16,20},{20,16},{24,28},{28,24},{1,5},{5... | collective-permute-start | bytes 5000 | tf_op jit(solution)/shard_map/ppermute | solution.py:338
  14.0 0.1 collective-permute-done.3.refs_6_
  14.1 0.9 %collective-permute-done.4.refs_7_ = bf16[32,256]{1,0:T(8,128)(2,1)S(1)} collective-permute-done((bf16[32,256]{1,0:T(8,128)(2,1)S(1)}, bf16[32,256]{1,0:T(8,128)(2,1)S(1)}, u32[]{:S(2)}, u32[]{:S(2)}) %collective-permute-start.4) | collective-permute-done | bytes 16416 | tf_op jit(solution)/shard_map/ppermute | solution.py:338
  15.0 1.1 %collective-permute-done.5.refs_9_ = s32[4,4,26]{2,1,0:T(4,128)S(1)} collective-permute-done((s32[4,4,26]{2,1,0:T(4,128)S(1)}, s32[4,4,26]{2,1,0:T(4,128)S(1)}, u32[]{:S(2)}, u32[]{:S(2)}) %collective-permute-start.5) | collective-permute-done | bytes 1696 | tf_op jit(solution)/shard_map/ppermute | solution.py:338
  16.1 2.6 %assemble.1 = (bf16[8,80,256]{2,1,0:T(8,128)(2,1)}, s32[1,128]{1,0:T(1,128)S(1)}) custom-call(s32[1]{0:T(128)} %bitcast.1.refs_0_.refs_1_, s32[2,26]{1,0:T(2,128)S(1)} %copy-done.9, s32[4]{0:T(128)S(1)} %copy-done.11, s32[2,16,128]{2,1,0:T(8,128)S(1)} %copy-done.8, bf16[32,256]{1,0:T(8,128)(2,1)S(1)} %get-tuple-element.43.refs_4_, ...), custom_call_target="tpu_custom_call" | custom-call | flops 1048576 | bytes 12582912 | tf_op jit(solution)/shard_map/assemble/pallas_call | solution.py:315
  18.8 3.8 %all-to-all-start = ((bf16[8,80,256]{2,1,0:T(8,128)(2,1)}), bf16[8,80,256]{2,1,0:T(8,128)(2,1)S(1)}, u32[]{:S(2)}, u32[]{:S(2)}) async-start(bf16[8,80,256]{2,1,0:T(8,128)(2,1)} %get-tuple-element.51), calls=%async_computation | async-start | bytes 655360 | tf_op jit(solution)/shard_map/all_to_all | solution.py:840
  22.6 1.5 %collective-permute-start.7 = (bf16[192,512]{1,0:T(8,128)(2,1)S(1)}, bf16[192,512]{1,0:T(8,128)(2,1)S(1)}, u32[]{:S(2)}, u32[]{:S(2)}) collective-permute-start(bf16[192,512]{1,0:T(8,128)(2,1)S(1)} %get-tuple-element.59.refs_3_), channel_id=1, source_target_pairs={{0,2},{1,3},{2,0},{3,1},{4,6},{5,7},{6,4},{7,5},{8,10},{9,11},{10,... | collective-permute-start | bytes 589832 | tf_op jit(solution)/shard_map/ppermute | solution.py:338
  24.1 0.0 collective-permute-start.6
  24.1 4.2 %collective-permute-done.7.refs_5_ = bf16[192,512]{1,0:T(8,128)(2,1)S(1)} collective-permute-done((bf16[192,512]{1,0:T(8,128)(2,1)S(1)}, bf16[192,512]{1,0:T(8,128)(2,1)S(1)}, u32[]{:S(2)}, u32[]{:S(2)}) %collective-permute-start.7) | collective-permute-done | bytes 196640 | tf_op jit(solution)/shard_map/ppermute | solution.py:338
  28.3 0.0 collective-permute-start.8
  28.3 0.0 collective-permute-done.6.refs_4_
  28.3 1.4 %collective-permute-done.8.refs_6_ = bf16[192,512]{1,0:T(8,128)(2,1)S(1)} collective-permute-done((bf16[192,512]{1,0:T(8,128)(2,1)S(1)}, bf16[192,512]{1,0:T(8,128)(2,1)S(1)}, u32[]{:S(2)}, u32[]{:S(2)}) %collective-permute-start.8) | collective-permute-done | bytes 196640 | tf_op jit(solution)/shard_map/ppermute | solution.py:338
  29.7 2.4 %all-to-all-done.refs_1_.refs_5_ = bf16[8,80,256]{2,1,0:T(8,128)(2,1)S(1)} async-done(((bf16[8,80,256]{2,1,0:T(8,128)(2,1)}), bf16[8,80,256]{2,1,0:T(8,128)(2,1)S(1)}, u32[]{:S(2)}, u32[]{:S(2)}) %all-to-all-start) | async-done | bytes 327712 | tf_op jit(solution)/shard_map/all_to_all | solution.py:840
  32.1 1.4 %collective-permute-start.9 = (bf16[8,32,256]{2,1,0:T(8,128)(2,1)S(1)}, bf16[8,32,256]{2,1,0:T(8,128)(2,1)S(1)}, u32[]{:S(2)}, u32[]{:S(2)}) collective-permute-start(bf16[8,32,256]{2,1,0:T(8,128)(2,1)S(1)} %slice.3.refs_1_), channel_id=1, source_target_pairs={{0,2},{1,3},{2,0},{3,1},{4,6},{5,7},{6,4},{7,5},{8,10},{9,11},{10,... | collective-permute-start | bytes 393224 | tf_op jit(solution)/shard_map/ppermute | solution.py:338
  33.5 1.2 %halo.1.refs_7_ = bf16[4,32,512]{2,1,0:T(8,128)(2,1)S(1)} custom-call(s32[1,128]{1,0:T(1,128)S(1)} %get-tuple-element.54.refs_0_, bf16[8,80,256]{2,1,0:T(8,128)(2,1)S(1)} %all-to-all-done.refs_1_.refs_5_), custom_call_target="tpu_custom_call" | custom-call | tf_op jit(solution)/shard_map/halo/pallas_call | solution.py:409
  34.7 2.4 %collective-permute-done.9.refs_3_ = bf16[8,32,256]{2,1,0:T(8,128)(2,1)S(1)} collective-permute-done((bf16[8,32,256]{2,1,0:T(8,128)(2,1)S(1)}, bf16[8,32,256]{2,1,0:T(8,128)(2,1)S(1)}, u32[]{:S(2)}, u32[]{:S(2)}) %collective-permute-start.9) | collective-permute-done | bytes 131104 | tf_op jit(solution)/shard_map/ppermute | solution.py:338
  37.1 0.0 collective-permute-start.11
  37.1 0.5 collective-permute-start.12
  37.6 1.3 %collective-permute-start.10 = (bf16[4,32,512]{2,1,0:T(8,128)(2,1)S(1)}, bf16[4,32,512]{2,1,0:T(8,128)(2,1)S(1)}, u32[]{:S(2)}, u32[]{:S(2)}) collective-permute-start(bf16[4,32,512]{2,1,0:T(8,128)(2,1)S(1)} %halo.1.refs_7_), channel_id=1, source_target_pairs={{0,2},{1,3},{2,0},{3,1},{4,6},{5,7},{6,4},{7,5},{8,10},{9,11},{10,... | collective-permute-start | bytes 393224 | tf_op jit(solution)/shard_map/ppermute | solution.py:338
  39.0 0.0 collective-permute-done.11.refs_2_
  39.0 0.0 collective-permute-done.12.refs_4_
  39.0 0.0 copy-start.1
  39.0 0.0 copy-start.2
  39.0 0.0 copy-start.12
  39.0 3.6 %coarse.1.refs_1_ = bf16[1,32,2048]{2,1,0:T(8,128)(2,1)S(1)} custom-call(s32[1]{0:T(128)} %bitcast.refs_0_, bf16[8,32,256]{2,1,0:T(8,128)(2,1)S(1)} %slice.3.refs_1_, bf16[8,32,256]{2,1,0:T(8,128)(2,1)S(1)} %collective-permute-done.11.refs_2_, bf16[8,32,256]{2,1,0:T(8,128)(2,1)S(1)} %collective-permute-done.9.refs_3_, ...), custom_call_target="tpu_custom_call" | custom-call | flops 452984832 | bytes 2097152 | tf_op jit(solution)/shard_map/coarse/pallas_call | solution.py:530
  42.6 0.5 collective-permute-done.10.refs_9_
  43.0 0.0 collective-permute-start.14
  43.0 0.5 collective-permute-start.15
  43.5 1.3 %collective-permute-start.13 = (bf16[1,32,2048]{2,1,0:T(8,128)(2,1)S(1)}, bf16[1,32,2048]{2,1,0:T(8,128)(2,1)S(1)}, u32[]{:S(2)}, u32[]{:S(2)}) collective-permute-start(bf16[1,32,2048]{2,1,0:T(8,128)(2,1)S(1)} %coarse.1.refs_1_), channel_id=1, source_target_pairs={{0,2},{1,3},{2,0},{3,1},{4,6},{5,7},{6,4},{7,5},{8,10},{9,11},{10,... | collective-permute-start | bytes 393224 | tf_op jit(solution)/shard_map/ppermute | solution.py:338
  44.9 1.2 %frames.1 = (bf16[100,48,128]{2,1,0:T(8,128)(2,1)S(1)}, bf16[1,9,48,128]{3,2,1,0:T(8,128)(2,1)S(1)}, bf16[8,128,128]{2,1,0:T(8,128)(2,1)S(1)}) custom-call(s32[1]{0:T(128)} %bitcast.refs_0_, s32[1]{0:T(128)} %bitcast.1.refs_0_.refs_1_, s32[4,26]{1,0:T(4,128)S(1)} %copy-done.7, bf16[192,512]{1,0:T(8,128)(2,1)S(1)} %get-tuple-element.59.refs_3_, ...), custom_call_target="tpu_custom_call" | custom-call | tf_op jit(solution)/shard_map/frames/pallas_call | solution.py:653
  46.1 2.9 %collective-permute-done.13.refs_3_ = bf16[1,32,2048]{2,1,0:T(8,128)(2,1)S(1)} collective-permute-done((bf16[1,32,2048]{2,1,0:T(8,128)(2,1)S(1)}, bf16[1,32,2048]{2,1,0:T(8,128)(2,1)S(1)}, u32[]{:S(2)}, u32[]{:S(2)}) %collective-permute-start.13) | collective-permute-done | bytes 131104 | tf_op jit(solution)/shard_map/ppermute | solution.py:338
  49.0 0.5 collective-permute-start.17
  49.5 0.8 %collective-permute-done.16.refs_2_ = bf16[1,32,2048]{2,1,0:T(8,128)(2,1)S(1)} collective-permute-done((bf16[1,32,2048]{2,1,0:T(8,128)(2,1)S(1)}, bf16[1,32,2048]{2,1,0:T(8,128)(2,1)S(1)}, u32[]{:S(2)}, u32[]{:S(2)}) %collective-permute-start.16) | collective-permute-done | bytes 131104 | tf_op jit(solution)/shard_map/ppermute | solution.py:338
  50.3 0.2 collective-permute-done.17.refs_4_
  50.5 4.1 %refine.1 = bf16[4,32,512]{2,1,0:T(8,128)(2,1)} custom-call(s32[1]{0:T(128)} %bitcast.refs_0_, bf16[1,32,2048]{2,1,0:T(8,128)(2,1)S(1)} %coarse.1.refs_1_, bf16[1,32,2048]{2,1,0:T(8,128)(2,1)S(1)} %collective-permute-done.16.refs_2_, bf16[1,32,2048]{2,1,0:T(8,128)(2,1)S(1)} %collective-permute-done.13.refs_3_, ...), custom_call_target="tpu_custom_call" | custom-call | flops 452984832 | bytes 4194304 | tf_op jit(solution)/shard_map/refine/pallas_call | solution.py:772
  (29 shorter events, 0.1 us)
Async XLA Ops:
  0.0 16.1 %copy-start.8 = (s32[2,16,128]{2,1,0:T(8,128)S(1)}, s32[2,16,128]{2,1,0:T(8,128)}, u32[]{:S(2)}) copy-start(s32[2,16,128]{2,1,0:T(8,128)} %constant.20.clone.refs_3_) | copy-start | bytes 49156
  0.0 16.1 %copy-start.10 = (s32[2,128]{1,0:T(2,128)S(1)}, s32[2,128]{1,0:T(2,128)}, u32[]{:S(2)}) copy-start(s32[2,128]{1,0:T(2,128)} %constant.21.clone.refs_11_) | copy-start | bytes 3076
  0.0 8.7 %copy-start.7 = (s32[4,26]{1,0:T(4,128)S(1)}, s32[4,26]{1,0:T(4,128)}, u32[]{:S(2)}) copy-start(s32[4,26]{1,0:T(4,128)} %refs_2_.4) | copy-start | bytes 1252
  0.0 16.1 %copy-start.9 = (s32[2,26]{1,0:T(2,128)S(1)}, s32[2,26]{1,0:T(2,128)}, u32[]{:S(2)}) copy-start(s32[2,26]{1,0:T(2,128)} %refs_1_.1) | copy-start | bytes 628
  0.0 16.1 %copy-start.11 = (s32[4]{0:T(128)S(1)}, s32[4]{0:T(128)}, u32[]{:S(2)}) copy-start(s32[4]{0:T(128)} %refs_2_.3) | copy-start | bytes 52
  0.0 8.7 %collective-permute-start = (s32[1,4,26]{2,1,0:T(4,128)}, s32[1,4,26]{2,1,0:T(4,128)S(1)}, u32[]{:S(2)}, u32[]{:S(2)}) collective-permute-start(s32[1,4,26]{2,1,0:T(4,128)} %bitcast.11), channel_id=1, source_target_pairs={{0,16},{4,20},{8,24},{12,28},{16,0},{20,4},{24,8},{28,12},{1,17},{... | collective-permute-start | bytes 1256 | tf_op jit(solution)/shard_map/ppermute | solution.py:338
  4.1 1.3 %copy-start = (bf16[512,1152]{1,0:T(8,128)(2,1)S(1)}, bf16[512,1152]{1,0:T(8,128)(2,1)}, u32[]{:S(2)}) copy-start(bf16[512,1152]{1,0:T(8,128)(2,1)} %constant.19.clone.refs_2_) | copy-start | bytes 3538948
  5.4 0.9 %copy-start.3 = (bf16[4,32,512]{2,1,0:T(8,128)(2,1)S(1)}, bf16[4,32,512]{2,1,0:T(8,128)(2,1)}, u32[]{:S(2)}) copy-start(bf16[4,32,512]{2,1,0:T(8,128)(2,1)} %param.15) | copy-start | bytes 393220
  6.3 0.8 %copy-start.4 = (bf16[8,128,32]{1,2,0:T(8,128)(2,1)S(1)}, bf16[8,128,32]{1,2,0:T(8,128)(2,1)}, u32[]{:S(2)}) copy-start(bf16[8,128,32]{1,2,0:T(8,128)(2,1)} %param.19) | copy-start | bytes 196612
  7.1 0.8 %copy-start.5 = (bf16[8,32,128]{2,1,0:T(8,128)(2,1)S(1)}, bf16[8,32,128]{2,1,0:T(8,128)(2,1)}, u32[]{:S(2)}) copy-start(bf16[8,32,128]{2,1,0:T(8,128)(2,1)} %param.21) | copy-start | bytes 196612
  8.0 8.1 %copy-start.6 = (bf16[128,128]{1,0:T(8,128)(2,1)S(1)}, bf16[128,128]{1,0:T(8,128)(2,1)}, u32[]{:S(2)}) copy-start(bf16[128,128]{1,0:T(8,128)(2,1)} %constant.22.clone.refs_12_) | copy-start | bytes 98308
  8.7 30.3 %copy-start.13 = (bf16[27,32,128]{2,1,0:T(8,128)(2,1)S(1)}, bf16[27,32,128]{2,1,0:T(8,128)(2,1)}, u32[]{:S(2)}) copy-start(bf16[27,32,128]{2,1,0:T(8,128)(2,1)} %refs_6_.1) | copy-start | bytes 663556
  8.7 30.3 %copy-start.14 = (f32[32]{0:T(128)S(1)}, f32[32]{0:T(128)}, u32[]{:S(2)}) copy-start(f32[32]{0:T(128)} %param.23) | copy-start | bytes 388
  8.7 3.7 %collective-permute-start.1 = (s32[2,4,26]{2,1,0:T(4,128)S(1)}, s32[2,4,26]{2,1,0:T(4,128)S(1)}, u32[]{:S(2)}, u32[]{:S(2)}) collective-permute-start(s32[2,4,26]{2,1,0:T(4,128)S(1)} %pad_add_fusion.1), channel_id=1, source_target_pairs={{0,8},{4,12},{8,0},{12,4},{16,24},{20,28},{24,16},{28,20},{1,9},{5... | collective-permute-start | bytes 2504 | tf_op jit(solution)/shard_map/ppermute | solution.py:338
  10.4 2.0 %collective-permute-start.2 = (bf16[32,256]{1,0:T(8,128)(2,1)S(1)}, bf16[32,256]{1,0:T(8,128)(2,1)S(1)}, u32[]{:S(2)}, u32[]{:S(2)}) collective-permute-start(bf16[32,256]{1,0:T(8,128)(2,1)S(1)} %get-tuple-element.45), channel_id=1, source_target_pairs={{0,1},{1,0},{2,3},{3,2},{4,5},{5,4},{6,7},{7,6},{8,9},{9,8},{10,11... | collective-permute-start | bytes 49160 | tf_op jit(solution)/shard_map/ppermute | solution.py:338
  10.4 3.7 %collective-permute-start.3 = (bf16[32,256]{1,0:T(8,128)(2,1)S(1)}, bf16[32,256]{1,0:T(8,128)(2,1)S(1)}, u32[]{:S(2)}, u32[]{:S(2)}) collective-permute-start(bf16[32,256]{1,0:T(8,128)(2,1)S(1)} %get-tuple-element.47), channel_id=1, source_target_pairs={{0,2},{1,3},{2,0},{3,1},{4,6},{5,7},{6,4},{7,5},{8,10},{9,11},{10,... | collective-permute-start | bytes 49160 | tf_op jit(solution)/shard_map/ppermute | solution.py:338
  11.9 3.2 %collective-permute-start.4 = (bf16[32,256]{1,0:T(8,128)(2,1)S(1)}, bf16[32,256]{1,0:T(8,128)(2,1)S(1)}, u32[]{:S(2)}, u32[]{:S(2)}) collective-permute-start(bf16[32,256]{1,0:T(8,128)(2,1)S(1)} %get-tuple-element.48), channel_id=1, source_target_pairs={{0,3},{1,2},{2,1},{3,0},{4,7},{5,6},{6,5},{7,4},{8,11},{9,10},{10,... | collective-permute-start | bytes 49160 | tf_op jit(solution)/shard_map/ppermute | solution.py:338
  12.4 3.7 %collective-permute-start.5 = (s32[4,4,26]{2,1,0:T(4,128)S(1)}, s32[4,4,26]{2,1,0:T(4,128)S(1)}, u32[]{:S(2)}, u32[]{:S(2)}) collective-permute-start(s32[4,4,26]{2,1,0:T(4,128)S(1)} %pad_add_fusion.refs_8_), channel_id=1, source_target_pairs={{0,4},{4,0},{8,12},{12,8},{16,20},{20,16},{24,28},{28,24},{1,5},{5... | collective-permute-start | bytes 5000 | tf_op jit(solution)/shard_map/ppermute | solution.py:338
  18.8 13.3 %all-to-all-start = ((bf16[8,80,256]{2,1,0:T(8,128)(2,1)}), bf16[8,80,256]{2,1,0:T(8,128)(2,1)S(1)}, u32[]{:S(2)}, u32[]{:S(2)}) async-start(bf16[8,80,256]{2,1,0:T(8,128)(2,1)} %get-tuple-element.51), calls=%async_computation | async-start | bytes 655360 | tf_op jit(solution)/shard_map/all_to_all | solution.py:840
  22.6 5.7 %collective-permute-start.7 = (bf16[192,512]{1,0:T(8,128)(2,1)S(1)}, bf16[192,512]{1,0:T(8,128)(2,1)S(1)}, u32[]{:S(2)}, u32[]{:S(2)}) collective-permute-start(bf16[192,512]{1,0:T(8,128)(2,1)S(1)} %get-tuple-element.59.refs_3_), channel_id=1, source_target_pairs={{0,2},{1,3},{2,0},{3,1},{4,6},{5,7},{6,4},{7,5},{8,10},{9,11},{10,... | collective-permute-start | bytes 589832 | tf_op jit(solution)/shard_map/ppermute | solution.py:338
  24.1 4.2 %collective-permute-start.6 = (bf16[192,512]{1,0:T(8,128)(2,1)S(1)}, bf16[192,512]{1,0:T(8,128)(2,1)S(1)}, u32[]{:S(2)}, u32[]{:S(2)}) collective-permute-start(bf16[192,512]{1,0:T(8,128)(2,1)S(1)} %get-tuple-element.59.refs_3_), channel_id=1, source_target_pairs={{0,1},{1,0},{2,3},{3,2},{4,5},{5,4},{6,7},{7,6},{8,9},{9,8},{10,11... | collective-permute-start | bytes 589832 | tf_op jit(solution)/shard_map/ppermute | solution.py:338
  28.3 1.4 %collective-permute-start.8 = (bf16[192,512]{1,0:T(8,128)(2,1)S(1)}, bf16[192,512]{1,0:T(8,128)(2,1)S(1)}, u32[]{:S(2)}, u32[]{:S(2)}) collective-permute-start(bf16[192,512]{1,0:T(8,128)(2,1)S(1)} %collective-permute-done.7.refs_5_), channel_id=1, source_target_pairs={{0,1},{1,0},{2,3},{3,2},{4,5},{5,4},{6,7},{7,6},{8,9},{9,8},{10,11... | collective-permute-start | bytes 589832 | tf_op jit(solution)/shard_map/ppermute | solution.py:338
  32.1 5.0 %collective-permute-start.9 = (bf16[8,32,256]{2,1,0:T(8,128)(2,1)S(1)}, bf16[8,32,256]{2,1,0:T(8,128)(2,1)S(1)}, u32[]{:S(2)}, u32[]{:S(2)}) collective-permute-start(bf16[8,32,256]{2,1,0:T(8,128)(2,1)S(1)} %slice.3.refs_1_), channel_id=1, source_target_pairs={{0,2},{1,3},{2,0},{3,1},{4,6},{5,7},{6,4},{7,5},{8,10},{9,11},{10,... | collective-permute-start | bytes 393224 | tf_op jit(solution)/shard_map/ppermute | solution.py:338
  37.1 1.8 %collective-permute-start.11 = (bf16[8,32,256]{2,1,0:T(8,128)(2,1)S(1)}, bf16[8,32,256]{2,1,0:T(8,128)(2,1)S(1)}, u32[]{:S(2)}, u32[]{:S(2)}) collective-permute-start(bf16[8,32,256]{2,1,0:T(8,128)(2,1)S(1)} %slice.3.refs_1_), channel_id=1, source_target_pairs={{0,1},{1,0},{2,3},{3,2},{4,5},{5,4},{6,7},{7,6},{8,9},{9,8},{10,11... | collective-permute-start | bytes 393224 | tf_op jit(solution)/shard_map/ppermute | solution.py:338
  37.1 1.8 %collective-permute-start.12 = (bf16[8,32,256]{2,1,0:T(8,128)(2,1)S(1)}, bf16[8,32,256]{2,1,0:T(8,128)(2,1)S(1)}, u32[]{:S(2)}, u32[]{:S(2)}) collective-permute-start(bf16[8,32,256]{2,1,0:T(8,128)(2,1)S(1)} %collective-permute-done.9.refs_3_), channel_id=1, source_target_pairs={{0,1},{1,0},{2,3},{3,2},{4,5},{5,4},{6,7},{7,6},{8,9},{9,8},{10,11... | collective-permute-start | bytes 393224 | tf_op jit(solution)/shard_map/ppermute | solution.py:338
  37.6 5.4 %collective-permute-start.10 = (bf16[4,32,512]{2,1,0:T(8,128)(2,1)S(1)}, bf16[4,32,512]{2,1,0:T(8,128)(2,1)S(1)}, u32[]{:S(2)}, u32[]{:S(2)}) collective-permute-start(bf16[4,32,512]{2,1,0:T(8,128)(2,1)S(1)} %halo.1.refs_7_), channel_id=1, source_target_pairs={{0,2},{1,3},{2,0},{3,1},{4,6},{5,7},{6,4},{7,5},{8,10},{9,11},{10,... | collective-permute-start | bytes 393224 | tf_op jit(solution)/shard_map/ppermute | solution.py:338
  39.0 11.5 %copy-start.1 = (bf16[27,32,128]{2,1,0:T(8,128)(2,1)S(1)}, bf16[27,32,128]{2,1,0:T(8,128)(2,1)}, u32[]{:S(2)}) copy-start(bf16[27,32,128]{2,1,0:T(8,128)(2,1)} %refs_8_.1) | copy-start | bytes 663556
  39.0 11.5 %copy-start.2 = (bf16[256,256]{1,0:T(8,128)(2,1)S(1)}, bf16[256,256]{1,0:T(8,128)(2,1)}, u32[]{:S(2)}) copy-start(bf16[256,256]{1,0:T(8,128)(2,1)} %constant.23.clone.refs_10_) | copy-start | bytes 393220
  39.0 11.5 %copy-start.12 = (f32[32]{0:T(128)S(1)}, f32[32]{0:T(128)}, u32[]{:S(2)}) copy-start(f32[32]{0:T(128)} %param.24) | copy-start | bytes 388
  43.0 1.8 %collective-permute-start.14 = (bf16[4,32,512]{2,1,0:T(8,128)(2,1)S(1)}, bf16[4,32,512]{2,1,0:T(8,128)(2,1)S(1)}, u32[]{:S(2)}, u32[]{:S(2)}) collective-permute-start(bf16[4,32,512]{2,1,0:T(8,128)(2,1)S(1)} %halo.1.refs_7_), channel_id=1, source_target_pairs={{0,1},{1,0},{2,3},{3,2},{4,5},{5,4},{6,7},{7,6},{8,9},{9,8},{10,11... | collective-permute-start | bytes 393224 | tf_op jit(solution)/shard_map/ppermute | solution.py:338
  43.0 1.8 %collective-permute-start.15 = (bf16[4,32,512]{2,1,0:T(8,128)(2,1)S(1)}, bf16[4,32,512]{2,1,0:T(8,128)(2,1)S(1)}, u32[]{:S(2)}, u32[]{:S(2)}) collective-permute-start(bf16[4,32,512]{2,1,0:T(8,128)(2,1)S(1)} %collective-permute-done.10.refs_9_), channel_id=1, source_target_pairs={{0,1},{1,0},{2,3},{3,2},{4,5},{5,4},{6,7},{7,6},{8,9},{9,8},{10,11... | collective-permute-start | bytes 393224 | tf_op jit(solution)/shard_map/ppermute | solution.py:338
  43.5 5.4 %collective-permute-start.13 = (bf16[1,32,2048]{2,1,0:T(8,128)(2,1)S(1)}, bf16[1,32,2048]{2,1,0:T(8,128)(2,1)S(1)}, u32[]{:S(2)}, u32[]{:S(2)}) collective-permute-start(bf16[1,32,2048]{2,1,0:T(8,128)(2,1)S(1)} %coarse.1.refs_1_), channel_id=1, source_target_pairs={{0,2},{1,3},{2,0},{3,1},{4,6},{5,7},{6,4},{7,5},{8,10},{9,11},{10,... | collective-permute-start | bytes 393224 | tf_op jit(solution)/shard_map/ppermute | solution.py:338
  48.9 1.3 %collective-permute-start.16 = (bf16[1,32,2048]{2,1,0:T(8,128)(2,1)S(1)}, bf16[1,32,2048]{2,1,0:T(8,128)(2,1)S(1)}, u32[]{:S(2)}, u32[]{:S(2)}) collective-permute-start(bf16[1,32,2048]{2,1,0:T(8,128)(2,1)S(1)} %coarse.1.refs_1_), channel_id=1, source_target_pairs={{0,1},{1,0},{2,3},{3,2},{4,5},{5,4},{6,7},{7,6},{8,9},{9,8},{10,11... | collective-permute-start | bytes 393224 | tf_op jit(solution)/shard_map/ppermute | solution.py:338
  49.0 1.5 %collective-permute-start.17 = (bf16[1,32,2048]{2,1,0:T(8,128)(2,1)S(1)}, bf16[1,32,2048]{2,1,0:T(8,128)(2,1)S(1)}, u32[]{:S(2)}, u32[]{:S(2)}) collective-permute-start(bf16[1,32,2048]{2,1,0:T(8,128)(2,1)S(1)} %collective-permute-done.13.refs_3_), channel_id=1, source_target_pairs={{0,1},{1,0},{2,3},{3,2},{4,5},{5,4},{6,7},{7,6},{8,9},{9,8},{10,11... | collective-permute-start | bytes 393224 | tf_op jit(solution)/shard_map/ppermute | solution.py:338

commit v5 on v4

--- a/solution.py
+++ b/solution.py
@@ -380,8 +380,17 @@
     return have
 
 
-def halo_kernel(q, base, from_ref, recv_ref, out_ref):
+def halo_kernel(q, base, owner_ref, links_ref, from_ref, recv_ref, out_ref, sel_ref):
     fine = out_ref.shape[0]
+
+    def selectors(block, _):
+        sel_ref[block] = jnp.concatenate(line_selectors(fine, owner_ref[0], links_ref, block), axis=0)
+        return 0
+
+    if sel_ref.shape[0] == 1:
+        selectors(0, 0)
+    else:
+        lax.fori_loop(0, sel_ref.shape[0], selectors, 0)
     half = q // 2
     lane = lax.broadcasted_iota(jnp.int32, (q, 128), 1)
     for b in range(fine):
@@ -405,15 +414,18 @@
             out_ref[b, :, chunk * 128 : (chunk + 1) * 128] = here.astype(BF16)
 
 
-def halo(places, recv, base, fine, q, vox):
+def halo(owner, links, places, recv, base, fine, q, vox):
     return pl.pallas_call(
         lambda *refs: halo_kernel(q, base, *refs),
-        out_shape=jax.ShapeDtypeStruct((fine, q, vox), BF16),
-        in_specs=[pl.BlockSpec(memory_space=SM), pl.BlockSpec(memory_space=VM)],
-        out_specs=pl.BlockSpec(memory_space=VM),
+        out_shape=[
+            jax.ShapeDtypeStruct((fine, q, vox), BF16),
+            jax.ShapeDtypeStruct((recv.shape[0] * fine // NBLK, 9 * 8 * fine, 128), BF16),
+        ],
+        in_specs=[pl.BlockSpec(memory_space=SM)] * 3 + [pl.BlockSpec(memory_space=VM)],
+        out_specs=[pl.BlockSpec(memory_space=VM)] * 2,
         compiler_params=params(),
         name="halo",
-    )(places, recv)
+    )(owner, links, places, recv)
 
 
 def axis_places(u):
@@ -432,7 +444,51 @@
     return jnp.sum(jnp.where(on, square, 0.0), axis=1, keepdims=True)
 
 
-def coarse_kernel(chans, codes, me_ref, *refs):
+LINES = [
+    (ux, uy, a, b)
+    for ux in range(HALF)
+    for uy in range(HALF)
+    for a in axis_places(ux)
+    for b in axis_places(uy)
+]
+
+
+def line_selectors(fine, owner, links_ref, block):
+    lane = lax.broadcasted_iota(jnp.int32, (8, 128), 1)
+    row = lax.broadcasted_iota(jnp.int32, (8, 128), 0)
+    made = []
+    for dx in (-1, 0, 1):
+        for dy in (-1, 0, 1):
+            tiles = []
+            for b in range(fine):
+                at = []
+                for dz in (-1, 0, 1):
+                    k = HEADING_INDEX[(dx, dy, dz)]
+                    n = owner * fine + b if k == len(HEADINGS) else links_ref[b, k]
+                    n = n - block * NBLK
+                    at.append(jnp.where((n >= 0) & (n < NBLK), n, -1024))
+                want = jnp.where(row == 0, at[0] + (HALF - 1) * NBLK, at[1] + (row - 1) * NBLK)
+                want = jnp.where(row == HALF + 1, at[2], want)
+                tiles.append(((lane == want) & (row < HALF + 2)).astype(F32))
+            made.append(jnp.concatenate(tiles, axis=0).astype(BF16))
+    return made
+
+
+def line_spreader(fine, rows):
+    wide = 8 * fine
+    lines = 128 // wide
+    sel = np.zeros((lines * rows, 128), np.float32)
+    for i in range(lines):
+        for b in range(fine):
+            first = i * wide + b * 8
+            for z in range(EDGE):
+                sel[i * rows + b * EDGE + z, first + 1 + z // 2] = 1
+            for side in range(2):
+                sel[i * rows + wide + 2 * b + side, first + side * (HALF + 1)] = 1
+    return sel
+
+
+def coarse_kernel(chans, codes, me_ref, picker_ref, *refs):
     slots, refs = refs[:chans], refs[chans:]
     recv_ref, w_ref, bias_ref, out_ref, proj_ref, rows_ref, sel_ref, nb_ref, parent_ref, table_ref = refs
     owners, q, lanes = slots[0].shape
@@ -499,7 +555,21 @@
     step = HALF * HALF * NBLK
     n = HALF * step
     res = acc[0:q, 0:n] + acc[q : 2 * q, step : step + n] + acc[2 * q : 3 * q, 2 * step : 2 * step + n]
-    out_ref[0] = jnp.maximum(res + bias_column(bias_ref[...]), 0.0).astype(BF16)
+    res = jnp.maximum(res + bias_column(bias_ref[...]), 0.0).astype(BF16)
+    size = picker_ref.shape[1] // 9
+    pickers = [picker_ref[0, i * size : (i + 1) * size, :] for i in range(9)]
+    found = []
+    for ux in range(HALF):
+        for uy in range(HALF):
+            col = (ux * HALF + uy) * 128
+            mine = [pickers[3 * (a[0] + 1) + b[0] + 1] for x, y, a, b in LINES if (x, y) == (ux, uy)]
+            found.append(dot_t(res[:, col : col + 128], jnp.concatenate(mine, axis=0)))
+    found = jnp.concatenate(found, axis=1).astype(BF16)
+    if pl.num_programs(0) == 1:
+        out_ref[...] = found
+    else:
+        before = out_ref[...]
+        out_ref[...] = jnp.where(pl.program_id(0) == 0, jnp.zeros_like(before), before) + found
 
 
 def conv_rows(w_ref, rows_of, together):
@@ -520,25 +590,26 @@
     return acc
 
 
-def coarse(me, slots, recv, codes, weight, bias):
+def coarse(me, pickers, slots, recv, codes, weight, bias):
     chans = len(slots)
     owners, q, lanes = slots[0].shape
-    total = owners * lanes // CUBE
+    fine = lanes // CUBE
+    total = owners * fine
     blocks = total // NBLK
     c_in = weight.shape[2]
     whole = lambda a: pl.BlockSpec(a.shape, lambda i: (0,) * a.ndim)
     return pl.pallas_call(
         lambda *refs: coarse_kernel(chans, codes, *refs),
-        out_shape=jax.ShapeDtypeStruct((blocks, q, CUBE * NBLK), BF16),
+        out_shape=jax.ShapeDtypeStruct((q, len(LINES) * 8 * fine), BF16),
         grid=(blocks,),
-        in_specs=[pl.BlockSpec(memory_space=SM)]
+        in_specs=[pl.BlockSpec(memory_space=SM), pl.BlockSpec((1,) + pickers.shape[1:], lambda i: (i, 0, 0))]
         + [whole(a) for a in slots]
         + [
             pl.BlockSpec((owners, codes, recv.shape[2]), lambda i: (0, recv.shape[1] // codes - 1, 0)),
             whole(weight),
             whole(bias),
         ],
-        out_specs=pl.BlockSpec((1, q, CUBE * NBLK), lambda i: (i, 0, 0)),
+        out_specs=pl.BlockSpec((q, len(LINES) * 8 * fine), lambda i: (0, 0)),
         scratch_shapes=[
             pltpu.VMEM((chans, owners, q, lanes), BF16),
             pltpu.VMEM((CUBE * total, c_in), F32),
@@ -550,7 +621,7 @@
         compiler_params=params(),
         cost_estimate=cost(2 * 27 * c_in * q * CUBE * total, 2 * 1024 * 1024),
         name="coarse",
-    )(me, *slots, recv, weight, bias)
+    )(me, pickers, *slots, recv, weight, bias)
 
 
 def frame_axis(f):
@@ -561,11 +632,10 @@
     return 0, f - 1
 
 
-def frame_kernel(chans, me_ref, owner_ref, links_ref, *refs):
+def frame_kernel(chans, me_ref, *refs):
     packs, halos, refs = refs[:chans], refs[chans : 2 * chans], refs[2 * chans :]
-    ff_ref, sel_ref, up_ref, both, inner, outer, plane = refs
+    ff_ref, up_ref, both, inner, outer, plane = refs
     fine, q, vox = halos[0].shape
-    owner = owner_ref[0]
     me = me_ref[0]
     for s in range(chans):
         at = pl.ds(pl.multiple_of((me ^ s) * q, q), q)
@@ -613,39 +683,9 @@
             tiles.append(plane[(fx * FRAME + fy) * 8 : (fx * FRAME + fy) * 8 + 8, :])
             tiles.append(jnp.zeros((8, plane.shape[1]), F32))
             ff_ref[at] = jnp.concatenate(tiles, axis=0).astype(BF16)
-    blocks = sel_ref.shape[0]
-    lane = lax.broadcasted_iota(jnp.int32, (8, 128), 1)
-    row = lax.broadcasted_iota(jnp.int32, (8, 128), 0)
-
-    def pick(j, _):
-        for dx in (-1, 0, 1):
-            for dy in (-1, 0, 1):
-                def brick(b, dz):
-                    k = HEADING_INDEX[(dx, dy, dz)]
-                    n = owner * fine + b if k == len(HEADINGS) else links_ref[b, k]
-                    n = n - j * NBLK
-                    return jnp.where((n >= 0) & (n < NBLK), n, -1024)
-
-                tiles = []
-                for b in range(fine):
-                    tiles.append((lane - (row // 2) * NBLK == brick(b, 0)).astype(F32))
-                low = jnp.full((8, 128), -1024, jnp.int32)
-                for b in range(fine):
-                    for s in range(2):
-                        n = brick(b, 2 * s - 1) + (HALF - 1) * (1 - s) * NBLK
-                        low = jnp.where(row == 2 * b + s, n, low)
-                tiles.append((lane == low).astype(F32))
-                tiles.append(jnp.zeros((8, 128), F32))
-                sel_ref[j, 3 * (dx + 1) + dy + 1] = jnp.concatenate(tiles, axis=0).astype(BF16)
-        return 0
-
-    if blocks == 1:
-        pick(0, 0)
-    else:
-        lax.fori_loop(0, blocks, pick, 0)
-
-
-def frames(me, owner, links, packs, halos, blocks):
+
+
+def frames(me, packs, halos):
     chans = len(packs)
     fine, q, vox = halos[0].shape
     rows = 8 * fine + 16
@@ -654,11 +694,10 @@
         lambda *refs: frame_kernel(chans, *refs),
         out_shape=[
             jax.ShapeDtypeStruct((FRAME * FRAME, rows, c_all), BF16),
-            jax.ShapeDtypeStruct((blocks, 9, rows, 128), BF16),
             jax.ShapeDtypeStruct((8, c_all, c_all), BF16),
         ],
-        in_specs=[pl.BlockSpec(memory_space=SM)] * 3 + [pl.BlockSpec(memory_space=VM)] * (2 * chans),
-        out_specs=[pl.BlockSpec(memory_space=VM)] * 3,
+        in_specs=[pl.BlockSpec(memory_space=SM)] + [pl.BlockSpec(memory_space=VM)] * (2 * chans),
+        out_specs=[pl.BlockSpec(memory_space=VM)] * 2,
         scratch_shapes=[
             pltpu.VMEM((2, fine, c_all, vox), BF16),
             pltpu.VMEM((fine, vox, c_all), F32),
@@ -667,46 +706,25 @@
         ],
         compiler_params=params(),
         name="frames",
-    )(me, owner, links, *packs, *halos)
+    )(me, *packs, *halos)
 
 
 def fine_kernel(chans, me_ref, *refs):
     slots, refs = refs[:chans], refs[chans:]
     ff_ref, sel_ref, up_ref, w_ref, bias_ref, pair_ref, out_ref, co_ref, cr, g3 = refs
-    blocks, q, _ = slots[0].shape
+    q = slots[0].shape[0]
     c_all = chans * q
     for s in range(chans):
         co_ref[me_ref[0] ^ s] = slots[s][...]
     fine = out_ref.shape[0]
     rows = ff_ref.shape[1]
-    for ux in range(HALF):
-        for uy in range(HALF):
-            places = [
-                (3 * (a[0] + 1) + b[0] + 1, a[1], b[1])
-                for a in axis_places(ux)
-                for b in axis_places(uy)
-            ]
-            col = (ux * HALF + uy) * 128
-
-            def part(j):
-                source = jnp.concatenate(
-                    [co_ref[c, j, :, col : col + 128] for c in range(chans)], axis=0
-                )
-                picker = jnp.concatenate([sel_ref[j, d] for d, _, _ in places], axis=0)
-                return dot_t(picker, source)
-
-            if blocks == 1:
-                got = part(0)
-            else:
-                got = lax.fori_loop(
-                    0,
-                    blocks,
-                    lambda j, a: a + part(j),
-                    jnp.zeros((len(places) * rows, c_all), F32),
-                )
-            got = got.astype(BF16)
-            for i, (_, x, y) in enumerate(places):
-                cr[x, y] = got[i * rows : (i + 1) * rows]
+    lines = 128 // (8 * fine)
+    for i in range(0, len(LINES), lines):
+        col = i * 8 * fine
+        source = jnp.concatenate([co_ref[c, :, col : col + 128] for c in range(chans)], axis=0)
+        got = dot_t(sel_ref[...], source).astype(BF16)
+        for j, (_, _, x, y) in enumerate(LINES[i : i + lines]):
+            cr[x[1], y[1]] = got[j * rows : (j + 1) * rows]
     r = lax.broadcasted_iota(jnp.int32, (rows, c_all), 0)
     odd = (r % 2 == 1) ^ (r >= 8 * fine)
     sub = lax.broadcasted_iota(jnp.int32, (5, 8, c_all), 1)
@@ -763,9 +781,9 @@
                 out_ref[2 * pair + b, :, 128 * h : 128 * h + 128] = turned[:, 128 * b : 128 * b + 128]
 
 
-def refine(me, slots, ff, sel, up_weight, weight, bias):
+def refine(me, slots, ff, up_weight, weight, bias):
     chans = len(slots)
-    blocks, q, wide = slots[0].shape
+    q, wide = slots[0].shape
     rows = ff.shape[1]
     fine = (rows - 16) // 8
     c_all = chans * q
@@ -775,14 +793,14 @@
         in_specs=[pl.BlockSpec(memory_space=SM)] + [pl.BlockSpec(memory_space=VM)] * (chans + 6),
         out_specs=pl.BlockSpec(memory_space=VM),
         scratch_shapes=[
-            pltpu.VMEM((chans, blocks, q, wide), BF16),
+            pltpu.VMEM((chans, q, wide), BF16),
             pltpu.VMEM((HALF + 2, HALF + 2, rows, c_all), BF16),
             pltpu.VMEM((3, fine // 2, FRAME, FRAME, 2 * EDGE, c_all), BF16),
         ],
         compiler_params=params(),
         cost_estimate=cost(2 * 27 * c_all * q * fine * EDGE**3, 4 * 1024 * 1024),
         name="refine",
-    )(me, *slots, ff, sel, up_weight, weight, bias, jnp.asarray(pair_selector(), BF16))
+    )(me, *slots, ff, jnp.asarray(line_spreader(fine, rows), BF16), up_weight, weight, bias, jnp.asarray(pair_selector(), BF16))
 
 
 def octant_table():
@@ -840,18 +858,18 @@
     recv = lax.all_to_all(sending, "brick", split_axis=0, concat_axis=0, tiled=True)
     packs, _ = relayed(packed, chans)
     recv, packs = lax.optimization_barrier((recv, packs))
-    slots, around = relayed(recv[:, :q], chans, lambda: halo(places, recv, q, fine, q, vox))
+    slots, (around, pickers) = relayed(
+        recv[:, :q],
+        chans,
+        lambda: halo(owner[None], fine_links, places, recv, q, fine, q, vox),
+    )
     halos, co = relayed(
         around,
         chans,
-        lambda: coarse(me[None], slots, recv, codes, coarse_weight, coarse_bias[None]),
+        lambda: coarse(me[None], pickers, slots, recv, codes, coarse_weight, coarse_bias[None]),
     )
-    cos, (ff, sel, up_all) = relayed(
-        co,
-        chans,
-        lambda: frames(me[None], owner[None], fine_links, packs, halos, co.shape[0]),
-    )
-    return refine(me[None], cos, ff, sel, up_all, fine_weight, fine_bias[None])
+    cos, (ff, up_all) = relayed(co, chans, lambda: frames(me[None], packs, halos))
+    return refine(me[None], cos, ff, up_all, fine_weight, fine_bias[None])
 
 
 def solution(mesh):

time: 55 us -> 53.6 us (0.975)
  waiting for transfers between devices: 17.1 us -> 16.1 us
    ppermute x18, waiting for transfers between devices: 14.8 us -> 13.8 us  [partner(): return lax.ppermute(x, axis, [(i, i ^ step) for i in range(count)])]
    pallas_call x1, Pallas kernels: 1.19 us -> 0.53 us  [frames(): pl.pallas_call(lambda *refs: frame_kernel(chans, *refs), out_shape=[jax.S...]
    unnamed x30 -> x32, local copies, waits for them, and re-layouts: 3.91 us -> 3.91 us
where the time goes in v5:
time: 53.6 us; the launch traced here: 53.3 us
  starting transfers between devices  20.1 us (38%)
  waiting for transfers between devices  16.1 us (30%)
  Pallas kernels  13 us (24%)
  local copies, waits for them, and re-layouts  3.92 us (7%)
    ppermute x18, starting transfers between devices, partner(): return lax.ppermute(x, axis, [(i, i ^ step) for i in range(count)])  16.3 us
    ppermute x18, waiting for transfers between devices, partner(): return lax.ppermute(x, axis, [(i, i ^ step) for i in range(count)])  13.8 us
    pallas_call x1, Pallas kernels, refine(): pl.pallas_call(lambda *refs: fine_kernel(chans, *refs), out_shape=jax.Sha...  3.94 us
    unnamed x32, local copies, waits for them, and re-layouts  3.91 us
    all_to_all x1, starting transfers between devices, per_device(): lax.all_to_all(sending, 'brick', split_axis=0, concat_axis=0, tiled=True)  3.79 us
    pallas_call x1, Pallas kernels, coarse(): pl.pallas_call(lambda *refs: coarse_kernel(chans, codes, *refs), out_shap...  3.77 us
    pallas_call x1, Pallas kernels, assemble(): pl.pallas_call(lambda *refs: assemble_kernel(len(slots), len(asked), fine...  2.63 us
    all_to_all x1, waiting for transfers between devices, per_device(): lax.all_to_all(sending, 'brick', split_axis=0, concat_axis=0, tiled=True)  2.35 us
  transfers between devices with their start and end apart: 19, of which 12 were waited for; matrix products, arithmetic and copies ran while one was open for 0% of the time, Pallas kernels for 12%

profile of v5, /device:TPU:0, one launch (start us, length us, event | category | flops | bytes accessed | tf_op | source)
XLA Modules:
  0.0 53.3 jit_solution(11674073984018119276)
XLA Ops:
  0.0 4.1 %collective-permute-start = (s32[1,4,26]{2,1,0:T(4,128)}, s32[1,4,26]{2,1,0:T(4,128)S(1)}, u32[]{:S(2)}, u32[]{:S(2)}) collective-permute-start(s32[1,4,26]{2,1,0:T(4,128)} %bitcast.11), channel_id=1, source_target_pairs={{0,16},{4,20},{8,24},{12,28},{16,0},{20,4},{24,8},{28,12},{1,17},{... | collective-permute-start | bytes 1256 | tf_op jit(solution)/shard_map/ppermute | solution.py:338
  4.1 1.3 %copy-done = bf16[512,1152]{1,0:T(8,128)(2,1)S(1)} copy-done((bf16[512,1152]{1,0:T(8,128)(2,1)S(1)}, bf16[512,1152]{1,0:T(8,128)(2,1)}, u32[]{:S(2)}) %copy-start) | copy-done | bytes 1179672
  5.4 0.9 %copy-done.3 = bf16[4,32,512]{2,1,0:T(8,128)(2,1)S(1)} copy-done((bf16[4,32,512]{2,1,0:T(8,128)(2,1)S(1)}, bf16[4,32,512]{2,1,0:T(8,128)(2,1)}, u32[]{:S(2)}) %copy-start.3) | copy-done | bytes 131096
  6.3 0.8 %copy-done.4 = bf16[8,128,32]{1,2,0:T(8,128)(2,1)S(1)} copy-done((bf16[8,128,32]{1,2,0:T(8,128)(2,1)S(1)}, bf16[8,128,32]{1,2,0:T(8,128)(2,1)}, u32[]{:S(2)}) %copy-start.4) | copy-done | bytes 65560
  7.1 0.8 %copy-done.5 = bf16[8,32,128]{2,1,0:T(8,128)(2,1)S(1)} copy-done((bf16[8,32,128]{2,1,0:T(8,128)(2,1)S(1)}, bf16[8,32,128]{2,1,0:T(8,128)(2,1)}, u32[]{:S(2)}) %copy-start.5) | copy-done | bytes 65560
  8.0 0.7 %project.1 = (bf16[32,256]{1,0:T(8,128)(2,1)S(1)}, bf16[32,256]{1,0:T(8,128)(2,1)S(1)}, bf16[32,256]{1,0:T(8,128)(2,1)S(1)}, bf16[32,256]{1,0:T(8,128)(2,1)S(1)}...) custom-call(s32[1]{0:T(128)} %bitcast.refs_0_, bf16[128,512]{1,0:T(8,128)(2,1)S(1)} %bitcast.8, ...), custom_call_target="tpu_custom_call" | custom-call | tf_op jit(solution)/shard_map/project/pallas_call | solution.py:176
  8.7 0.0 collective-permute-done
  8.7 1.6 %collective-permute-start.1 = (s32[2,4,26]{2,1,0:T(4,128)S(1)}, s32[2,4,26]{2,1,0:T(4,128)S(1)}, u32[]{:S(2)}, u32[]{:S(2)}) collective-permute-start(s32[2,4,26]{2,1,0:T(4,128)S(1)} %pad_add_fusion.1), channel_id=1, source_target_pairs={{0,8},{4,12},{8,0},{12,4},{16,24},{20,28},{24,16},{28,20},{1,9},{5... | collective-permute-start | bytes 2504 | tf_op jit(solution)/shard_map/ppermute | solution.py:338
  10.3 0.0 collective-permute-start.2
  10.3 1.5 %collective-permute-start.3 = (bf16[32,256]{1,0:T(8,128)(2,1)S(1)}, bf16[32,256]{1,0:T(8,128)(2,1)S(1)}, u32[]{:S(2)}, u32[]{:S(2)}) collective-permute-start(bf16[32,256]{1,0:T(8,128)(2,1)S(1)} %get-tuple-element.48), channel_id=1, source_target_pairs={{0,2},{1,3},{2,0},{3,1},{4,6},{5,7},{6,4},{7,5},{8,10},{9,11},{10,... | collective-permute-start | bytes 49160 | tf_op jit(solution)/shard_map/ppermute | solution.py:338
  11.9 0.3 collective-permute-start.4
  12.2 0.2 collective-permute-done.1
  12.4 0.0 collective-permute-done.2.refs_5_
  12.4 1.6 %collective-permute-start.5 = (s32[4,4,26]{2,1,0:T(4,128)S(1)}, s32[4,4,26]{2,1,0:T(4,128)S(1)}, u32[]{:S(2)}, u32[]{:S(2)}) collective-permute-start(s32[4,4,26]{2,1,0:T(4,128)S(1)} %pad_add_fusion.refs_8_), channel_id=1, source_target_pairs={{0,4},{4,0},{8,12},{12,8},{16,20},{20,16},{24,28},{28,24},{1,5},{5... | collective-permute-start | bytes 5000 | tf_op jit(solution)/shard_map/ppermute | solution.py:338
  13.9 0.1 collective-permute-done.3.refs_6_
  14.1 0.9 %collective-permute-done.4.refs_7_ = bf16[32,256]{1,0:T(8,128)(2,1)S(1)} collective-permute-done((bf16[32,256]{1,0:T(8,128)(2,1)S(1)}, bf16[32,256]{1,0:T(8,128)(2,1)S(1)}, u32[]{:S(2)}, u32[]{:S(2)}) %collective-permute-start.4) | collective-permute-done | bytes 16416 | tf_op jit(solution)/shard_map/ppermute | solution.py:338
  15.0 1.1 %collective-permute-done.5.refs_9_ = s32[4,4,26]{2,1,0:T(4,128)S(1)} collective-permute-done((s32[4,4,26]{2,1,0:T(4,128)S(1)}, s32[4,4,26]{2,1,0:T(4,128)S(1)}, u32[]{:S(2)}, u32[]{:S(2)}) %collective-permute-start.5) | collective-permute-done | bytes 1696 | tf_op jit(solution)/shard_map/ppermute | solution.py:338
  16.1 2.6 %assemble.1 = (bf16[8,80,256]{2,1,0:T(8,128)(2,1)}, s32[1,128]{1,0:T(1,128)S(1)}) custom-call(s32[1]{0:T(128)} %bitcast.1.refs_0_, s32[2,26]{1,0:T(2,128)S(1)} %copy-done.10, s32[4]{0:T(128)S(1)} %copy-done.12, s32[2,16,128]{2,1,0:T(8,128)S(1)} %copy-done.9, bf16[32,256]{1,0:T(8,128)(2,1)S(1)} %get-tuple-element.44.refs_4_, ...), custom_call_target="tpu_custom_call" | custom-call | flops 1048576 | bytes 12582912 | tf_op jit(solution)/shard_map/assemble/pallas_call | solution.py:315
  18.8 3.8 %all-to-all-start = ((bf16[8,80,256]{2,1,0:T(8,128)(2,1)}), bf16[8,80,256]{2,1,0:T(8,128)(2,1)S(1)}, u32[]{:S(2)}, u32[]{:S(2)}) async-start(bf16[8,80,256]{2,1,0:T(8,128)(2,1)} %get-tuple-element.52), calls=%async_computation | async-start | bytes 655360 | tf_op jit(solution)/shard_map/all_to_all | solution.py:858
  22.6 1.5 %collective-permute-start.7 = (bf16[192,512]{1,0:T(8,128)(2,1)S(1)}, bf16[192,512]{1,0:T(8,128)(2,1)S(1)}, u32[]{:S(2)}, u32[]{:S(2)}) collective-permute-start(bf16[192,512]{1,0:T(8,128)(2,1)S(1)} %get-tuple-element.63.refs_1_), channel_id=1, source_target_pairs={{0,2},{1,3},{2,0},{3,1},{4,6},{5,7},{6,4},{7,5},{8,10},{9,11},{10,... | collective-permute-start | bytes 589832 | tf_op jit(solution)/shard_map/ppermute | solution.py:338
  24.1 0.0 collective-permute-start.6
  24.1 4.2 %collective-permute-done.7.refs_3_ = bf16[192,512]{1,0:T(8,128)(2,1)S(1)} collective-permute-done((bf16[192,512]{1,0:T(8,128)(2,1)S(1)}, bf16[192,512]{1,0:T(8,128)(2,1)S(1)}, u32[]{:S(2)}, u32[]{:S(2)}) %collective-permute-start.7) | collective-permute-done | bytes 196640 | tf_op jit(solution)/shard_map/ppermute | solution.py:338
  28.3 1.4 %collective-permute-done.8.refs_4_ = bf16[192,512]{1,0:T(8,128)(2,1)S(1)} collective-permute-done((bf16[192,512]{1,0:T(8,128)(2,1)S(1)}, bf16[192,512]{1,0:T(8,128)(2,1)S(1)}, u32[]{:S(2)}, u32[]{:S(2)}) %collective-permute-start.8) | collective-permute-done | bytes 196640 | tf_op jit(solution)/shard_map/ppermute | solution.py:338
  29.7 2.4 %all-to-all-done.refs_3_.refs_6_ = bf16[8,80,256]{2,1,0:T(8,128)(2,1)S(1)} async-done(((bf16[8,80,256]{2,1,0:T(8,128)(2,1)}), bf16[8,80,256]{2,1,0:T(8,128)(2,1)S(1)}, u32[]{:S(2)}, u32[]{:S(2)}) %all-to-all-start) | async-done | bytes 327712 | tf_op jit(solution)/shard_map/all_to_all | solution.py:858
  32.1 1.4 %collective-permute-start.9 = (bf16[8,32,256]{2,1,0:T(8,128)(2,1)S(1)}, bf16[8,32,256]{2,1,0:T(8,128)(2,1)S(1)}, u32[]{:S(2)}, u32[]{:S(2)}) collective-permute-start(bf16[8,32,256]{2,1,0:T(8,128)(2,1)S(1)} %slice.3.refs_2_), channel_id=1, source_target_pairs={{0,2},{1,3},{2,0},{3,1},{4,6},{5,7},{6,4},{7,5},{8,10},{9,11},{10,... | collective-permute-start | bytes 393224 | tf_op jit(solution)/shard_map/ppermute | solution.py:338
  33.5 1.5 %halo.1 = (bf16[4,32,512]{2,1,0:T(8,128)(2,1)S(1)}, bf16[1,288,128]{2,1,0:T(8,128)(2,1)S(1)}) custom-call(s32[1]{0:T(128)} %bitcast.1.refs_0_, s32[4,26]{1,0:T(4,128)S(1)} %copy-done.8, s32[1,128]{1,0:T(1,128)S(1)} %get-tuple-element.55.refs_2_, bf16[8,80,256]{2,1,0:T(8,128)(2,1)S(1)} %all-to-all-done.refs_3_.refs_6_), custom_call_target="tpu_custom_call" | custom-call | tf_op jit(solution)/shard_map/halo/pallas_call | solution.py:418
  34.9 2.2 %collective-permute-done.9.refs_4_ = bf16[8,32,256]{2,1,0:T(8,128)(2,1)S(1)} collective-permute-done((bf16[8,32,256]{2,1,0:T(8,128)(2,1)S(1)}, bf16[8,32,256]{2,1,0:T(8,128)(2,1)S(1)}, u32[]{:S(2)}, u32[]{:S(2)}) %collective-permute-start.9) | collective-permute-done | bytes 131104 | tf_op jit(solution)/shard_map/ppermute | solution.py:338
  37.1 0.0 collective-permute-start.11
  37.1 0.5 collective-permute-start.12
  37.6 1.3 %collective-permute-start.10 = (bf16[4,32,512]{2,1,0:T(8,128)(2,1)S(1)}, bf16[4,32,512]{2,1,0:T(8,128)(2,1)S(1)}, u32[]{:S(2)}, u32[]{:S(2)}) collective-permute-start(bf16[4,32,512]{2,1,0:T(8,128)(2,1)S(1)} %get-tuple-element.67.refs_5_), channel_id=1, source_target_pairs={{0,2},{1,3},{2,0},{3,1},{4,6},{5,7},{6,4},{7,5},{8,10},{9,11},{10,... | collective-permute-start | bytes 393224 | tf_op jit(solution)/shard_map/ppermute | solution.py:338
  38.9 0.0 collective-permute-done.11.refs_3_
  38.9 0.0 collective-permute-done.12.refs_5_
  39.0 0.0 copy-start.1
  39.0 0.0 copy-start.2
  39.0 0.0 copy-start.6
  39.0 0.0 copy-start.13
  39.0 3.8 %coarse.1.refs_1_ = bf16[32,1152]{1,0:T(8,128)(2,1)S(1)} custom-call(s32[1]{0:T(128)} %bitcast.refs_0_, bf16[1,288,128]{2,1,0:T(8,128)(2,1)S(1)} %get-tuple-element.59.refs_1_, bf16[8,32,256]{2,1,0:T(8,128)(2,1)S(1)} %slice.3.refs_2_, bf16[8,32,256]{2,1,0:T(8,128)(2,1)S(1)} %collective-permute-done.11.refs_3_, ...), custom_call_target="tpu_custom_call" | custom-call | flops 452984832 | bytes 2097152 | tf_op jit(solution)/shard_map/coarse/pallas_call | solution.py:601
  42.8 0.2 collective-permute-done.10.refs_7_
  43.0 0.0 collective-permute-start.14
  43.0 0.5 collective-permute-start.15
  43.5 1.3 %collective-permute-start.13 = (bf16[32,1152]{1,0:T(8,128)(2,1)S(1)}, bf16[32,1152]{1,0:T(8,128)(2,1)S(1)}, u32[]{:S(2)}, u32[]{:S(2)}) collective-permute-start(bf16[32,1152]{1,0:T(8,128)(2,1)S(1)} %coarse.1.refs_1_), channel_id=1, source_target_pairs={{0,2},{1,3},{2,0},{3,1},{4,6},{5,7},{6,4},{7,5},{8,10},{9,11},{10,... | collective-permute-start | bytes 221192 | tf_op jit(solution)/shard_map/ppermute | solution.py:338
  44.9 0.0 collective-permute-done.15.refs_8_
  44.9 0.5 frames.1
  45.4 2.5 %collective-permute-done.13.refs_3_ = bf16[32,1152]{1,0:T(8,128)(2,1)S(1)} collective-permute-done((bf16[32,1152]{1,0:T(8,128)(2,1)S(1)}, bf16[32,1152]{1,0:T(8,128)(2,1)S(1)}, u32[]{:S(2)}, u32[]{:S(2)}) %collective-permute-start.13) | collective-permute-done | bytes 73760 | tf_op jit(solution)/shard_map/ppermute | solution.py:338
  47.9 0.5 collective-permute-start.17
  48.4 0.8 %collective-permute-done.16.refs_2_ = bf16[32,1152]{1,0:T(8,128)(2,1)S(1)} collective-permute-done((bf16[32,1152]{1,0:T(8,128)(2,1)S(1)}, bf16[32,1152]{1,0:T(8,128)(2,1)S(1)}, u32[]{:S(2)}, u32[]{:S(2)}) %collective-permute-start.16) | collective-permute-done | bytes 73760 | tf_op jit(solution)/shard_map/ppermute | solution.py:338
  49.1 0.2 collective-permute-done.17.refs_4_
  49.3 3.9 %refine.1 = bf16[4,32,512]{2,1,0:T(8,128)(2,1)} custom-call(s32[1]{0:T(128)} %bitcast.refs_0_, bf16[32,1152]{1,0:T(8,128)(2,1)S(1)} %coarse.1.refs_1_, bf16[32,1152]{1,0:T(8,128)(2,1)S(1)} %collective-permute-done.16.refs_2_, bf16[32,1152]{1,0:T(8,128)(2,1)S(1)} %collective-permute-done.13.refs_3_, bf16[32,1152]{1,0:T(8,128)(2,1)S(1)} %collective-permute-done.17.refs_4_, ...), custom_call_target="tpu_custom_call" | custom-call | flops 452984832 | bytes 4194304 | tf_op jit(solution)/shard_map/refine/pallas_call | solution.py:790
  (31 shorter events, 0.1 us)
Async XLA Ops:
  0.0 16.1 %copy-start.9 = (s32[2,16,128]{2,1,0:T(8,128)S(1)}, s32[2,16,128]{2,1,0:T(8,128)}, u32[]{:S(2)}) copy-start(s32[2,16,128]{2,1,0:T(8,128)} %constant.22.clone.refs_3_) | copy-start | bytes 49156
  0.0 16.1 %copy-start.11 = (s32[2,128]{1,0:T(2,128)S(1)}, s32[2,128]{1,0:T(2,128)}, u32[]{:S(2)}) copy-start(s32[2,128]{1,0:T(2,128)} %constant.23.clone.refs_11_) | copy-start | bytes 3076
  0.0 8.7 %copy-start.8 = (s32[4,26]{1,0:T(4,128)S(1)}, s32[4,26]{1,0:T(4,128)}, u32[]{:S(2)}) copy-start(s32[4,26]{1,0:T(4,128)} %refs_1_.3) | copy-start | bytes 1252
  0.0 16.1 %copy-start.10 = (s32[2,26]{1,0:T(2,128)S(1)}, s32[2,26]{1,0:T(2,128)}, u32[]{:S(2)}) copy-start(s32[2,26]{1,0:T(2,128)} %refs_1_.2) | copy-start | bytes 628
  0.0 16.1 %copy-start.12 = (s32[4]{0:T(128)S(1)}, s32[4]{0:T(128)}, u32[]{:S(2)}) copy-start(s32[4]{0:T(128)} %refs_2_.2) | copy-start | bytes 52
  0.0 8.6 %collective-permute-start = (s32[1,4,26]{2,1,0:T(4,128)}, s32[1,4,26]{2,1,0:T(4,128)S(1)}, u32[]{:S(2)}, u32[]{:S(2)}) collective-permute-start(s32[1,4,26]{2,1,0:T(4,128)} %bitcast.11), channel_id=1, source_target_pairs={{0,16},{4,20},{8,24},{12,28},{16,0},{20,4},{24,8},{28,12},{1,17},{... | collective-permute-start | bytes 1256 | tf_op jit(solution)/shard_map/ppermute | solution.py:338
  4.1 1.3 %copy-start = (bf16[512,1152]{1,0:T(8,128)(2,1)S(1)}, bf16[512,1152]{1,0:T(8,128)(2,1)}, u32[]{:S(2)}) copy-start(bf16[512,1152]{1,0:T(8,128)(2,1)} %constant.21.clone.refs_2_) | copy-start | bytes 3538948
  5.4 0.9 %copy-start.3 = (bf16[4,32,512]{2,1,0:T(8,128)(2,1)S(1)}, bf16[4,32,512]{2,1,0:T(8,128)(2,1)}, u32[]{:S(2)}) copy-start(bf16[4,32,512]{2,1,0:T(8,128)(2,1)} %param.16) | copy-start | bytes 393220
  6.3 0.8 %copy-start.4 = (bf16[8,128,32]{1,2,0:T(8,128)(2,1)S(1)}, bf16[8,128,32]{1,2,0:T(8,128)(2,1)}, u32[]{:S(2)}) copy-start(bf16[8,128,32]{1,2,0:T(8,128)(2,1)} %param.20) | copy-start | bytes 196612
  7.1 0.8 %copy-start.5 = (bf16[8,32,128]{2,1,0:T(8,128)(2,1)S(1)}, bf16[8,32,128]{2,1,0:T(8,128)(2,1)}, u32[]{:S(2)}) copy-start(bf16[8,32,128]{2,1,0:T(8,128)(2,1)} %param.22) | copy-start | bytes 196612
  8.0 8.1 %copy-start.7 = (bf16[128,128]{1,0:T(8,128)(2,1)S(1)}, bf16[128,128]{1,0:T(8,128)(2,1)}, u32[]{:S(2)}) copy-start(bf16[128,128]{1,0:T(8,128)(2,1)} %constant.24.clone.refs_12_) | copy-start | bytes 98308
  8.0 31.0 %copy-start.14 = (bf16[27,32,128]{2,1,0:T(8,128)(2,1)S(1)}, bf16[27,32,128]{2,1,0:T(8,128)(2,1)}, u32[]{:S(2)}) copy-start(bf16[27,32,128]{2,1,0:T(8,128)(2,1)} %refs_7_.1) | copy-start | bytes 663556
  8.0 31.0 %copy-start.15 = (f32[32]{0:T(128)S(1)}, f32[32]{0:T(128)}, u32[]{:S(2)}) copy-start(f32[32]{0:T(128)} %param.24) | copy-start | bytes 388
  8.7 3.7 %collective-permute-start.1 = (s32[2,4,26]{2,1,0:T(4,128)S(1)}, s32[2,4,26]{2,1,0:T(4,128)S(1)}, u32[]{:S(2)}, u32[]{:S(2)}) collective-permute-start(s32[2,4,26]{2,1,0:T(4,128)S(1)} %pad_add_fusion.1), channel_id=1, source_target_pairs={{0,8},{4,12},{8,0},{12,4},{16,24},{20,28},{24,16},{28,20},{1,9},{5... | collective-permute-start | bytes 2504 | tf_op jit(solution)/shard_map/ppermute | solution.py:338
  10.3 2.0 %collective-permute-start.2 = (bf16[32,256]{1,0:T(8,128)(2,1)S(1)}, bf16[32,256]{1,0:T(8,128)(2,1)S(1)}, u32[]{:S(2)}, u32[]{:S(2)}) collective-permute-start(bf16[32,256]{1,0:T(8,128)(2,1)S(1)} %get-tuple-element.46), channel_id=1, source_target_pairs={{0,1},{1,0},{2,3},{3,2},{4,5},{5,4},{6,7},{7,6},{8,9},{9,8},{10,11... | collective-permute-start | bytes 49160 | tf_op jit(solution)/shard_map/ppermute | solution.py:338
  10.3 3.7 %collective-permute-start.3 = (bf16[32,256]{1,0:T(8,128)(2,1)S(1)}, bf16[32,256]{1,0:T(8,128)(2,1)S(1)}, u32[]{:S(2)}, u32[]{:S(2)}) collective-permute-start(bf16[32,256]{1,0:T(8,128)(2,1)S(1)} %get-tuple-element.48), channel_id=1, source_target_pairs={{0,2},{1,3},{2,0},{3,1},{4,6},{5,7},{6,4},{7,5},{8,10},{9,11},{10,... | collective-permute-start | bytes 49160 | tf_op jit(solution)/shard_map/ppermute | solution.py:338
  11.9 3.2 %collective-permute-start.4 = (bf16[32,256]{1,0:T(8,128)(2,1)S(1)}, bf16[32,256]{1,0:T(8,128)(2,1)S(1)}, u32[]{:S(2)}, u32[]{:S(2)}) collective-permute-start(bf16[32,256]{1,0:T(8,128)(2,1)S(1)} %get-tuple-element.49), channel_id=1, source_target_pairs={{0,3},{1,2},{2,1},{3,0},{4,7},{5,6},{6,5},{7,4},{8,11},{9,10},{10,... | collective-permute-start | bytes 49160 | tf_op jit(solution)/shard_map/ppermute | solution.py:338
  12.4 3.7 %collective-permute-start.5 = (s32[4,4,26]{2,1,0:T(4,128)S(1)}, s32[4,4,26]{2,1,0:T(4,128)S(1)}, u32[]{:S(2)}, u32[]{:S(2)}) collective-permute-start(s32[4,4,26]{2,1,0:T(4,128)S(1)} %pad_add_fusion.refs_8_), channel_id=1, source_target_pairs={{0,4},{4,0},{8,12},{12,8},{16,20},{20,16},{24,28},{28,24},{1,5},{5... | collective-permute-start | bytes 5000 | tf_op jit(solution)/shard_map/ppermute | solution.py:338
  18.8 13.3 %all-to-all-start = ((bf16[8,80,256]{2,1,0:T(8,128)(2,1)}), bf16[8,80,256]{2,1,0:T(8,128)(2,1)S(1)}, u32[]{:S(2)}, u32[]{:S(2)}) async-start(bf16[8,80,256]{2,1,0:T(8,128)(2,1)} %get-tuple-element.52), calls=%async_computation | async-start | bytes 655360 | tf_op jit(solution)/shard_map/all_to_all | solution.py:858
  22.6 5.7 %collective-permute-start.7 = (bf16[192,512]{1,0:T(8,128)(2,1)S(1)}, bf16[192,512]{1,0:T(8,128)(2,1)S(1)}, u32[]{:S(2)}, u32[]{:S(2)}) collective-permute-start(bf16[192,512]{1,0:T(8,128)(2,1)S(1)} %get-tuple-element.63.refs_1_), channel_id=1, source_target_pairs={{0,2},{1,3},{2,0},{3,1},{4,6},{5,7},{6,4},{7,5},{8,10},{9,11},{10,... | collective-permute-start | bytes 589832 | tf_op jit(solution)/shard_map/ppermute | solution.py:338
  24.1 4.2 %collective-permute-start.6 = (bf16[192,512]{1,0:T(8,128)(2,1)S(1)}, bf16[192,512]{1,0:T(8,128)(2,1)S(1)}, u32[]{:S(2)}, u32[]{:S(2)}) collective-permute-start(bf16[192,512]{1,0:T(8,128)(2,1)S(1)} %get-tuple-element.63.refs_1_), channel_id=1, source_target_pairs={{0,1},{1,0},{2,3},{3,2},{4,5},{5,4},{6,7},{7,6},{8,9},{9,8},{10,11... | collective-permute-start | bytes 589832 | tf_op jit(solution)/shard_map/ppermute | solution.py:338
  28.3 1.4 %collective-permute-start.8 = (bf16[192,512]{1,0:T(8,128)(2,1)S(1)}, bf16[192,512]{1,0:T(8,128)(2,1)S(1)}, u32[]{:S(2)}, u32[]{:S(2)}) collective-permute-start(bf16[192,512]{1,0:T(8,128)(2,1)S(1)} %collective-permute-done.7.refs_3_), channel_id=1, source_target_pairs={{0,1},{1,0},{2,3},{3,2},{4,5},{5,4},{6,7},{7,6},{8,9},{9,8},{10,11... | collective-permute-start | bytes 589832 | tf_op jit(solution)/shard_map/ppermute | solution.py:338
  32.1 5.0 %collective-permute-start.9 = (bf16[8,32,256]{2,1,0:T(8,128)(2,1)S(1)}, bf16[8,32,256]{2,1,0:T(8,128)(2,1)S(1)}, u32[]{:S(2)}, u32[]{:S(2)}) collective-permute-start(bf16[8,32,256]{2,1,0:T(8,128)(2,1)S(1)} %slice.3.refs_2_), channel_id=1, source_target_pairs={{0,2},{1,3},{2,0},{3,1},{4,6},{5,7},{6,4},{7,5},{8,10},{9,11},{10,... | collective-permute-start | bytes 393224 | tf_op jit(solution)/shard_map/ppermute | solution.py:338
  37.1 1.8 %collective-permute-start.11 = (bf16[8,32,256]{2,1,0:T(8,128)(2,1)S(1)}, bf16[8,32,256]{2,1,0:T(8,128)(2,1)S(1)}, u32[]{:S(2)}, u32[]{:S(2)}) collective-permute-start(bf16[8,32,256]{2,1,0:T(8,128)(2,1)S(1)} %slice.3.refs_2_), channel_id=1, source_target_pairs={{0,1},{1,0},{2,3},{3,2},{4,5},{5,4},{6,7},{7,6},{8,9},{9,8},{10,11... | collective-permute-start | bytes 393224 | tf_op jit(solution)/shard_map/ppermute | solution.py:338
  37.1 1.8 %collective-permute-start.12 = (bf16[8,32,256]{2,1,0:T(8,128)(2,1)S(1)}, bf16[8,32,256]{2,1,0:T(8,128)(2,1)S(1)}, u32[]{:S(2)}, u32[]{:S(2)}) collective-permute-start(bf16[8,32,256]{2,1,0:T(8,128)(2,1)S(1)} %collective-permute-done.9.refs_4_), channel_id=1, source_target_pairs={{0,1},{1,0},{2,3},{3,2},{4,5},{5,4},{6,7},{7,6},{8,9},{9,8},{10,11... | collective-permute-start | bytes 393224 | tf_op jit(solution)/shard_map/ppermute | solution.py:338
  37.6 5.4 %collective-permute-start.10 = (bf16[4,32,512]{2,1,0:T(8,128)(2,1)S(1)}, bf16[4,32,512]{2,1,0:T(8,128)(2,1)S(1)}, u32[]{:S(2)}, u32[]{:S(2)}) collective-permute-start(bf16[4,32,512]{2,1,0:T(8,128)(2,1)S(1)} %get-tuple-element.67.refs_5_), channel_id=1, source_target_pairs={{0,2},{1,3},{2,0},{3,1},{4,6},{5,7},{6,4},{7,5},{8,10},{9,11},{10,... | collective-permute-start | bytes 393224 | tf_op jit(solution)/shard_map/ppermute | solution.py:338
  39.0 10.4 %copy-start.1 = (bf16[27,32,128]{2,1,0:T(8,128)(2,1)S(1)}, bf16[27,32,128]{2,1,0:T(8,128)(2,1)}, u32[]{:S(2)}) copy-start(bf16[27,32,128]{2,1,0:T(8,128)(2,1)} %refs_8_.1) | copy-start | bytes 663556
  39.0 10.3 %copy-start.2 = (bf16[256,256]{1,0:T(8,128)(2,1)S(1)}, bf16[256,256]{1,0:T(8,128)(2,1)}, u32[]{:S(2)}) copy-start(bf16[256,256]{1,0:T(8,128)(2,1)} %constant.26.clone.refs_10_) | copy-start | bytes 393220
  39.0 10.3 %copy-start.6 = (bf16[192,128]{1,0:T(8,128)(2,1)S(1)}, bf16[192,128]{1,0:T(8,128)(2,1)}, u32[]{:S(2)}) copy-start(bf16[192,128]{1,0:T(8,128)(2,1)} %constant.25.clone.refs_6_) | copy-start | bytes 147460
  39.0 10.3 %copy-start.13 = (f32[32]{0:T(128)S(1)}, f32[32]{0:T(128)}, u32[]{:S(2)}) copy-start(f32[32]{0:T(128)} %param.25) | copy-start | bytes 388
  43.0 1.8 %collective-permute-start.14 = (bf16[4,32,512]{2,1,0:T(8,128)(2,1)S(1)}, bf16[4,32,512]{2,1,0:T(8,128)(2,1)S(1)}, u32[]{:S(2)}, u32[]{:S(2)}) collective-permute-start(bf16[4,32,512]{2,1,0:T(8,128)(2,1)S(1)} %get-tuple-element.67.refs_5_), channel_id=1, source_target_pairs={{0,1},{1,0},{2,3},{3,2},{4,5},{5,4},{6,7},{7,6},{8,9},{9,8},{10,11... | collective-permute-start | bytes 393224 | tf_op jit(solution)/shard_map/ppermute | solution.py:338
  43.0 1.8 %collective-permute-start.15 = (bf16[4,32,512]{2,1,0:T(8,128)(2,1)S(1)}, bf16[4,32,512]{2,1,0:T(8,128)(2,1)S(1)}, u32[]{:S(2)}, u32[]{:S(2)}) collective-permute-start(bf16[4,32,512]{2,1,0:T(8,128)(2,1)S(1)} %collective-permute-done.10.refs_7_), channel_id=1, source_target_pairs={{0,1},{1,0},{2,3},{3,2},{4,5},{5,4},{6,7},{7,6},{8,9},{9,8},{10,11... | collective-permute-start | bytes 393224 | tf_op jit(solution)/shard_map/ppermute | solution.py:338
  43.5 4.4 %collective-permute-start.13 = (bf16[32,1152]{1,0:T(8,128)(2,1)S(1)}, bf16[32,1152]{1,0:T(8,128)(2,1)S(1)}, u32[]{:S(2)}, u32[]{:S(2)}) collective-permute-start(bf16[32,1152]{1,0:T(8,128)(2,1)S(1)} %coarse.1.refs_1_), channel_id=1, source_target_pairs={{0,2},{1,3},{2,0},{3,1},{4,6},{5,7},{6,4},{7,5},{8,10},{9,11},{10,... | collective-permute-start | bytes 221192 | tf_op jit(solution)/shard_map/ppermute | solution.py:338
  47.9 1.3 %collective-permute-start.16 = (bf16[32,1152]{1,0:T(8,128)(2,1)S(1)}, bf16[32,1152]{1,0:T(8,128)(2,1)S(1)}, u32[]{:S(2)}, u32[]{:S(2)}) collective-permute-start(bf16[32,1152]{1,0:T(8,128)(2,1)S(1)} %coarse.1.refs_1_), channel_id=1, source_target_pairs={{0,1},{1,0},{2,3},{3,2},{4,5},{5,4},{6,7},{7,6},{8,9},{9,8},{10,11... | collective-permute-start | bytes 221192 | tf_op jit(solution)/shard_map/ppermute | solution.py:338
  47.9 1.4 %collective-permute-start.17 = (bf16[32,1152]{1,0:T(8,128)(2,1)S(1)}, bf16[32,1152]{1,0:T(8,128)(2,1)S(1)}, u32[]{:S(2)}, u32[]{:S(2)}) collective-permute-start(bf16[32,1152]{1,0:T(8,128)(2,1)S(1)} %collective-permute-done.13.refs_3_), channel_id=1, source_target_pairs={{0,1},{1,0},{2,3},{3,2},{4,5},{5,4},{6,7},{7,6},{8,9},{9,8},{10,11... | collective-permute-start | bytes 221192 | tf_op jit(solution)/shard_map/ppermute | solution.py:338

commit v6 on v5

--- a/solution.py
+++ b/solution.py
@@ -863,11 +863,8 @@
         chans,
         lambda: halo(owner[None], fine_links, places, recv, q, fine, q, vox),
     )
-    halos, co = relayed(
-        around,
-        chans,
-        lambda: coarse(me[None], pickers, slots, recv, codes, coarse_weight, coarse_bias[None]),
-    )
+    halos = exchanged(around, chans)
+    co = coarse(me[None], pickers, slots, recv, codes, coarse_weight, coarse_bias[None])
     cos, (ff, up_all) = relayed(co, chans, lambda: frames(me[None], packs, halos))
     return refine(me[None], cos, ff, up_all, fine_weight, fine_bias[None])
 

time: 53.6 us -> 53.5 us (level)
  no operation moved by 1% of the time
where the time goes in v6:
time: 53.5 us; the launch traced here: 53.2 us
  starting transfers between devices  20.1 us (38%)
  waiting for transfers between devices  16 us (30%)
  Pallas kernels  13 us (24%)
  local copies, waits for them, and re-layouts  3.92 us (7%)
    ppermute x18, starting transfers between devices, partner(): return lax.ppermute(x, axis, [(i, i ^ step) for i in range(count)])  16.3 us
    ppermute x18, waiting for transfers between devices, partner(): return lax.ppermute(x, axis, [(i, i ^ step) for i in range(count)])  13.6 us
    pallas_call x1, Pallas kernels, refine(): pl.pallas_call(lambda *refs: fine_kernel(chans, *refs), out_shape=jax.Sha...  3.94 us
    unnamed x32, local copies, waits for them, and re-layouts  3.91 us
    all_to_all x1, starting transfers between devices, per_device(): lax.all_to_all(sending, 'brick', split_axis=0, concat_axis=0, tiled=True)  3.79 us
    pallas_call x1, Pallas kernels, coarse(): pl.pallas_call(lambda *refs: coarse_kernel(chans, codes, *refs), out_shap...  3.77 us
    pallas_call x1, Pallas kernels, assemble(): pl.pallas_call(lambda *refs: assemble_kernel(len(slots), len(asked), fine...  2.63 us
    all_to_all x1, waiting for transfers between devices, per_device(): lax.all_to_all(sending, 'brick', split_axis=0, concat_axis=0, tiled=True)  2.35 us
  transfers between devices with their start and end apart: 19, of which 12 were waited for; matrix products, arithmetic and copies ran while one was open for 0% of the time, Pallas kernels for 12%

profile of v6, /device:TPU:0, one launch (start us, length us, event | category | flops | bytes accessed | tf_op | source)
XLA Modules:
  0.0 53.2 jit_solution(3514073815525275337)
XLA Ops:
  0.0 4.1 %collective-permute-start = (s32[1,4,26]{2,1,0:T(4,128)}, s32[1,4,26]{2,1,0:T(4,128)S(1)}, u32[]{:S(2)}, u32[]{:S(2)}) collective-permute-start(s32[1,4,26]{2,1,0:T(4,128)} %bitcast.11), channel_id=1, source_target_pairs={{0,16},{4,20},{8,24},{12,28},{16,0},{20,4},{24,8},{28,12},{1,17},{... | collective-permute-start | bytes 1256 | tf_op jit(solution)/shard_map/ppermute | solution.py:338
  4.1 1.3 %copy-done = bf16[512,1152]{1,0:T(8,128)(2,1)S(1)} copy-done((bf16[512,1152]{1,0:T(8,128)(2,1)S(1)}, bf16[512,1152]{1,0:T(8,128)(2,1)}, u32[]{:S(2)}) %copy-start) | copy-done | bytes 1179672
  5.4 0.9 %copy-done.3 = bf16[4,32,512]{2,1,0:T(8,128)(2,1)S(1)} copy-done((bf16[4,32,512]{2,1,0:T(8,128)(2,1)S(1)}, bf16[4,32,512]{2,1,0:T(8,128)(2,1)}, u32[]{:S(2)}) %copy-start.3) | copy-done | bytes 131096
  6.3 0.8 %copy-done.4 = bf16[8,128,32]{1,2,0:T(8,128)(2,1)S(1)} copy-done((bf16[8,128,32]{1,2,0:T(8,128)(2,1)S(1)}, bf16[8,128,32]{1,2,0:T(8,128)(2,1)}, u32[]{:S(2)}) %copy-start.4) | copy-done | bytes 65560
  7.1 0.8 %copy-done.5 = bf16[8,32,128]{2,1,0:T(8,128)(2,1)S(1)} copy-done((bf16[8,32,128]{2,1,0:T(8,128)(2,1)S(1)}, bf16[8,32,128]{2,1,0:T(8,128)(2,1)}, u32[]{:S(2)}) %copy-start.5) | copy-done | bytes 65560
  8.0 0.7 %project.1 = (bf16[32,256]{1,0:T(8,128)(2,1)S(1)}, bf16[32,256]{1,0:T(8,128)(2,1)S(1)}, bf16[32,256]{1,0:T(8,128)(2,1)S(1)}, bf16[32,256]{1,0:T(8,128)(2,1)S(1)}...) custom-call(s32[1]{0:T(128)} %bitcast.refs_0_, bf16[128,512]{1,0:T(8,128)(2,1)S(1)} %bitcast.8, ...), custom_call_target="tpu_custom_call" | custom-call | tf_op jit(solution)/shard_map/project/pallas_call | solution.py:176
  8.7 0.0 collective-permute-done
  8.7 1.6 %collective-permute-start.1 = (s32[2,4,26]{2,1,0:T(4,128)S(1)}, s32[2,4,26]{2,1,0:T(4,128)S(1)}, u32[]{:S(2)}, u32[]{:S(2)}) collective-permute-start(s32[2,4,26]{2,1,0:T(4,128)S(1)} %pad_add_fusion.1), channel_id=1, source_target_pairs={{0,8},{4,12},{8,0},{12,4},{16,24},{20,28},{24,16},{28,20},{1,9},{5... | collective-permute-start | bytes 2504 | tf_op jit(solution)/shard_map/ppermute | solution.py:338
  10.3 0.0 collective-permute-start.2
  10.3 1.5 %collective-permute-start.3 = (bf16[32,256]{1,0:T(8,128)(2,1)S(1)}, bf16[32,256]{1,0:T(8,128)(2,1)S(1)}, u32[]{:S(2)}, u32[]{:S(2)}) collective-permute-start(bf16[32,256]{1,0:T(8,128)(2,1)S(1)} %get-tuple-element.45), channel_id=1, source_target_pairs={{0,2},{1,3},{2,0},{3,1},{4,6},{5,7},{6,4},{7,5},{8,10},{9,11},{10,... | collective-permute-start | bytes 49160 | tf_op jit(solution)/shard_map/ppermute | solution.py:338
  11.9 0.3 collective-permute-start.4
  12.2 0.2 collective-permute-done.1
  12.4 0.0 collective-permute-done.2.refs_5_
  12.4 1.6 %collective-permute-start.5 = (s32[4,4,26]{2,1,0:T(4,128)S(1)}, s32[4,4,26]{2,1,0:T(4,128)S(1)}, u32[]{:S(2)}, u32[]{:S(2)}) collective-permute-start(s32[4,4,26]{2,1,0:T(4,128)S(1)} %pad_add_fusion.refs_8_), channel_id=1, source_target_pairs={{0,4},{4,0},{8,12},{12,8},{16,20},{20,16},{24,28},{28,24},{1,5},{5... | collective-permute-start | bytes 5000 | tf_op jit(solution)/shard_map/ppermute | solution.py:338
  13.9 0.1 collective-permute-done.3.refs_6_
  14.1 0.9 %collective-permute-done.4.refs_7_ = bf16[32,256]{1,0:T(8,128)(2,1)S(1)} collective-permute-done((bf16[32,256]{1,0:T(8,128)(2,1)S(1)}, bf16[32,256]{1,0:T(8,128)(2,1)S(1)}, u32[]{:S(2)}, u32[]{:S(2)}) %collective-permute-start.4) | collective-permute-done | bytes 16416 | tf_op jit(solution)/shard_map/ppermute | solution.py:338
  15.0 1.1 %collective-permute-done.5.refs_9_ = s32[4,4,26]{2,1,0:T(4,128)S(1)} collective-permute-done((s32[4,4,26]{2,1,0:T(4,128)S(1)}, s32[4,4,26]{2,1,0:T(4,128)S(1)}, u32[]{:S(2)}, u32[]{:S(2)}) %collective-permute-start.5) | collective-permute-done | bytes 1696 | tf_op jit(solution)/shard_map/ppermute | solution.py:338
  16.1 2.6 %assemble.1 = (bf16[8,80,256]{2,1,0:T(8,128)(2,1)}, s32[1,128]{1,0:T(1,128)S(1)}) custom-call(s32[1]{0:T(128)} %bitcast.1.refs_0_, s32[2,26]{1,0:T(2,128)S(1)} %copy-done.10, s32[4]{0:T(128)S(1)} %copy-done.12, s32[2,16,128]{2,1,0:T(8,128)S(1)} %copy-done.9, bf16[32,256]{1,0:T(8,128)(2,1)S(1)} %get-tuple-element.41.refs_4_, ...), custom_call_target="tpu_custom_call" | custom-call | flops 1048576 | bytes 12582912 | tf_op jit(solution)/shard_map/assemble/pallas_call | solution.py:315
  18.8 3.8 %all-to-all-start = ((bf16[8,80,256]{2,1,0:T(8,128)(2,1)}), bf16[8,80,256]{2,1,0:T(8,128)(2,1)S(1)}, u32[]{:S(2)}, u32[]{:S(2)}) async-start(bf16[8,80,256]{2,1,0:T(8,128)(2,1)} %get-tuple-element.49), calls=%async_computation | async-start | bytes 655360 | tf_op jit(solution)/shard_map/all_to_all | solution.py:858
  22.6 1.5 %collective-permute-start.7 = (bf16[192,512]{1,0:T(8,128)(2,1)S(1)}, bf16[192,512]{1,0:T(8,128)(2,1)S(1)}, u32[]{:S(2)}, u32[]{:S(2)}) collective-permute-start(bf16[192,512]{1,0:T(8,128)(2,1)S(1)} %get-tuple-element.58.refs_1_), channel_id=1, source_target_pairs={{0,2},{1,3},{2,0},{3,1},{4,6},{5,7},{6,4},{7,5},{8,10},{9,11},{10,... | collective-permute-start | bytes 589832 | tf_op jit(solution)/shard_map/ppermute | solution.py:338
  24.1 0.0 collective-permute-start.6
  24.1 4.2 %collective-permute-done.7.refs_3_ = bf16[192,512]{1,0:T(8,128)(2,1)S(1)} collective-permute-done((bf16[192,512]{1,0:T(8,128)(2,1)S(1)}, bf16[192,512]{1,0:T(8,128)(2,1)S(1)}, u32[]{:S(2)}, u32[]{:S(2)}) %collective-permute-start.7) | collective-permute-done | bytes 196640 | tf_op jit(solution)/shard_map/ppermute | solution.py:338
  28.3 0.0 collective-permute-start.8
  28.3 0.0 collective-permute-done.6.refs_2_
  28.3 1.4 %collective-permute-done.8.refs_4_ = bf16[192,512]{1,0:T(8,128)(2,1)S(1)} collective-permute-done((bf16[192,512]{1,0:T(8,128)(2,1)S(1)}, bf16[192,512]{1,0:T(8,128)(2,1)S(1)}, u32[]{:S(2)}, u32[]{:S(2)}) %collective-permute-start.8) | collective-permute-done | bytes 196640 | tf_op jit(solution)/shard_map/ppermute | solution.py:338
  29.7 2.4 %all-to-all-done.refs_3_.refs_6_ = bf16[8,80,256]{2,1,0:T(8,128)(2,1)S(1)} async-done(((bf16[8,80,256]{2,1,0:T(8,128)(2,1)}), bf16[8,80,256]{2,1,0:T(8,128)(2,1)S(1)}, u32[]{:S(2)}, u32[]{:S(2)}) %all-to-all-start) | async-done | bytes 327712 | tf_op jit(solution)/shard_map/all_to_all | solution.py:858
  32.1 1.4 %collective-permute-start.9 = (bf16[8,32,256]{2,1,0:T(8,128)(2,1)S(1)}, bf16[8,32,256]{2,1,0:T(8,128)(2,1)S(1)}, u32[]{:S(2)}, u32[]{:S(2)}) collective-permute-start(bf16[8,32,256]{2,1,0:T(8,128)(2,1)S(1)} %slice.3.refs_2_), channel_id=1, source_target_pairs={{0,2},{1,3},{2,0},{3,1},{4,6},{5,7},{6,4},{7,5},{8,10},{9,11},{10,... | collective-permute-start | bytes 393224 | tf_op jit(solution)/shard_map/ppermute | solution.py:338
  33.5 1.5 %halo.1 = (bf16[4,32,512]{2,1,0:T(8,128)(2,1)S(1)}, bf16[1,288,128]{2,1,0:T(8,128)(2,1)S(1)}) custom-call(s32[1]{0:T(128)} %bitcast.1.refs_0_, s32[4,26]{1,0:T(4,128)S(1)} %copy-done.8, s32[1,128]{1,0:T(1,128)S(1)} %get-tuple-element.52.refs_2_, bf16[8,80,256]{2,1,0:T(8,128)(2,1)S(1)} %all-to-all-done.refs_3_.refs_6_), custom_call_target="tpu_custom_call" | custom-call | tf_op jit(solution)/shard_map/halo/pallas_call | solution.py:418
  34.9 2.2 %collective-permute-done.9.refs_4_ = bf16[8,32,256]{2,1,0:T(8,128)(2,1)S(1)} collective-permute-done((bf16[8,32,256]{2,1,0:T(8,128)(2,1)S(1)}, bf16[8,32,256]{2,1,0:T(8,128)(2,1)S(1)}, u32[]{:S(2)}, u32[]{:S(2)}) %collective-permute-start.9) | collective-permute-done | bytes 131104 | tf_op jit(solution)/shard_map/ppermute | solution.py:338
  37.1 0.0 collective-permute-start.10
  37.1 0.5 collective-permute-start.11
  37.6 0.9 %collective-permute-start.15 = (bf16[4,32,512]{2,1,0:T(8,128)(2,1)S(1)}, bf16[4,32,512]{2,1,0:T(8,128)(2,1)S(1)}, u32[]{:S(2)}, u32[]{:S(2)}) collective-permute-start(bf16[4,32,512]{2,1,0:T(8,128)(2,1)S(1)} %get-tuple-element.62.refs_5_), channel_id=1, source_target_pairs={{0,3},{1,2},{2,1},{3,0},{4,7},{5,6},{6,5},{7,4},{8,11},{9,10},{10,... | collective-permute-start | bytes 393224 | tf_op jit(solution)/shard_map/ppermute | solution.py:338
  38.5 0.7 %collective-permute-start.14 = (bf16[4,32,512]{2,1,0:T(8,128)(2,1)S(1)}, bf16[4,32,512]{2,1,0:T(8,128)(2,1)S(1)}, u32[]{:S(2)}, u32[]{:S(2)}) collective-permute-start(bf16[4,32,512]{2,1,0:T(8,128)(2,1)S(1)} %get-tuple-element.62.refs_5_), channel_id=1, source_target_pairs={{0,2},{1,3},{2,0},{3,1},{4,6},{5,7},{6,4},{7,5},{8,10},{9,11},{10,... | collective-permute-start | bytes 393224 | tf_op jit(solution)/shard_map/ppermute | solution.py:338
  39.2 0.2 collective-permute-start.13
  39.5 0.0 collective-permute-done.11.refs_5_
  39.5 0.0 copy-start.1
  39.5 0.0 copy-start.2
  39.5 0.0 copy-start.6
  39.5 0.0 copy-start.13
  39.5 3.8 %coarse.1.refs_1_ = bf16[32,1152]{1,0:T(8,128)(2,1)S(1)} custom-call(s32[1]{0:T(128)} %bitcast.refs_0_, bf16[1,288,128]{2,1,0:T(8,128)(2,1)S(1)} %get-tuple-element.55.refs_1_, bf16[8,32,256]{2,1,0:T(8,128)(2,1)S(1)} %slice.3.refs_2_, bf16[8,32,256]{2,1,0:T(8,128)(2,1)S(1)} %collective-permute-done.10.refs_3_, ...), custom_call_target="tpu_custom_call" | custom-call | flops 452984832 | bytes 2097152 | tf_op jit(solution)/shard_map/coarse/pallas_call | solution.py:601
  43.3 1.4 %collective-permute-start.12 = (bf16[32,1152]{1,0:T(8,128)(2,1)S(1)}, bf16[32,1152]{1,0:T(8,128)(2,1)S(1)}, u32[]{:S(2)}, u32[]{:S(2)}) collective-permute-start(bf16[32,1152]{1,0:T(8,128)(2,1)S(1)} %coarse.1.refs_1_), channel_id=1, source_target_pairs={{0,2},{1,3},{2,0},{3,1},{4,6},{5,7},{6,4},{7,5},{8,10},{9,11},{10,... | collective-permute-start | bytes 221192 | tf_op jit(solution)/shard_map/ppermute | solution.py:338
  44.7 1.5 %collective-permute-done.14.refs_7_ = bf16[4,32,512]{2,1,0:T(8,128)(2,1)S(1)} collective-permute-done((bf16[4,32,512]{2,1,0:T(8,128)(2,1)S(1)}, bf16[4,32,512]{2,1,0:T(8,128)(2,1)S(1)}, u32[]{:S(2)}, u32[]{:S(2)}) %collective-permute-start.14) | collective-permute-done | bytes 131104 | tf_op jit(solution)/shard_map/ppermute | solution.py:338
  46.2 0.5 frames.1
  46.8 1.1 %collective-permute-done.12.refs_3_ = bf16[32,1152]{1,0:T(8,128)(2,1)S(1)} collective-permute-done((bf16[32,1152]{1,0:T(8,128)(2,1)S(1)}, bf16[32,1152]{1,0:T(8,128)(2,1)S(1)}, u32[]{:S(2)}, u32[]{:S(2)}) %collective-permute-start.12) | collective-permute-done | bytes 73760 | tf_op jit(solution)/shard_map/ppermute | solution.py:338
  47.8 0.5 collective-permute-start.17
  48.3 0.8 %collective-permute-done.16.refs_2_ = bf16[32,1152]{1,0:T(8,128)(2,1)S(1)} collective-permute-done((bf16[32,1152]{1,0:T(8,128)(2,1)S(1)}, bf16[32,1152]{1,0:T(8,128)(2,1)S(1)}, u32[]{:S(2)}, u32[]{:S(2)}) %collective-permute-start.16) | collective-permute-done | bytes 73760 | tf_op jit(solution)/shard_map/ppermute | solution.py:338
  49.1 0.2 collective-permute-done.17.refs_4_
  49.3 3.9 %refine.1 = bf16[4,32,512]{2,1,0:T(8,128)(2,1)} custom-call(s32[1]{0:T(128)} %bitcast.refs_0_, bf16[32,1152]{1,0:T(8,128)(2,1)S(1)} %coarse.1.refs_1_, bf16[32,1152]{1,0:T(8,128)(2,1)S(1)} %collective-permute-done.16.refs_2_, bf16[32,1152]{1,0:T(8,128)(2,1)S(1)} %collective-permute-done.12.refs_3_, bf16[32,1152]{1,0:T(8,128)(2,1)S(1)} %collective-permute-done.17.refs_4_, ...), custom_call_target="tpu_custom_call" | custom-call | flops 452984832 | bytes 4194304 | tf_op jit(solution)/shard_map/refine/pallas_call | solution.py:790
  (31 shorter events, 0.1 us)
Async XLA Ops:
  0.0 16.1 %copy-start.11 = (s32[2,128]{1,0:T(2,128)S(1)}, s32[2,128]{1,0:T(2,128)}, u32[]{:S(2)}) copy-start(s32[2,128]{1,0:T(2,128)} %constant.23.clone.refs_11_) | copy-start | bytes 3076
  0.0 16.1 %copy-start.9 = (s32[2,16,128]{2,1,0:T(8,128)S(1)}, s32[2,16,128]{2,1,0:T(8,128)}, u32[]{:S(2)}) copy-start(s32[2,16,128]{2,1,0:T(8,128)} %constant.22.clone.refs_3_) | copy-start | bytes 49156
  0.0 8.7 %copy-start.8 = (s32[4,26]{1,0:T(4,128)S(1)}, s32[4,26]{1,0:T(4,128)}, u32[]{:S(2)}) copy-start(s32[4,26]{1,0:T(4,128)} %refs_1_.3) | copy-start | bytes 1252
  0.0 16.1 %copy-start.12 = (s32[4]{0:T(128)S(1)}, s32[4]{0:T(128)}, u32[]{:S(2)}) copy-start(s32[4]{0:T(128)} %refs_2_.2) | copy-start | bytes 52
  0.0 8.7 %collective-permute-start = (s32[1,4,26]{2,1,0:T(4,128)}, s32[1,4,26]{2,1,0:T(4,128)S(1)}, u32[]{:S(2)}, u32[]{:S(2)}) collective-permute-start(s32[1,4,26]{2,1,0:T(4,128)} %bitcast.11), channel_id=1, source_target_pairs={{0,16},{4,20},{8,24},{12,28},{16,0},{20,4},{24,8},{28,12},{1,17},{... | collective-permute-start | bytes 1256 | tf_op jit(solution)/shard_map/ppermute | solution.py:338
  4.1 1.3 %copy-start = (bf16[512,1152]{1,0:T(8,128)(2,1)S(1)}, bf16[512,1152]{1,0:T(8,128)(2,1)}, u32[]{:S(2)}) copy-start(bf16[512,1152]{1,0:T(8,128)(2,1)} %constant.21.clone.refs_2_) | copy-start | bytes 3538948
  5.4 0.9 %copy-start.3 = (bf16[4,32,512]{2,1,0:T(8,128)(2,1)S(1)}, bf16[4,32,512]{2,1,0:T(8,128)(2,1)}, u32[]{:S(2)}) copy-start(bf16[4,32,512]{2,1,0:T(8,128)(2,1)} %param.16) | copy-start | bytes 393220
  6.3 0.8 %copy-start.4 = (bf16[8,128,32]{1,2,0:T(8,128)(2,1)S(1)}, bf16[8,128,32]{1,2,0:T(8,128)(2,1)}, u32[]{:S(2)}) copy-start(bf16[8,128,32]{1,2,0:T(8,128)(2,1)} %param.20) | copy-start | bytes 196612
  7.1 0.8 %copy-start.5 = (bf16[8,32,128]{2,1,0:T(8,128)(2,1)S(1)}, bf16[8,32,128]{2,1,0:T(8,128)(2,1)}, u32[]{:S(2)}) copy-start(bf16[8,32,128]{2,1,0:T(8,128)(2,1)} %param.22) | copy-start | bytes 196612
  8.0 8.1 %copy-start.7 = (bf16[128,128]{1,0:T(8,128)(2,1)S(1)}, bf16[128,128]{1,0:T(8,128)(2,1)}, u32[]{:S(2)}) copy-start(bf16[128,128]{1,0:T(8,128)(2,1)} %constant.24.clone.refs_12_) | copy-start | bytes 98308
  8.0 8.1 %copy-start.10 = (s32[2,26]{1,0:T(2,128)S(1)}, s32[2,26]{1,0:T(2,128)}, u32[]{:S(2)}) copy-start(s32[2,26]{1,0:T(2,128)} %refs_1_.2) | copy-start | bytes 628
  8.0 31.5 %copy-start.14 = (bf16[27,32,128]{2,1,0:T(8,128)(2,1)S(1)}, bf16[27,32,128]{2,1,0:T(8,128)(2,1)}, u32[]{:S(2)}) copy-start(bf16[27,32,128]{2,1,0:T(8,128)(2,1)} %refs_7_.1) | copy-start | bytes 663556
  8.0 31.5 %copy-start.15 = (f32[32]{0:T(128)S(1)}, f32[32]{0:T(128)}, u32[]{:S(2)}) copy-start(f32[32]{0:T(128)} %param.24) | copy-start | bytes 388
  8.7 3.7 %collective-permute-start.1 = (s32[2,4,26]{2,1,0:T(4,128)S(1)}, s32[2,4,26]{2,1,0:T(4,128)S(1)}, u32[]{:S(2)}, u32[]{:S(2)}) collective-permute-start(s32[2,4,26]{2,1,0:T(4,128)S(1)} %pad_add_fusion.1), channel_id=1, source_target_pairs={{0,8},{4,12},{8,0},{12,4},{16,24},{20,28},{24,16},{28,20},{1,9},{5... | collective-permute-start | bytes 2504 | tf_op jit(solution)/shard_map/ppermute | solution.py:338
  10.3 2.0 %collective-permute-start.2 = (bf16[32,256]{1,0:T(8,128)(2,1)S(1)}, bf16[32,256]{1,0:T(8,128)(2,1)S(1)}, u32[]{:S(2)}, u32[]{:S(2)}) collective-permute-start(bf16[32,256]{1,0:T(8,128)(2,1)S(1)} %get-tuple-element.43), channel_id=1, source_target_pairs={{0,1},{1,0},{2,3},{3,2},{4,5},{5,4},{6,7},{7,6},{8,9},{9,8},{10,11... | collective-permute-start | bytes 49160 | tf_op jit(solution)/shard_map/ppermute | solution.py:338
  10.3 3.7 %collective-permute-start.3 = (bf16[32,256]{1,0:T(8,128)(2,1)S(1)}, bf16[32,256]{1,0:T(8,128)(2,1)S(1)}, u32[]{:S(2)}, u32[]{:S(2)}) collective-permute-start(bf16[32,256]{1,0:T(8,128)(2,1)S(1)} %get-tuple-element.45), channel_id=1, source_target_pairs={{0,2},{1,3},{2,0},{3,1},{4,6},{5,7},{6,4},{7,5},{8,10},{9,11},{10,... | collective-permute-start | bytes 49160 | tf_op jit(solution)/shard_map/ppermute | solution.py:338
  11.9 3.2 %collective-permute-start.4 = (bf16[32,256]{1,0:T(8,128)(2,1)S(1)}, bf16[32,256]{1,0:T(8,128)(2,1)S(1)}, u32[]{:S(2)}, u32[]{:S(2)}) collective-permute-start(bf16[32,256]{1,0:T(8,128)(2,1)S(1)} %get-tuple-element.46), channel_id=1, source_target_pairs={{0,3},{1,2},{2,1},{3,0},{4,7},{5,6},{6,5},{7,4},{8,11},{9,10},{10,... | collective-permute-start | bytes 49160 | tf_op jit(solution)/shard_map/ppermute | solution.py:338
  12.4 3.7 %collective-permute-start.5 = (s32[4,4,26]{2,1,0:T(4,128)S(1)}, s32[4,4,26]{2,1,0:T(4,128)S(1)}, u32[]{:S(2)}, u32[]{:S(2)}) collective-permute-start(s32[4,4,26]{2,1,0:T(4,128)S(1)} %pad_add_fusion.refs_8_), channel_id=1, source_target_pairs={{0,4},{4,0},{8,12},{12,8},{16,20},{20,16},{24,28},{28,24},{1,5},{5... | collective-permute-start | bytes 5000 | tf_op jit(solution)/shard_map/ppermute | solution.py:338
  18.8 13.3 %all-to-all-start = ((bf16[8,80,256]{2,1,0:T(8,128)(2,1)}), bf16[8,80,256]{2,1,0:T(8,128)(2,1)S(1)}, u32[]{:S(2)}, u32[]{:S(2)}) async-start(bf16[8,80,256]{2,1,0:T(8,128)(2,1)} %get-tuple-element.49), calls=%async_computation | async-start | bytes 655360 | tf_op jit(solution)/shard_map/all_to_all | solution.py:858
  22.6 5.7 %collective-permute-start.7 = (bf16[192,512]{1,0:T(8,128)(2,1)S(1)}, bf16[192,512]{1,0:T(8,128)(2,1)S(1)}, u32[]{:S(2)}, u32[]{:S(2)}) collective-permute-start(bf16[192,512]{1,0:T(8,128)(2,1)S(1)} %get-tuple-element.58.refs_1_), channel_id=1, source_target_pairs={{0,2},{1,3},{2,0},{3,1},{4,6},{5,7},{6,4},{7,5},{8,10},{9,11},{10,... | collective-permute-start | bytes 589832 | tf_op jit(solution)/shard_map/ppermute | solution.py:338
  24.1 4.2 %collective-permute-start.6 = (bf16[192,512]{1,0:T(8,128)(2,1)S(1)}, bf16[192,512]{1,0:T(8,128)(2,1)S(1)}, u32[]{:S(2)}, u32[]{:S(2)}) collective-permute-start(bf16[192,512]{1,0:T(8,128)(2,1)S(1)} %get-tuple-element.58.refs_1_), channel_id=1, source_target_pairs={{0,1},{1,0},{2,3},{3,2},{4,5},{5,4},{6,7},{7,6},{8,9},{9,8},{10,11... | collective-permute-start | bytes 589832 | tf_op jit(solution)/shard_map/ppermute | solution.py:338
  28.3 1.4 %collective-permute-start.8 = (bf16[192,512]{1,0:T(8,128)(2,1)S(1)}, bf16[192,512]{1,0:T(8,128)(2,1)S(1)}, u32[]{:S(2)}, u32[]{:S(2)}) collective-permute-start(bf16[192,512]{1,0:T(8,128)(2,1)S(1)} %collective-permute-done.7.refs_3_), channel_id=1, source_target_pairs={{0,1},{1,0},{2,3},{3,2},{4,5},{5,4},{6,7},{7,6},{8,9},{9,8},{10,11... | collective-permute-start | bytes 589832 | tf_op jit(solution)/shard_map/ppermute | solution.py:338
  32.1 5.0 %collective-permute-start.9 = (bf16[8,32,256]{2,1,0:T(8,128)(2,1)S(1)}, bf16[8,32,256]{2,1,0:T(8,128)(2,1)S(1)}, u32[]{:S(2)}, u32[]{:S(2)}) collective-permute-start(bf16[8,32,256]{2,1,0:T(8,128)(2,1)S(1)} %slice.3.refs_2_), channel_id=1, source_target_pairs={{0,2},{1,3},{2,0},{3,1},{4,6},{5,7},{6,4},{7,5},{8,10},{9,11},{10,... | collective-permute-start | bytes 393224 | tf_op jit(solution)/shard_map/ppermute | solution.py:338
  37.1 2.4 %collective-permute-start.10 = (bf16[8,32,256]{2,1,0:T(8,128)(2,1)S(1)}, bf16[8,32,256]{2,1,0:T(8,128)(2,1)S(1)}, u32[]{:S(2)}, u32[]{:S(2)}) collective-permute-start(bf16[8,32,256]{2,1,0:T(8,128)(2,1)S(1)} %slice.3.refs_2_), channel_id=1, source_target_pairs={{0,1},{1,0},{2,3},{3,2},{4,5},{5,4},{6,7},{7,6},{8,9},{9,8},{10,11... | collective-permute-start | bytes 393224 | tf_op jit(solution)/shard_map/ppermute | solution.py:338
  37.1 2.4 %collective-permute-start.11 = (bf16[8,32,256]{2,1,0:T(8,128)(2,1)S(1)}, bf16[8,32,256]{2,1,0:T(8,128)(2,1)S(1)}, u32[]{:S(2)}, u32[]{:S(2)}) collective-permute-start(bf16[8,32,256]{2,1,0:T(8,128)(2,1)S(1)} %collective-permute-done.9.refs_4_), channel_id=1, source_target_pairs={{0,1},{1,0},{2,3},{3,2},{4,5},{5,4},{6,7},{7,6},{8,9},{9,8},{10,11... | collective-permute-start | bytes 393224 | tf_op jit(solution)/shard_map/ppermute | solution.py:338
  37.6 7.1 %collective-permute-start.15 = (bf16[4,32,512]{2,1,0:T(8,128)(2,1)S(1)}, bf16[4,32,512]{2,1,0:T(8,128)(2,1)S(1)}, u32[]{:S(2)}, u32[]{:S(2)}) collective-permute-start(bf16[4,32,512]{2,1,0:T(8,128)(2,1)S(1)} %get-tuple-element.62.refs_5_), channel_id=1, source_target_pairs={{0,3},{1,2},{2,1},{3,0},{4,7},{5,6},{6,5},{7,4},{8,11},{9,10},{10,... | collective-permute-start | bytes 393224 | tf_op jit(solution)/shard_map/ppermute | solution.py:338
  38.5 7.7 %collective-permute-start.14 = (bf16[4,32,512]{2,1,0:T(8,128)(2,1)S(1)}, bf16[4,32,512]{2,1,0:T(8,128)(2,1)S(1)}, u32[]{:S(2)}, u32[]{:S(2)}) collective-permute-start(bf16[4,32,512]{2,1,0:T(8,128)(2,1)S(1)} %get-tuple-element.62.refs_5_), channel_id=1, source_target_pairs={{0,2},{1,3},{2,0},{3,1},{4,6},{5,7},{6,4},{7,5},{8,10},{9,11},{10,... | collective-permute-start | bytes 393224 | tf_op jit(solution)/shard_map/ppermute | solution.py:338
  39.2 7.0 %collective-permute-start.13 = (bf16[4,32,512]{2,1,0:T(8,128)(2,1)S(1)}, bf16[4,32,512]{2,1,0:T(8,128)(2,1)S(1)}, u32[]{:S(2)}, u32[]{:S(2)}) collective-permute-start(bf16[4,32,512]{2,1,0:T(8,128)(2,1)S(1)} %get-tuple-element.62.refs_5_), channel_id=1, source_target_pairs={{0,1},{1,0},{2,3},{3,2},{4,5},{5,4},{6,7},{7,6},{8,9},{9,8},{10,11... | collective-permute-start | bytes 393224 | tf_op jit(solution)/shard_map/ppermute | solution.py:338
  39.5 9.7 %copy-start.1 = (bf16[27,32,128]{2,1,0:T(8,128)(2,1)S(1)}, bf16[27,32,128]{2,1,0:T(8,128)(2,1)}, u32[]{:S(2)}) copy-start(bf16[27,32,128]{2,1,0:T(8,128)(2,1)} %refs_8_.1) | copy-start | bytes 663556
  39.5 9.7 %copy-start.2 = (bf16[256,256]{1,0:T(8,128)(2,1)S(1)}, bf16[256,256]{1,0:T(8,128)(2,1)}, u32[]{:S(2)}) copy-start(bf16[256,256]{1,0:T(8,128)(2,1)} %constant.26.clone.refs_10_) | copy-start | bytes 393220
  39.5 9.7 %copy-start.6 = (bf16[192,128]{1,0:T(8,128)(2,1)S(1)}, bf16[192,128]{1,0:T(8,128)(2,1)}, u32[]{:S(2)}) copy-start(bf16[192,128]{1,0:T(8,128)(2,1)} %constant.25.clone.refs_6_) | copy-start | bytes 147460
  39.5 9.7 %copy-start.13 = (f32[32]{0:T(128)S(1)}, f32[32]{0:T(128)}, u32[]{:S(2)}) copy-start(f32[32]{0:T(128)} %param.25) | copy-start | bytes 388
  43.3 4.5 %collective-permute-start.12 = (bf16[32,1152]{1,0:T(8,128)(2,1)S(1)}, bf16[32,1152]{1,0:T(8,128)(2,1)S(1)}, u32[]{:S(2)}, u32[]{:S(2)}) collective-permute-start(bf16[32,1152]{1,0:T(8,128)(2,1)S(1)} %coarse.1.refs_1_), channel_id=1, source_target_pairs={{0,2},{1,3},{2,0},{3,1},{4,6},{5,7},{6,4},{7,5},{8,10},{9,11},{10,... | collective-permute-start | bytes 221192 | tf_op jit(solution)/shard_map/ppermute | solution.py:338
  47.8 1.3 %collective-permute-start.16 = (bf16[32,1152]{1,0:T(8,128)(2,1)S(1)}, bf16[32,1152]{1,0:T(8,128)(2,1)S(1)}, u32[]{:S(2)}, u32[]{:S(2)}) collective-permute-start(bf16[32,1152]{1,0:T(8,128)(2,1)S(1)} %coarse.1.refs_1_), channel_id=1, source_target_pairs={{0,1},{1,0},{2,3},{3,2},{4,5},{5,4},{6,7},{7,6},{8,9},{9,8},{10,11... | collective-permute-start | bytes 221192 | tf_op jit(solution)/shard_map/ppermute | solution.py:338
  47.8 1.4 %collective-permute-start.17 = (bf16[32,1152]{1,0:T(8,128)(2,1)S(1)}, bf16[32,1152]{1,0:T(8,128)(2,1)S(1)}, u32[]{:S(2)}, u32[]{:S(2)}) collective-permute-start(bf16[32,1152]{1,0:T(8,128)(2,1)S(1)} %collective-permute-done.12.refs_3_), channel_id=1, source_target_pairs={{0,1},{1,0},{2,3},{3,2},{4,5},{5,4},{6,7},{7,6},{8,9},{9,8},{10,11... | collective-permute-start | bytes 221192 | tf_op jit(solution)/shard_map/ppermute | solution.py:338
